TPU v7x, 32 devices: a whole 2x2x4 slice. The times are simulated.
32 devices in a mesh: grp: 2 (over x), seq: 8 (over z, y), head: 2 (over core).
Axes of the slice: x: 2, y: 2, z: 4, core: 2. Of those that a mesh axis runs over, the one named last changes fastest.
Arguments:
- query: bfloat16 [2048, 4096], P(('grp', 'seq'), 'head'), parts along dimension 0, may hold values from -6 to 6
- keys: bfloat16 [2048, 4096], P(('grp', 'seq'), 'head'), parts along dimension 0, may hold values from -6 to 6
- values: bfloat16 [2048, 4096], P(('grp', 'seq'), 'head'), parts along dimension 0, may hold values from -6 to 6
- resid: bfloat16 [2048, 3072], P(('grp', 'seq'), 'head'), parts along dimension 0, may hold values from -6 to 6
- attn_gain: float32 [4096], P('head'), may hold values from 0.2 to 1.8
- out_weight: bfloat16 [4096, 3072], P('head', 'seq'), may hold values from -0.09375 to 0.09375
- moe_gain: float32 [3072], replicated, may hold values from 0.2 to 1.8
- routes: int32 [2048, 2], P(('grp', 'seq')), parts along dimension 0, may hold values from 0 to 7, all different within a row; in each aligned block of 128 rows (0 to 127, 128 to 255, ...) at most 36 rows name the same one
- route_weights: float32 [2048, 2], P(('grp', 'seq')), parts along dimension 0, may hold values from 0.2 to 1
- w_gate: bfloat16 [3072, 36864], P(None, ('seq', 'head')), may hold values from -0.109375 to 0.109375
- w_up: bfloat16 [3072, 36864], P(None, ('seq', 'head')), may hold values from -0.109375 to 0.109375
- w_down: bfloat16 [36864, 3072], P(('seq', 'head')), may hold values from -0.09375 to 0.09375
Outputs:
- mixed: bfloat16 [2048, 3072], P(('grp', 'seq'), 'head'), parts along dimension 0
There are 2 independent parts, one for each index of `grp`. A program takes and returns all parts, laid end to end along the dimension named above; an argument that names none is the same for every part. Nothing has to cross between parts.
Inputs may be any that keep to these rules, and one draw needn't show every extreme that they name: A token's 2 experts differ. Within each aligned block of 128 tokens no expert is named by more than 36 routes, and in every draw some expert is named by exactly 36 routes of some block.
All inputs are finite; a program needn't handle non-finite values.
Results may differ from a plain program's by a relative error of at most 0.015.
Values may be sent and summed in bfloat16 or wider, within the bound.
No kernel may reach another device: no remote copies, remote signals or barrier semaphores. Data moves between devices by JAX's collectives and lax.ppermute only.
A program may use at most 128 MiB of HBM per device.

v0:
```python
import functools

import jax
import jax.numpy as jnp
from jax import lax
from jax.experimental import pallas as pl
from jax.experimental.pallas import tpu as pltpu
from jax.sharding import PartitionSpec as P

HD = 128
EXPERTS = 8
TOP = 2
CAP = 36
EPS = 1e-06
NOTES = 8
FOLD = 4
BF = jnp.bfloat16
F32 = jnp.float32
MIB = 1024 * 1024
VMEM_BYTES = 10 * MIB


def swap_cores(x):
    return lax.ppermute(x, "head", [(0, 1), (1, 0)])


def dot(a, b):
    return jnp.dot(a, b, preferred_element_type=F32)


def contract(a, b, dims):
    return lax.dot_general(a, b, ((dims[:1], dims[1:]), ((), ())), preferred_element_type=F32)


def state_kernel(heads, half, routes_ref, weights_ref, k_hbm, v_hbm, out_ref, k_ref, v_ref, sems):
    width = heads * HD
    copies = []
    for j in range(half):
        at = pl.ds(j * width, width)
        pair = [
            pltpu.make_async_copy(k_hbm.at[:, at], k_ref.at[j], sems.at[0, j]),
            pltpu.make_async_copy(v_hbm.at[:, at], v_ref.at[j], sems.at[1, j]),
        ]
        for copy in pair:
            copy.start()
        copies.append(pair)
    routes = routes_ref[...].astype(F32)
    weights = weights_ref[...]
    rows = [routes[0:1], routes[1:2]]
    for i in range(TOP):
        rest = weights[i : i + 1]
        for _ in range(3):
            piece = rest.astype(BF).astype(F32)
            rows.append(piece)
            rest = rest - piece
    spare = jnp.zeros((out_ref.shape[1] - width - NOTES, routes.shape[1]), F32)
    notes = jnp.concatenate(rows + [spare], axis=0).astype(BF)
    for j in range(half):
        for copy in copies[j]:
            copy.wait()
        for n in range(heads):
            lo = n * HD
            state = contract(k_ref[j, :, lo : lo + HD], v_ref[j, :, lo : lo + HD], (0, 0))
            out_ref[j, lo : lo + HD] = state.astype(BF)
        out_ref[j, width:] = notes


def total_kernel(width, x_ref, out_ref):
    blocks = x_ref.shape[0]
    total = x_ref[0, :width].astype(F32)
    for b in range(1, blocks):
        total = total + x_ref[b, :width].astype(F32)
    out_ref[:width] = total.astype(BF)
    notes = [x_ref[b, width : width + NOTES].astype(F32) for b in range(blocks)]
    out_ref[width:] = jnp.concatenate(notes, axis=0).astype(BF)


def before_kernel(flags_ref, x_ref, far_ref, out_ref):
    blocks, width, _ = out_ref.shape
    running = jnp.where(flags_ref[1] == 1, far_ref[:width].astype(F32), 0.0)
    for b in range(blocks):
        out_ref[b] = running.astype(BF)
        if b < blocks - 1:
            running = running + x_ref[b, :width].astype(F32)


def attention_kernel(q_ref, k_ref, v_ref, before_ref, gain_ref, out_ref):
    tok, all_lanes = q_ref.shape
    owners = before_ref.shape[0]
    each = all_lanes // HD // owners
    row = lax.broadcasted_iota(jnp.int32, (tok, tok), 0)
    column = lax.broadcasted_iota(jnp.int32, (tok, tok), 1)
    causal = row >= column
    for n in range(owners * each):
        at = slice(n * HD, (n + 1) * HD)
        state_at = slice(n % each * HD, (n % each + 1) * HD)
        q = q_ref[:, at]
        inter = dot(q, before_ref[n // each, state_at])
        scores = jnp.where(causal, contract(q, k_ref[:, at], (1, 1)), 0.0).astype(BF)
        attention = inter + dot(scores, v_ref[:, at])
        mean = jnp.mean(attention * attention, axis=-1, keepdims=True)
        normed = attention * lax.rsqrt(mean + EPS) * gain_ref[0:1, at]
        out_ref[:, at] = normed.astype(BF)


def ranks_of(hits):
    rows, tok = hits.shape
    row = lax.broadcasted_iota(jnp.int32, (tok, tok), 0)
    column = lax.broadcasted_iota(jnp.int32, (tok, tok), 1)
    before = jnp.where(row < column, 1.0, 0.0).astype(BF)
    return dot(hits.astype(BF), before)


def dispatch_kernel(
    per_expert, flags_ref, acc_ref, other_ref, resid_ref, notes_ref, far_ref, *refs
):
    outs, place_ref = refs[:-1], refs[-1]
    core = flags_ref[0]
    blocks, tok, cols = other_ref.shape
    parts = []
    for b in range(blocks):
        own = acc_ref[core * blocks + b] + other_ref[b].astype(F32)
        parts.append((own + resid_ref[b ^ flags_ref[2]].astype(F32)).astype(BF))
    hidden = jnp.concatenate(parts, axis=0)
    first = notes_ref.shape[0] - NOTES * blocks
    near = core == flags_ref[1]
    notes = jnp.where(near, notes_ref[first:].astype(F32), far_ref[first:].astype(F32))
    expert = lax.broadcasted_iota(jnp.int32, (EXPERTS, tok), 0).astype(F32)
    for b in range(blocks):
        at = b * NOTES
        hit = (notes[at : at + 1] == expert) | (notes[at + 1 : at + 2] == expert)
        ranks = ranks_of(jnp.where(hit, 1.0, 0.0))
        place_ref[:, b * tok : (b + 1) * tok] = jnp.where(hit, ranks + b * CAP, -1.0)
    rows = outs[0].shape[0]
    slot = lax.broadcasted_iota(jnp.int32, (rows, blocks * tok), 0).astype(F32)
    for k, out_ref in enumerate(outs):
        e = (flags_ref[5] ^ k) // per_expert
        pick = jnp.where(slot == place_ref[pl.ds(e, 1), :], 1.0, 0.0).astype(BF)
        out_ref[...] = dot(pick, hidden).astype(BF)


def return_kernel(flags_ref, mine_ref, theirs_ref, x_refs, notes_ref, far_ref, outs, row_ref):
    core, upper, expert, leads = flags_ref[0], flags_ref[1], flags_ref[3], flags_ref[4]
    near_own, near_other, rest_own, rest_other = x_refs
    pieces, rows, width = near_own.shape
    blocks = rows // CAP
    tok = notes_ref.shape[1]
    first = notes_ref.shape[0] - NOTES * blocks
    piece_width = mine_ref.shape[1] // FOLD
    slot = lax.broadcasted_iota(jnp.int32, (rows, blocks * tok), 0).astype(F32)
    block_of = lax.broadcasted_iota(jnp.int32, (blocks, tok), 0).astype(F32)
    wanted = expert.astype(F32)
    lead = jnp.where(leads == 1, 1.0, 0.0)

    def hidden_piece(ref, m):
        if pieces == 1:
            return ref[0, :, m * piece_width : (m + 1) * piece_width].astype(F32)
        return ref[flags_ref[2] ^ m].astype(F32)

    for half in range(2):
        notes = jnp.where(upper == half, notes_ref[first:].astype(F32), far_ref[first:].astype(F32))

        def line(i):
            return jnp.concatenate(
                [notes[b * NOTES + i : b * NOTES + i + 1] for b in range(blocks)], axis=0
            )

        hit = jnp.where(line(0) == wanted, 1.0, 0.0)
        second = jnp.where(line(1) == wanted, 1.0, 0.0)
        any_hit = hit + second
        weight = hit * (line(2) + line(3) + line(4)) + second * (line(5) + line(6) + line(7))
        place = jnp.where(any_hit > 0.0, ranks_of(any_hit) + block_of * CAP, -1.0)

        def flat(x):
            return jnp.concatenate([x[b : b + 1] for b in range(blocks)], axis=1)

        equal = slot == flat(place)
        row_weight = jnp.sum(jnp.where(equal, flat(weight), 0.0), axis=1, keepdims=True)
        row_first = jnp.sum(jnp.where(equal, flat(hit * lead), 0.0), axis=1, keepdims=True)
        at = slice(half * rows, (half + 1) * rows)
        parts = []
        for m in range(FOLD):
            lanes = slice(m * piece_width, (m + 1) * piece_width)
            near = jnp.where(core == half, hidden_piece(near_own, m), hidden_piece(near_other, m))
            rest = jnp.where(core == half, hidden_piece(rest_own, m), hidden_piece(rest_other, m))
            hidden = jnp.where(core == upper, near, rest)
            out = mine_ref[at, lanes].astype(F32) + theirs_ref[at, lanes].astype(F32)
            parts.append(out * row_weight + hidden * row_first)
        for b in range(blocks):
            slots = slice(b * CAP, (b + 1) * CAP)
            folded = jnp.concatenate([part[slots] for part in parts], axis=0)
            row_ref[(half * blocks + b) ^ flags_ref[5]] = folded.astype(BF)
    for k, out_ref in enumerate(outs):
        out_ref[...] = row_ref[k]


def return_entry(flags_ref, mine_ref, theirs_ref, a, b, c, d, notes_ref, far_ref, *refs):
    return_kernel(
        flags_ref, mine_ref, theirs_ref, (a, b, c, d), notes_ref, far_ref, refs[:-1], refs[-1]
    )


def combine_kernel(per_expert, flags_ref, routes_ref, *refs):
    backs, out_ref, place_ref = refs[:-2], refs[-2], refs[-1]
    folded, width = backs[0].shape
    tok = routes_ref.shape[1]
    routes = routes_ref[...]
    expert = lax.broadcasted_iota(jnp.int32, (EXPERTS, tok), 0)
    hit = (routes[0:1] == expert) | (routes[1:2] == expert)
    place_ref[...] = jnp.where(hit, ranks_of(jnp.where(hit, 1.0, 0.0)), -float(folded))
    slot = lax.broadcasted_iota(jnp.int32, (folded, tok), 0).astype(F32)
    places = [
        place_ref[pl.ds((flags_ref[5] ^ k) // per_expert, 1), :] for k in range(len(backs))
    ]
    back = jnp.concatenate([ref[...] for ref in backs], axis=0)
    for m in range(folded // CAP):
        picks = [jnp.where(slot == place + m * CAP, 1.0, 0.0) for place in places]
        pick = jnp.concatenate(picks, axis=0).astype(BF)
        out_ref[:, m * width : (m + 1) * width] = contract(pick, back, (0, 0)).astype(BF)


def place_rows(info_ref, own_ref, other_ref, gain_ref, x_ref):
    pieces, rows, width = own_ref.shape
    core = info_ref[0]

    def place(ref, base):
        total = jnp.zeros((rows, 1), F32)
        for p in range(pieces):
            at = 0 if pieces == 1 else pl.multiple_of(info_ref[2 + p] * width, width)
            wide = ref[p].astype(F32)
            total = total + jnp.sum(wide * wide, axis=-1, keepdims=True)
            gain = gain_ref[0:1, pl.ds(at, width)]
            x_ref[pl.ds(base, rows), pl.ds(at, width)] = (wide * gain).astype(BF)
        return total

    own_total = place(own_ref, pl.multiple_of(core * rows, rows))
    other_total = place(other_ref, pl.multiple_of((1 - core) * rows, rows))
    low = jnp.where(core == 0, own_total, other_total)
    high = jnp.where(core == 0, other_total, own_total)
    return jnp.concatenate([low, high], axis=0)


def weight_copies(info_ref, sources, buffers, sems, tile):
    depth = buffers[0].shape[1]
    base = pl.multiple_of(info_ref[1] * depth, depth)
    copies = []
    for i in range(buffers[0].shape[0]):
        pair = []
        for n, (source, buffer) in enumerate(zip(sources, buffers)):
            piece = source.at[pl.ds(base, depth), pl.ds(i * tile, tile)]
            copy = pltpu.make_async_copy(piece, buffer.at[i], sems.at[n, i])
            copy.start()
            pair.append(copy)
        copies.append(pair)
    return copies


def first_kernel(
    tile, info_ref, own_ref, other_ref, gain_ref, weight_hbm,
    out_ref, total_out, x_ref, weight_ref, sems,
):
    copies = weight_copies(info_ref, (weight_hbm,), (weight_ref,), sems, tile)
    total = place_rows(info_ref, own_ref, other_ref, gain_ref, x_ref)
    total_out[...] = jnp.broadcast_to(total, total_out.shape)
    x = x_ref[...]
    for i, (copy,) in enumerate(copies):
        copy.wait()
        out_ref[:, i * tile : (i + 1) * tile] = dot(x, weight_ref[i])


def second_kernel(
    tile, out_tile, info_ref, own_ref, other_ref, gain_ref, gate_in, up_in, total_in,
    gate_hbm, up_hbm, down_hbm,
    mine_ref, theirs_ref, x_ref, inner_ref, gate_ref, up_ref, down_ref, sems, down_sems,
):
    core = info_ref[0]
    copies = weight_copies(info_ref, (gate_hbm, up_hbm), (gate_ref, up_ref), sems, tile)
    half = mine_ref.shape[1]
    downs = []
    for i in range(2 * half // out_tile):
        side = 1 - core if i * out_tile < half else core
        at = pl.multiple_of(side * half + i * out_tile % half, out_tile)
        copy = pltpu.make_async_copy(
            down_hbm.at[:, pl.ds(at, out_tile)], down_ref.at[i], down_sems.at[i]
        )
        copy.start()
        downs.append(copy)
    total = place_rows(info_ref, own_ref, other_ref, gain_ref, x_ref)
    features = 2 * half
    scale = lax.rsqrt((total + total_in[:, 0:1]) / features + EPS)
    x = x_ref[...]
    for i, pair in enumerate(copies):
        at = slice(i * tile, (i + 1) * tile)
        pair[0].wait()
        gate = (gate_in[:, at] + dot(x, gate_ref[i])) * scale
        pair[1].wait()
        upward = (up_in[:, at] + dot(x, up_ref[i])) * scale
        inner_ref[:, at] = (gate / (1.0 + jnp.exp(-gate)) * upward).astype(BF)
    inner = inner_ref[...]
    for i, copy in enumerate(downs):
        copy.wait()
        value = dot(inner, down_ref[i]).astype(BF)
        lo = i * out_tile % half
        out_ref = theirs_ref if i * out_tile < half else mine_ref
        out_ref[:, lo : lo + out_tile] = value


def tile_of(size):
    for tile in (768, 256, 128):
        if size % tile == 0:
            return tile
    return size


def by_rows(fn, rows, arrays, fixed):
    limit = EXPERTS * CAP // 2
    if rows <= limit or rows % limit:
        return fn(*arrays, *fixed)
    parts = []
    for r in range(0, rows, limit):
        cut = [
            a[:, r : r + limit] if len(a.shape) == 3
            else a.reshape(2, rows, -1)[:, r : r + limit].reshape(2 * limit, -1)
            for a in arrays
        ]
        parts.append(fn(*cut, *fixed))
    joined = []
    for i in range(len(parts[0])):
        pieces = [p[i].reshape(2, limit, -1) for p in parts]
        joined.append(jnp.concatenate(pieces, axis=1).reshape(2 * rows, -1))
    return joined


def experts_first(name, info, own, other, gain, weight):
    pieces, rows, width = own.shape
    depth = pieces * width
    hidden = weight.shape[1]
    tile = tile_of(hidden)
    smem = pl.BlockSpec(memory_space=pltpu.SMEM)
    vmem = pl.BlockSpec(memory_space=pltpu.VMEM)
    hbm = pl.BlockSpec(memory_space=pltpu.HBM)
    product = jax.ShapeDtypeStruct((2 * rows, hidden), F32)
    return pl.pallas_call(
        functools.partial(first_kernel, tile),
        out_shape=(product, jax.ShapeDtypeStruct((2 * rows, 128), F32)),
        in_specs=[smem] + [vmem] * 3 + [hbm],
        out_specs=(vmem,) * 2,
        scratch_shapes=[
            pltpu.VMEM((2 * rows, depth), BF),
            pltpu.VMEM((hidden // tile, depth, tile), BF),
            pltpu.SemaphoreType.DMA((1, hidden // tile)),
        ],
        compiler_params=pltpu.CompilerParams(vmem_limit_bytes=16 * MIB),
        cost_estimate=pl.CostEstimate(
            flops=4 * rows * depth * hidden, bytes_accessed=2 * depth * hidden, transcendentals=0
        ),
        name=name,
    )(info, own, other, gain, weight)


def experts_second(info, own, other, gate, upward, total, gain, w_gate, w_up, w_down):
    pieces, rows, width = own.shape
    depth = pieces * width
    hidden, features = w_down.shape
    tile, out_tile = tile_of(hidden), tile_of(features // 2)
    smem = pl.BlockSpec(memory_space=pltpu.SMEM)
    vmem = pl.BlockSpec(memory_space=pltpu.VMEM)
    hbm = pl.BlockSpec(memory_space=pltpu.HBM)
    out = jax.ShapeDtypeStruct((2 * rows, features // 2), BF)
    buffer = pltpu.VMEM((hidden // tile, depth, tile), BF)
    return pl.pallas_call(
        functools.partial(second_kernel, tile, out_tile),
        out_shape=(out, out),
        in_specs=[smem] + [vmem] * 6 + [hbm] * 3,
        out_specs=(vmem, vmem),
        scratch_shapes=[
            pltpu.VMEM((2 * rows, depth), BF), pltpu.VMEM((2 * rows, hidden), BF), buffer, buffer,
            pltpu.VMEM((features // out_tile, hidden, out_tile), BF),
            pltpu.SemaphoreType.DMA((2, hidden // tile)),
            pltpu.SemaphoreType.DMA((features // out_tile,)),
        ],
        compiler_params=pltpu.CompilerParams(vmem_limit_bytes=40 * MIB),
        cost_estimate=pl.CostEstimate(
            flops=8 * rows * depth * hidden + 4 * rows * features * hidden,
            bytes_accessed=4 * depth * hidden + 2 * features * hidden,
            transcendentals=2 * rows * hidden,
        ),
        name="experts_second",
    )(info, own, other, gain, gate, upward, total, w_gate, w_up, w_down)


def on_chip(kernel, name, out, *operands, scalars=0, hbm=0, scratch=(), room=1):
    smem = pl.BlockSpec(memory_space=pltpu.SMEM)
    vmem = pl.BlockSpec(memory_space=pltpu.VMEM)
    anywhere = pl.BlockSpec(memory_space=pltpu.HBM)
    inside = len(operands) - scalars - hbm
    if isinstance(out, list):
        out_shape, out_specs = [jax.ShapeDtypeStruct(*o) for o in out], [vmem] * len(out)
    else:
        out_shape, out_specs = jax.ShapeDtypeStruct(*out), vmem
    return pl.pallas_call(
        kernel,
        out_shape=out_shape,
        in_specs=[smem] * scalars + [vmem] * inside + [anywhere] * hbm,
        out_specs=out_specs,
        scratch_shapes=scratch,
        compiler_params=pltpu.CompilerParams(vmem_limit_bytes=room * VMEM_BYTES),
        name=name,
    )(*operands)


def xor_shift(x, k):
    return lax.ppermute(x, "seq", [(s, s ^ k) for s in range(lax.axis_size("seq"))])


def ring_order(count):
    return list(range(0, count, 2)) + list(range(count - 1, 0, -2))


def ring_project(x, out_weight, seq_count, me):
    tok = x.shape[0]
    half = seq_count // 2
    order = ring_order(seq_count)
    here = jnp.where(me % 2 == 0, me // 2, seq_count - 1 - me // 2)
    ahead = [(order[i], order[(i + 1) % seq_count]) for i in range(seq_count)]
    behind = [(b, a) for a, b in ahead]
    acc = jnp.zeros((seq_count, tok, out_weight.shape[1]), F32)

    def chip(step):
        i = (here + step + seq_count) % seq_count
        return jnp.where(i < half, 2 * i, 2 * (seq_count - 1 - i) + 1)

    def add(acc, block, source, start):
        return lax.dynamic_update_slice(acc, dot(block, out_weight)[None], (source, start, 0))

    cut = tok // 2
    for start in (0, cut):
        acc = add(acc, x[start : start + cut], me, start)
    back = [x[:cut], x[cut:]]
    front = [x[:cut], x[cut:]]
    for step in range(1, half + 1):
        for i in (0, 1):
            if step < half or i == 0:
                back[i] = lax.ppermute(back[i], "seq", ahead)
                acc = add(acc, back[i], chip(-step), i * cut)
            if step < half or i == 1:
                front[i] = lax.ppermute(front[i], "seq", behind)
                acc = add(acc, front[i], chip(step), i * cut)
    return acc


def per_device(
    query, keys, values, resid, attn_gain, out_weight, moe_gain, routes, route_weights,
    w_gate, w_up, w_down,
):
    tok = query.shape[0]
    heads = query.shape[1] // HD
    cols = out_weight.shape[1]
    seq_count = lax.axis_size("seq")
    me = lax.axis_index("seq")
    core = lax.axis_index("head")
    half = seq_count // 2
    half_width = resid.shape[1]
    per_expert = seq_count // EXPERTS
    local = heads // half
    width = local * HD
    flags = jnp.stack(
        [core, me // half, me % half, me // per_expert, (me % per_expert == 0).astype(jnp.int32), me]
    ).astype(jnp.int32)
    routes_by_lane = routes.T
    chips = list(range(seq_count))
    groups = [chips[:half], chips[half:]]

    crossing = [(2 * j + 1, 2 * (half + j)) for j in range(half)]
    crossing = crossing + [(b, a) for a, b in crossing]
    crossed = lax.ppermute(resid, ("seq", "head"), crossing)

    hbm_blocks = pltpu.VMEM((half, tok, width), BF)
    states = on_chip(
        functools.partial(state_kernel, local, half), "states", ((half, width + 16, HD), BF),
        routes_by_lane, route_weights.T, keys, values,
        hbm=2, scratch=(hbm_blocks, hbm_blocks, pltpu.SemaphoreType.DMA((2, half))),
    )
    blocks = lax.all_to_all(states, "seq", 0, 0, axis_index_groups=groups, tiled=True)
    own_sum = on_chip(
        functools.partial(total_kernel, width), "totals", ((width + half * NOTES, HD), BF), blocks
    )
    far_sum = lax.ppermute(own_sum, "seq", [(s, (s + half) % seq_count) for s in chips])
    sums = on_chip(
        before_kernel, "sums", ((half, width, HD), BF), flags, blocks, far_sum, scalars=1
    )
    sums = lax.all_to_all(sums, "seq", 0, 0, axis_index_groups=groups, tiled=True)

    held = jnp.where(me // half == core, resid, crossed)
    columns = []
    for k in range(half):
        piece = lax.dynamic_slice_in_dim(held, ((me % half) ^ k) * cols, cols, 1)
        columns.append(xor_shift(piece, k) if k else piece)
    columns, sums = lax.optimization_barrier((jnp.stack(columns), sums))
    normed = on_chip(
        attention_kernel, "attention", ((tok, heads * HD), BF),
        query, keys, values, sums, attn_gain.reshape(1, heads * HD),
    )
    acc = ring_project(normed, out_weight, seq_count, me)
    theirs = lax.dynamic_slice_in_dim(acc, (1 - core) * half, half, 0)
    other = swap_cores(theirs.astype(BF))

    rows = half * CAP
    pieces = on_chip(
        functools.partial(dispatch_kernel, per_expert), "dispatch",
        [((rows, cols), BF)] * seq_count,
        flags, acc, other, columns, own_sum, far_sum,
        scalars=1, room=half // 4, scratch=[pltpu.VMEM((EXPERTS, half * tok), F32)],
    )
    got = [pieces[0]] + [None] * (seq_count - 1)
    for k in [half] + list(range(1, half)) + list(range(half + 1, seq_count)):
        got[k] = xor_shift(pieces[k], k)

    def part(ks):
        own = jnp.stack([got[k] for k in ks])
        if cols % 128:
            order = (me % half) ^ jnp.arange(half)
            own = jnp.take(own, order, axis=0).transpose(1, 0, 2).reshape(1, rows, half * cols)
        return own, swap_cores(own)

    turns = (me % half) ^ jnp.arange(half)
    side = me // half
    gains = moe_gain.reshape(2, 1, half_width)

    def info_of(which):
        return jnp.concatenate([jnp.stack([core, which]), turns]).astype(jnp.int32)

    near = part(range(half))
    near_gain = lax.dynamic_index_in_dim(gains, side, 0, keepdims=False)
    gate, total = by_rows(
        functools.partial(experts_first, "near_gate", info_of(side)), rows, near,
        (near_gain, w_gate),
    )
    waiting = lax.optimization_barrier((total, *got[half:]))
    total, got[half:] = waiting[0], waiting[1:]
    upward, _ = by_rows(
        functools.partial(experts_first, "near_up", info_of(side)), rows, near, (near_gain, w_up)
    )
    rest = part(range(half, seq_count))
    rest_gain = lax.dynamic_index_in_dim(gains, 1 - side, 0, keepdims=False)
    mine, theirs = by_rows(
        functools.partial(experts_second, info_of(1 - side)), rows,
        (*rest, gate, upward, total), (rest_gain, w_gate, w_up, w_down),
    )
    piece = half_width // FOLD
    out = on_chip(
        return_entry, "weigh", [((FOLD * CAP, piece), BF)] * seq_count,
        flags, mine, swap_cores(theirs), *near, *rest, own_sum, far_sum,
        scalars=1, room=half // 4, scratch=[pltpu.VMEM((seq_count, FOLD * CAP, piece), BF)],
    )
    back = [out[0]] + [None] * (seq_count - 1)
    for k in list(range(half, seq_count)) + list(range(1, half)):
        back[k] = xor_shift(out[k], k)
    return on_chip(
        functools.partial(combine_kernel, per_expert), "combine", ((tok, half_width), BF),
        flags, routes_by_lane, *back,
        scalars=1, room=half // 4, scratch=[pltpu.VMEM((EXPERTS, tok), F32)],
    )


def solution(mesh):
    return jax.shard_map(
        per_device,
        mesh=mesh,
        in_specs=(
            P(("grp", "seq"), "head"),
            P(("grp", "seq"), "head"),
            P(("grp", "seq"), "head"),
            P(("grp", "seq"), "head"),
            P("head"),
            P("head", "seq"),
            P(),
            P(("grp", "seq"), None),
            P(("grp", "seq"), None),
            P(None, ("seq", "head")),
            P(None, ("seq", "head")),
            P(("seq", "head"), None),
        ),
        out_specs=P(("grp", "seq"), "head"),
        check_vma=False,
    )
```

profile of v0, /device:TPU:0, one launch (start us, length us, event | category | flops | bytes accessed | tf_op | source)
XLA Modules:
  0.0 186.9 jit_solution(3181297789087490854)
XLA Ops:
  0.0 1.2 copy-done.4
  1.2 1.0 copy-done.6
  2.2 0.7 copy-done.14
  3.6 1.9 %states.1 = bf16[4,528,128]{2,1,0:T(8,128)(2,1)} custom-call(s32[2,128]{1,0:T(2,128)S(1)} %bitcast.122, f32[2,128]{1,0:T(2,128)S(1)} %bitcast.124, bf16[128,2048]{1,0:T(8,128)(2,1)S(1)} %copy-done.4, bf16[128,2048]{1,0:T(8,128)(2,1)S(1)} %copy-done.6), custom_call_target="tpu_custom_call" | custom-call | tf_op jit(solution)/shard_map/states/pallas_call | solution.py:401
  5.5 5.3 %all-to-all-start = ((bf16[4,528,128]{2,1,0:T(8,128)(2,1)}), bf16[4,528,128]{2,1,0:T(8,128)(2,1)S(1)}, u32[]{:S(2)}, u32[]{:S(2)}) async-start(bf16[4,528,128]{2,1,0:T(8,128)(2,1)} %states.1), calls=%async_computation | async-start | bytes 1081344 | tf_op jit(solution)/shard_map/all_to_all | solution.py:484
  10.7 1.4 collective-permute-start
  12.2 11.0 %all-to-all-done.x_ref = bf16[4,528,128]{2,1,0:T(8,128)(2,1)S(1)} async-done(((bf16[4,528,128]{2,1,0:T(8,128)(2,1)}), bf16[4,528,128]{2,1,0:T(8,128)(2,1)S(1)}, u32[]{:S(2)}, u32[]{:S(2)}) %all-to-all-start) | async-done | bytes 540704 | tf_op jit(solution)/shard_map/all_to_all | solution.py:484
  23.5 7.8 %collective-permute-done.4.far_ref = bf16[544,128]{1,0:T(8,128)(2,1)S(1)} collective-permute-done((bf16[544,128]{1,0:T(8,128)(2,1)S(1)}, bf16[544,128]{1,0:T(8,128)(2,1)S(1)}, u32[]{:S(2)}, u32[]{:S(2)}) %collective-permute-start.4) | collective-permute-done | bytes 139296 | tf_op jit(solution)/shard_map/ppermute | solution.py:488
  31.2 1.5 sums.1
  32.7 3.5 %all-to-all-start.1 = ((bf16[4,512,128]{2,1,0:T(8,128)(2,1)}), bf16[4,512,128]{2,1,0:T(8,128)(2,1)S(1)}, u32[]{:S(2)}, u32[]{:S(2)}) async-start(bf16[4,512,128]{2,1,0:T(8,128)(2,1)} %sums.1), calls=%async_computation.1 | async-start | bytes 1048576 | tf_op jit(solution)/shard_map/all_to_all | solution.py:492
  36.3 0.7 dynamic-slice_bitcast_fusion
  36.9 2.9 %collective-permute-start.3 = (bf16[128,384]{1,0:T(8,128)(2,1)S(1)}, bf16[128,384]{1,0:T(8,128)(2,1)S(1)}, u32[]{:S(2)}, u32[]{:S(2)}) collective-permute-start(bf16[128,384]{1,0:T(8,128)(2,1)S(1)} %get-tuple-element.64), channel_id=1, source_target_pairs={{0,6},{2,4},{4,2},{6,0},{8,14},{10,12},{12,10},{14,8},{1,7},{3,5},... | collective-permute-start | bytes 294920 | tf_op jit(solution)/shard_map/ppermute | solution.py:413
  40.4 8.1 %collective-permute-done.3 = bf16[128,384]{1,0:T(8,128)(2,1)S(1)} collective-permute-done((bf16[128,384]{1,0:T(8,128)(2,1)S(1)}, bf16[128,384]{1,0:T(8,128)(2,1)S(1)}, u32[]{:S(2)}, u32[]{:S(2)}) %collective-permute-start.3) | collective-permute-done | bytes 98336 | tf_op jit(solution)/shard_map/ppermute | solution.py:413
  49.2 1.1 pad_maximum_fusion.2.resid_ref
  50.3 1.0 copy-done.12
  51.4 1.0 attention.1
  52.4 1.2 collective-permute-start.7
  53.6 0.9 collective-permute-start.8
  54.5 1.1 collective-permute-start.5
  55.6 0.9 collective-permute-start.6
  57.4 4.3 %collective-permute-done.7 = bf16[64,2048]{1,0:T(8,128)(2,1)S(1)} collective-permute-done((bf16[64,2048]{1,0:T(8,128)(2,1)S(1)}, bf16[64,2048]{1,0:T(8,128)(2,1)S(1)}, u32[]{:S(2)}, u32[]{:S(2)}) %collective-permute-start.7) | collective-permute-done | bytes 262176 | tf_op jit(solution)/shard_map/ppermute | solution.py:444
  61.7 1.1 collective-permute-start.11
  62.8 0.9 collective-permute-start.12
  63.7 3.6 %collective-permute-done.5 = bf16[64,2048]{1,0:T(8,128)(2,1)S(1)} collective-permute-done((bf16[64,2048]{1,0:T(8,128)(2,1)S(1)}, bf16[64,2048]{1,0:T(8,128)(2,1)S(1)}, u32[]{:S(2)}, u32[]{:S(2)}) %collective-permute-start.5) | collective-permute-done | bytes 262176 | tf_op jit(solution)/shard_map/ppermute | solution.py:444
  67.3 1.1 collective-permute-start.9
  68.4 0.9 collective-permute-start.10
  70.8 2.1 %collective-permute-done.11 = bf16[64,2048]{1,0:T(8,128)(2,1)S(1)} collective-permute-done((bf16[64,2048]{1,0:T(8,128)(2,1)S(1)}, bf16[64,2048]{1,0:T(8,128)(2,1)S(1)}, u32[]{:S(2)}, u32[]{:S(2)}) %collective-permute-start.11) | collective-permute-done | bytes 262176 | tf_op jit(solution)/shard_map/ppermute | solution.py:444
  72.9 1.1 collective-permute-start.15
  74.0 0.9 collective-permute-start.16
  75.0 3.6 %collective-permute-done.9 = bf16[64,2048]{1,0:T(8,128)(2,1)S(1)} collective-permute-done((bf16[64,2048]{1,0:T(8,128)(2,1)S(1)}, bf16[64,2048]{1,0:T(8,128)(2,1)S(1)}, u32[]{:S(2)}, u32[]{:S(2)}) %collective-permute-start.9) | collective-permute-done | bytes 262176 | tf_op jit(solution)/shard_map/ppermute | solution.py:444
  78.5 1.1 collective-permute-start.13
  79.6 0.9 collective-permute-start.14
  82.0 3.2 %collective-permute-done.16 = bf16[64,2048]{1,0:T(8,128)(2,1)S(1)} collective-permute-done((bf16[64,2048]{1,0:T(8,128)(2,1)S(1)}, bf16[64,2048]{1,0:T(8,128)(2,1)S(1)}, u32[]{:S(2)}, u32[]{:S(2)}) %collective-permute-start.16) | collective-permute-done | bytes 262176 | tf_op jit(solution)/shard_map/ppermute | solution.py:447
  85.3 0.9 collective-permute-start.18
  86.2 1.4 collective-permute-done.13
  87.6 2.3 %collective-permute-start.17 = (bf16[64,2048]{1,0:T(8,128)(2,1)S(1)}, bf16[64,2048]{1,0:T(8,128)(2,1)S(1)}, u32[]{:S(2)}, u32[]{:S(2)}) collective-permute-start(bf16[64,2048]{1,0:T(8,128)(2,1)S(1)} %collective-permute-done.13), channel_id=1, source_target_pairs={{0,4},{4,8},{8,12},{12,14},{14,10},{10,6},{6,2},{2,0},{1,5},{5,9},... | collective-permute-start | bytes 786440 | tf_op jit(solution)/shard_map/ppermute | solution.py:444
  92.0 2.8 %collective-permute-done.17 = bf16[64,2048]{1,0:T(8,128)(2,1)S(1)} collective-permute-done((bf16[64,2048]{1,0:T(8,128)(2,1)S(1)}, bf16[64,2048]{1,0:T(8,128)(2,1)S(1)}, u32[]{:S(2)}, u32[]{:S(2)}) %collective-permute-start.17) | collective-permute-done | bytes 262176 | tf_op jit(solution)/shard_map/ppermute | solution.py:444
  95.8 1.7 collective-permute-done.19.other_ref
  97.5 1.5 dispatch.1
  99.0 0.8 collective-permute-start.20
  99.7 2.6 %collective-permute-start.21 = (bf16[144,384]{1,0:T(8,128)(2,1)S(1)}, bf16[144,384]{1,0:T(8,128)(2,1)S(1)}, u32[]{:S(2)}, u32[]{:S(2)}) collective-permute-start(bf16[144,384]{1,0:T(8,128)(2,1)S(1)} %get-tuple-element.37), channel_id=1, source_target_pairs={{0,4},{2,6},{4,0},{6,2},{8,12},{10,14},{12,8},{14,10},{1,5},{3,7},... | collective-permute-start | bytes 331784 | tf_op jit(solution)/shard_map/ppermute | solution.py:413
  102.9 1.2 collective-permute-done.20
  104.1 1.6 collective-permute-done.21
  105.8 2.6 %collective-permute-done.22 = bf16[144,384]{1,0:T(8,128)(2,1)S(1)} collective-permute-done((bf16[144,384]{1,0:T(8,128)(2,1)S(1)}, bf16[144,384]{1,0:T(8,128)(2,1)S(1)}, u32[]{:S(2)}, u32[]{:S(2)}) %collective-permute-start.22) | collective-permute-done | bytes 110624 | tf_op jit(solution)/shard_map/ppermute | solution.py:413
  108.6 2.5 %collective-permute-start.24 = (bf16[144,384]{1,0:T(8,128)(2,1)S(1)}, bf16[144,384]{1,0:T(8,128)(2,1)S(1)}, u32[]{:S(2)}, u32[]{:S(2)}) collective-permute-start(bf16[144,384]{1,0:T(8,128)(2,1)S(1)} %get-tuple-element.40), channel_id=1, source_target_pairs={{0,8},{2,10},{4,12},{6,14},{8,0},{10,2},{12,4},{14,6},{1,9},{3,11}... | collective-permute-start | bytes 331784 | tf_op jit(solution)/shard_map/ppermute | solution.py:413
  111.2 0.8 collective-permute-start.25
  111.9 2.6 %collective-permute-start.26 = (bf16[144,384]{1,0:T(8,128)(2,1)S(1)}, bf16[144,384]{1,0:T(8,128)(2,1)S(1)}, u32[]{:S(2)}, u32[]{:S(2)}) collective-permute-start(bf16[144,384]{1,0:T(8,128)(2,1)S(1)} %get-tuple-element.42), channel_id=1, source_target_pairs={{0,12},{2,14},{4,8},{6,10},{8,4},{10,6},{12,0},{14,2},{1,13},{3,15... | collective-permute-start | bytes 331784 | tf_op jit(solution)/shard_map/ppermute | solution.py:413
  114.5 1.8 collective-permute-start.27
  116.4 5.0 %copy-done.2 = bf16[3072,2304]{1,0:T(8,128)(2,1)S(1)} copy-done((bf16[3072,2304]{1,0:T(8,128)(2,1)S(1)}, bf16[3072,2304]{1,0:T(8,128)(2,1)}, u32[]{:S(2)}) %copy-start.2) | copy-done | bytes 14155800
  121.4 4.6 %near_gate.1 = (f32[288,2304]{1,0:T(8,128)S(1)}, f32[288,128]{1,0:T(8,128)S(1)}) custom-call(s32[6]{0:T(128)S(1)} %get-tuple-element.69.info_ref, bf16[4,144,384]{2,1,0:T(8,128)(2,1)S(1)} %pad_maximum_fusion.own_ref.a, bf16[4,144,384]{2,1,0:T(8,128)(2,1)S(1)} %collective-permute-done.23.other_ref.b, f32[1,1536]{1,0:T(1,128)S(1)} %get-tuple-element.68.gain_ref, ...), custom_call_target="tpu_custom_call" | custom-call | flops 2038431744 | bytes 7077888 | tf_op jit(solution)/shard_map/near_gate/pallas_call | solution.py:343
  126.0 1.6 collective-permute-done.25
  127.8 5.0 %copy-done.3 = bf16[3072,2304]{1,0:T(8,128)(2,1)S(1)} copy-done((bf16[3072,2304]{1,0:T(8,128)(2,1)S(1)}, bf16[3072,2304]{1,0:T(8,128)(2,1)}, u32[]{:S(2)}) %copy-start.3) | copy-done | bytes 14155800
  132.8 4.9 %near_up.1 = (f32[288,2304]{1,0:T(8,128)S(1)}, f32[288,128]{1,0:T(8,128)}) custom-call(s32[6]{0:T(128)S(1)} %get-tuple-element.69.info_ref, bf16[4,144,384]{2,1,0:T(8,128)(2,1)S(1)} %pad_maximum_fusion.own_ref.a, bf16[4,144,384]{2,1,0:T(8,128)(2,1)S(1)} %collective-permute-done.23.other_ref.b, f32[1,1536]{1,0:T(1,128)S(1)} %get-tuple-element.68.gain_ref, ...), custom_call_target="tpu_custom_call" | custom-call | flops 2038431744 | bytes 7077888 | tf_op jit(solution)/shard_map/near_up/pallas_call | solution.py:343
  137.7 16.3 %experts_second.1 = (bf16[288,1536]{1,0:T(8,128)(2,1)S(1)}, bf16[288,1536]{1,0:T(8,128)(2,1)S(1)}) custom-call(s32[6]{0:T(128)S(1)} %get-tuple-element.70.info_ref, bf16[4,144,384]{2,1,0:T(8,128)(2,1)S(1)} %pad_maximum_fusion.1.own_ref.c, bf16[4,144,384]{2,1,0:T(8,128)(2,1)S(1)} %collective-permute-done.28.other_ref.d, ...), custom_call_target="tpu_custom_call" | custom-call | flops 8153726976 | bytes 28311552 | tf_op jit(solution)/shard_map/experts_second/pallas_call | solution.py:371
  154.5 2.1 %collective-permute-done.29.theirs_ref = bf16[288,1536]{1,0:T(8,128)(2,1)S(1)} collective-permute-done((bf16[288,1536]{1,0:T(8,128)(2,1)S(1)}, bf16[288,1536]{1,0:T(8,128)(2,1)S(1)}, u32[]{:S(2)}, u32[]{:S(2)}) %collective-permute-start.29) | collective-permute-done | bytes 884768 | tf_op jit(solution)/shard_map/ppermute | solution.py:24
  156.6 1.8 weigh.1
  158.4 1.2 collective-permute-start.30
  159.6 4.9 %collective-permute-start.31 = (bf16[144,384]{1,0:T(8,128)(2,1)S(1)}, bf16[144,384]{1,0:T(8,128)(2,1)S(1)}, u32[]{:S(2)}, u32[]{:S(2)}) collective-permute-start(bf16[144,384]{1,0:T(8,128)(2,1)S(1)} %get-tuple-element.55), channel_id=1, source_target_pairs={{0,4},{2,6},{4,0},{6,2},{8,12},{10,14},{12,8},{14,10},{1,5},{3,7},... | collective-permute-start | bytes 331784 | tf_op jit(solution)/shard_map/ppermute | solution.py:413
  165.0 2.9 %collective-permute-start.33 = (bf16[144,384]{1,0:T(8,128)(2,1)S(1)}, bf16[144,384]{1,0:T(8,128)(2,1)S(1)}, u32[]{:S(2)}, u32[]{:S(2)}) collective-permute-start(bf16[144,384]{1,0:T(8,128)(2,1)S(1)} %get-tuple-element.57), channel_id=1, source_target_pairs={{0,8},{2,10},{4,12},{6,14},{8,0},{10,2},{12,4},{14,6},{1,9},{3,11}... | collective-permute-start | bytes 331784 | tf_op jit(solution)/shard_map/ppermute | solution.py:413
  168.6 2.4 %collective-permute-start.35 = (bf16[144,384]{1,0:T(8,128)(2,1)S(1)}, bf16[144,384]{1,0:T(8,128)(2,1)S(1)}, u32[]{:S(2)}, u32[]{:S(2)}) collective-permute-start(bf16[144,384]{1,0:T(8,128)(2,1)S(1)} %get-tuple-element.59), channel_id=1, source_target_pairs={{0,12},{2,14},{4,8},{6,10},{8,4},{10,6},{12,0},{14,2},{1,13},{3,15... | collective-permute-start | bytes 331784 | tf_op jit(solution)/shard_map/ppermute | solution.py:413
  170.9 1.8 collective-permute-start.36
  172.7 1.7 collective-permute-done.32.refs_3_
  174.4 10.2 %collective-permute-done.34.refs_5_ = bf16[144,384]{1,0:T(8,128)(2,1)S(1)} collective-permute-done((bf16[144,384]{1,0:T(8,128)(2,1)S(1)}, bf16[144,384]{1,0:T(8,128)(2,1)S(1)}, u32[]{:S(2)}, u32[]{:S(2)}) %collective-permute-start.34) | collective-permute-done | bytes 110624 | tf_op jit(solution)/shard_map/ppermute | solution.py:413
  184.5 2.3 %combine.1 = bf16[128,1536]{1,0:T(8,128)(2,1)} custom-call(s32[6]{0:T(128)S(1)} %stack.74.flags_ref, s32[2,128]{1,0:T(2,128)S(1)} %bitcast.123, bf16[144,384]{1,0:T(8,128)(2,1)S(1)} %get-tuple-element.53.refs_0_, bf16[144,384]{1,0:T(8,128)(2,1)S(1)} %collective-permute-done.30.refs_1_, bf16[144,384]{1,0:T(8,128)(2,1)S(1)} %collective-permute-done.31.refs_2_, ...), custom_call_target="tpu_custom_call" | custom-call | tf_op jit(solution)/shard_map/combine/pallas_call | solution.py:401
  (92 shorter events, 11.9 us)
Async XLA Ops:
  0.0 56.6 %copy-start = (bf16[2048,384]{1,0:T(8,128)(2,1)S(1)}, bf16[2048,384]{1,0:T(8,128)(2,1)}, u32[]{:S(2)}) copy-start(bf16[2048,384]{1,0:T(8,128)(2,1)} %param.17) | copy-start | bytes 4718596
  0.0 1.2 copy-start.4
  1.2 1.0 copy-start.6
  2.2 0.7 copy-start.14
  2.9 0.7 copy-start.16
  3.6 7.2 %copy-start.17 = (bf16[128,1536]{1,0:T(8,128)(2,1)S(1)}, bf16[128,1536]{1,0:T(8,128)(2,1)}, u32[]{:S(2)}) copy-start(bf16[128,1536]{1,0:T(8,128)(2,1)} %param.15) | copy-start | bytes 1179652
  5.5 17.7 %all-to-all-start = ((bf16[4,528,128]{2,1,0:T(8,128)(2,1)}), bf16[4,528,128]{2,1,0:T(8,128)(2,1)S(1)}, u32[]{:S(2)}, u32[]{:S(2)}) async-start(bf16[4,528,128]{2,1,0:T(8,128)(2,1)} %states.1), calls=%async_computation | async-start | bytes 1081344 | tf_op jit(solution)/shard_map/all_to_all | solution.py:484
  10.7 25.4 %collective-permute-start = (bf16[128,1536]{1,0:T(8,128)(2,1)S(1)}, bf16[128,1536]{1,0:T(8,128)(2,1)}, u32[]{:S(2)}, u32[]{:S(2)}) collective-permute-start(bf16[128,1536]{1,0:T(8,128)(2,1)S(1)} %copy-done.17), channel_id=1, source_target_pairs={{1,8},{3,10},{5,12},{7,14},{8,1},{10,3},{12,5},{14,7},{17,24},{19,... | collective-permute-start | bytes 1179656 | tf_op jit(solution)/shard_map/ppermute | solution.py:476
  23.2 9.4 %copy-start.10 = (bf16[544,128]{1,0:T(8,128)(2,1)}, bf16[544,128]{1,0:T(8,128)(2,1)S(1)}, u32[]{:S(2)}) copy-start(bf16[544,128]{1,0:T(8,128)(2,1)S(1)} %totals.1.notes_ref) | copy-start | bytes 417796
  23.2 8.0 %collective-permute-start.4 = (bf16[544,128]{1,0:T(8,128)(2,1)S(1)}, bf16[544,128]{1,0:T(8,128)(2,1)S(1)}, u32[]{:S(2)}, u32[]{:S(2)}) collective-permute-start(bf16[544,128]{1,0:T(8,128)(2,1)S(1)} %totals.1.notes_ref), channel_id=1, source_target_pairs={{0,8},{2,10},{4,12},{6,14},{8,0},{10,2},{12,4},{14,6},{1,9},{3,11}... | collective-permute-start | bytes 417800 | tf_op jit(solution)/shard_map/ppermute | solution.py:488
  31.2 1.5 copy-start.8
  32.7 17.6 %all-to-all-start.1 = ((bf16[4,512,128]{2,1,0:T(8,128)(2,1)}), bf16[4,512,128]{2,1,0:T(8,128)(2,1)S(1)}, u32[]{:S(2)}, u32[]{:S(2)}) async-start(bf16[4,512,128]{2,1,0:T(8,128)(2,1)} %sums.1), calls=%async_computation.1 | async-start | bytes 1048576 | tf_op jit(solution)/shard_map/all_to_all | solution.py:492
  36.1 14.1 %copy-start.5 = (bf16[128,2048]{1,0:T(8,128)(2,1)S(1)}, bf16[128,2048]{1,0:T(8,128)(2,1)}, u32[]{:S(2)}) copy-start(bf16[128,2048]{1,0:T(8,128)(2,1)} %k_ref.1) | copy-start | bytes 1572868
  36.2 14.1 %copy-start.7 = (bf16[128,2048]{1,0:T(8,128)(2,1)S(1)}, bf16[128,2048]{1,0:T(8,128)(2,1)}, u32[]{:S(2)}) copy-start(bf16[128,2048]{1,0:T(8,128)(2,1)} %v_ref.1) | copy-start | bytes 1572868
  36.2 14.1 %copy-start.13 = (f32[2048]{0:T(1024)S(1)}, f32[2048]{0:T(1024)}, u32[]{:S(2)}) copy-start(f32[2048]{0:T(1024)} %param.16) | copy-start | bytes 24580
  36.9 11.6 %collective-permute-start.3 = (bf16[128,384]{1,0:T(8,128)(2,1)S(1)}, bf16[128,384]{1,0:T(8,128)(2,1)S(1)}, u32[]{:S(2)}, u32[]{:S(2)}) collective-permute-start(bf16[128,384]{1,0:T(8,128)(2,1)S(1)} %get-tuple-element.64), channel_id=1, source_target_pairs={{0,6},{2,4},{4,2},{6,0},{8,14},{10,12},{12,10},{14,8},{1,7},{3,5},... | collective-permute-start | bytes 294920 | tf_op jit(solution)/shard_map/ppermute | solution.py:413
  39.8 9.1 %collective-permute-start.2 = (bf16[128,384]{1,0:T(8,128)(2,1)S(1)}, bf16[128,384]{1,0:T(8,128)(2,1)}, u32[]{:S(2)}, u32[]{:S(2)}) collective-permute-start(bf16[128,384]{1,0:T(8,128)(2,1)S(1)} %get-tuple-element.65), channel_id=1, source_target_pairs={{0,4},{2,6},{4,0},{6,2},{8,12},{10,14},{12,8},{14,10},{1,5},{3,7},... | collective-permute-start | bytes 294920 | tf_op jit(solution)/shard_map/ppermute | solution.py:413
  40.4 8.5 %collective-permute-start.1 = (bf16[128,384]{1,0:T(8,128)(2,1)S(1)}, bf16[128,384]{1,0:T(8,128)(2,1)}, u32[]{:S(2)}, u32[]{:S(2)}) collective-permute-start(bf16[128,384]{1,0:T(8,128)(2,1)S(1)} %get-tuple-element.66), channel_id=1, source_target_pairs={{0,2},{2,0},{4,6},{6,4},{8,10},{10,8},{12,14},{14,12},{1,3},{3,1},... | collective-permute-start | bytes 294920 | tf_op jit(solution)/shard_map/ppermute | solution.py:413
  48.5 0.6 copy-start.18
  50.3 1.0 copy-start.12
  52.4 9.3 %collective-permute-start.7 = (bf16[64,2048]{1,0:T(8,128)(2,1)S(1)}, bf16[64,2048]{1,0:T(8,128)(2,1)S(1)}, u32[]{:S(2)}, u32[]{:S(2)}) collective-permute-start(bf16[64,2048]{1,0:T(8,128)(2,1)S(1)} %get-tuple-element.61), channel_id=1, source_target_pairs={{0,4},{4,8},{8,12},{12,14},{14,10},{10,6},{6,2},{2,0},{1,5},{5,9},... | collective-permute-start | bytes 786440 | tf_op jit(solution)/shard_map/ppermute | solution.py:444
  53.6 9.2 %collective-permute-start.8 = (bf16[64,2048]{1,0:T(8,128)(2,1)S(1)}, bf16[64,2048]{1,0:T(8,128)(2,1)S(1)}, u32[]{:S(2)}, u32[]{:S(2)}) collective-permute-start(bf16[64,2048]{1,0:T(8,128)(2,1)S(1)} %get-tuple-element.61), channel_id=1, source_target_pairs={{4,0},{8,4},{12,8},{14,12},{10,14},{6,10},{2,6},{0,2},{5,1},{9,5},... | collective-permute-start | bytes 786440 | tf_op jit(solution)/shard_map/ppermute | solution.py:447
  54.5 12.8 %collective-permute-start.5 = (bf16[64,2048]{1,0:T(8,128)(2,1)S(1)}, bf16[64,2048]{1,0:T(8,128)(2,1)S(1)}, u32[]{:S(2)}, u32[]{:S(2)}) collective-permute-start(bf16[64,2048]{1,0:T(8,128)(2,1)S(1)} %get-tuple-element.62), channel_id=1, source_target_pairs={{0,4},{4,8},{8,12},{12,14},{14,10},{10,6},{6,2},{2,0},{1,5},{5,9},... | collective-permute-start | bytes 786440 | tf_op jit(solution)/shard_map/ppermute | solution.py:444
  55.6 12.8 %collective-permute-start.6 = (bf16[64,2048]{1,0:T(8,128)(2,1)S(1)}, bf16[64,2048]{1,0:T(8,128)(2,1)S(1)}, u32[]{:S(2)}, u32[]{:S(2)}) collective-permute-start(bf16[64,2048]{1,0:T(8,128)(2,1)S(1)} %get-tuple-element.62), channel_id=1, source_target_pairs={{4,0},{8,4},{12,8},{14,12},{10,14},{6,10},{2,6},{0,2},{5,1},{9,5},... | collective-permute-start | bytes 786440 | tf_op jit(solution)/shard_map/ppermute | solution.py:447
  61.7 11.2 %collective-permute-start.11 = (bf16[64,2048]{1,0:T(8,128)(2,1)S(1)}, bf16[64,2048]{1,0:T(8,128)(2,1)S(1)}, u32[]{:S(2)}, u32[]{:S(2)}) collective-permute-start(bf16[64,2048]{1,0:T(8,128)(2,1)S(1)} %collective-permute-done.7), channel_id=1, source_target_pairs={{0,4},{4,8},{8,12},{12,14},{14,10},{10,6},{6,2},{2,0},{1,5},{5,9},... | collective-permute-start | bytes 786440 | tf_op jit(solution)/shard_map/ppermute | solution.py:444
  62.8 11.2 %collective-permute-start.12 = (bf16[64,2048]{1,0:T(8,128)(2,1)S(1)}, bf16[64,2048]{1,0:T(8,128)(2,1)S(1)}, u32[]{:S(2)}, u32[]{:S(2)}) collective-permute-start(bf16[64,2048]{1,0:T(8,128)(2,1)S(1)} %collective-permute-done.8), channel_id=1, source_target_pairs={{4,0},{8,4},{12,8},{14,12},{10,14},{6,10},{2,6},{0,2},{5,1},{9,5},... | collective-permute-start | bytes 786440 | tf_op jit(solution)/shard_map/ppermute | solution.py:447
  67.3 11.2 %collective-permute-start.9 = (bf16[64,2048]{1,0:T(8,128)(2,1)S(1)}, bf16[64,2048]{1,0:T(8,128)(2,1)S(1)}, u32[]{:S(2)}, u32[]{:S(2)}) collective-permute-start(bf16[64,2048]{1,0:T(8,128)(2,1)S(1)} %collective-permute-done.5), channel_id=1, source_target_pairs={{0,4},{4,8},{8,12},{12,14},{14,10},{10,6},{6,2},{2,0},{1,5},{5,9},... | collective-permute-start | bytes 786440 | tf_op jit(solution)/shard_map/ppermute | solution.py:444
  68.4 11.2 %collective-permute-start.10 = (bf16[64,2048]{1,0:T(8,128)(2,1)S(1)}, bf16[64,2048]{1,0:T(8,128)(2,1)S(1)}, u32[]{:S(2)}, u32[]{:S(2)}) collective-permute-start(bf16[64,2048]{1,0:T(8,128)(2,1)S(1)} %collective-permute-done.6), channel_id=1, source_target_pairs={{4,0},{8,4},{12,8},{14,12},{10,14},{6,10},{2,6},{0,2},{5,1},{9,5},... | collective-permute-start | bytes 786440 | tf_op jit(solution)/shard_map/ppermute | solution.py:447
  72.9 18.3 %collective-permute-start.15 = (bf16[64,2048]{1,0:T(8,128)(2,1)S(1)}, bf16[64,2048]{1,0:T(8,128)(2,1)S(1)}, u32[]{:S(2)}, u32[]{:S(2)}) collective-permute-start(bf16[64,2048]{1,0:T(8,128)(2,1)S(1)} %collective-permute-done.11), channel_id=1, source_target_pairs={{0,4},{4,8},{8,12},{12,14},{14,10},{10,6},{6,2},{2,0},{1,5},{5,9},... | collective-permute-start | bytes 786440 | tf_op jit(solution)/shard_map/ppermute | solution.py:444
  74.0 11.2 %collective-permute-start.16 = (bf16[64,2048]{1,0:T(8,128)(2,1)S(1)}, bf16[64,2048]{1,0:T(8,128)(2,1)S(1)}, u32[]{:S(2)}, u32[]{:S(2)}) collective-permute-start(bf16[64,2048]{1,0:T(8,128)(2,1)S(1)} %collective-permute-done.12), channel_id=1, source_target_pairs={{4,0},{8,4},{12,8},{14,12},{10,14},{6,10},{2,6},{0,2},{5,1},{9,5},... | collective-permute-start | bytes 786440 | tf_op jit(solution)/shard_map/ppermute | solution.py:447
  78.5 9.1 %collective-permute-start.13 = (bf16[64,2048]{1,0:T(8,128)(2,1)S(1)}, bf16[64,2048]{1,0:T(8,128)(2,1)S(1)}, u32[]{:S(2)}, u32[]{:S(2)}) collective-permute-start(bf16[64,2048]{1,0:T(8,128)(2,1)S(1)} %collective-permute-done.9), channel_id=1, source_target_pairs={{0,4},{4,8},{8,12},{12,14},{14,10},{10,6},{6,2},{2,0},{1,5},{5,9},... | collective-permute-start | bytes 786440 | tf_op jit(solution)/shard_map/ppermute | solution.py:444
  79.6 11.2 %collective-permute-start.14 = (bf16[64,2048]{1,0:T(8,128)(2,1)S(1)}, bf16[64,2048]{1,0:T(8,128)(2,1)S(1)}, u32[]{:S(2)}, u32[]{:S(2)}) collective-permute-start(bf16[64,2048]{1,0:T(8,128)(2,1)S(1)} %collective-permute-done.10), channel_id=1, source_target_pairs={{4,0},{8,4},{12,8},{14,12},{10,14},{6,10},{2,6},{0,2},{5,1},{9,5},... | collective-permute-start | bytes 786440 | tf_op jit(solution)/shard_map/ppermute | solution.py:447
  85.3 10.0 %collective-permute-start.18 = (bf16[64,2048]{1,0:T(8,128)(2,1)S(1)}, bf16[64,2048]{1,0:T(8,128)(2,1)S(1)}, u32[]{:S(2)}, u32[]{:S(2)}) collective-permute-start(bf16[64,2048]{1,0:T(8,128)(2,1)S(1)} %collective-permute-done.16), channel_id=1, source_target_pairs={{4,0},{8,4},{12,8},{14,12},{10,14},{6,10},{2,6},{0,2},{5,1},{9,5},... | collective-permute-start | bytes 786440 | tf_op jit(solution)/shard_map/ppermute | solution.py:447
  87.6 7.2 %collective-permute-start.17 = (bf16[64,2048]{1,0:T(8,128)(2,1)S(1)}, bf16[64,2048]{1,0:T(8,128)(2,1)S(1)}, u32[]{:S(2)}, u32[]{:S(2)}) collective-permute-start(bf16[64,2048]{1,0:T(8,128)(2,1)S(1)} %collective-permute-done.13), channel_id=1, source_target_pairs={{0,4},{4,8},{8,12},{12,14},{14,10},{10,6},{6,2},{2,0},{1,5},{5,9},... | collective-permute-start | bytes 786440 | tf_op jit(solution)/shard_map/ppermute | solution.py:444
  95.2 2.3 %copy-start.9 = (bf16[544,128]{1,0:T(8,128)(2,1)S(1)}, bf16[544,128]{1,0:T(8,128)(2,1)}, u32[]{:S(2)}) copy-start(bf16[544,128]{1,0:T(8,128)(2,1)} %copy-done.8) | copy-start | bytes 417796
  95.2 2.3 %copy-start.11 = (bf16[544,128]{1,0:T(8,128)(2,1)S(1)}, bf16[544,128]{1,0:T(8,128)(2,1)}, u32[]{:S(2)}) copy-start(bf16[544,128]{1,0:T(8,128)(2,1)} %copy-done.10) | copy-start | bytes 417796
  95.7 13.0 %copy-start.19 = (f32[3072]{0:T(1024)S(1)}, f32[3072]{0:T(1024)}, u32[]{:S(2)}) copy-start(f32[3072]{0:T(1024)} %param.18) | copy-start | bytes 36868
  95.7 1.8 collective-permute-start.19
  99.0 5.2 %collective-permute-start.20 = (bf16[144,384]{1,0:T(8,128)(2,1)S(1)}, bf16[144,384]{1,0:T(8,128)(2,1)S(1)}, u32[]{:S(2)}, u32[]{:S(2)}) collective-permute-start(bf16[144,384]{1,0:T(8,128)(2,1)S(1)} %get-tuple-element.36), channel_id=1, source_target_pairs={{0,2},{2,0},{4,6},{6,4},{8,10},{10,8},{12,14},{14,12},{1,3},{3,1},... | collective-permute-start | bytes 331784 | tf_op jit(solution)/shard_map/ppermute | solution.py:413
  99.7 6.0 %collective-permute-start.21 = (bf16[144,384]{1,0:T(8,128)(2,1)S(1)}, bf16[144,384]{1,0:T(8,128)(2,1)S(1)}, u32[]{:S(2)}, u32[]{:S(2)}) collective-permute-start(bf16[144,384]{1,0:T(8,128)(2,1)S(1)} %get-tuple-element.37), channel_id=1, source_target_pairs={{0,4},{2,6},{4,0},{6,2},{8,12},{10,14},{12,8},{14,10},{1,5},{3,7},... | collective-permute-start | bytes 331784 | tf_op jit(solution)/shard_map/ppermute | solution.py:413
  102.3 6.1 %collective-permute-start.22 = (bf16[144,384]{1,0:T(8,128)(2,1)S(1)}, bf16[144,384]{1,0:T(8,128)(2,1)S(1)}, u32[]{:S(2)}, u32[]{:S(2)}) collective-permute-start(bf16[144,384]{1,0:T(8,128)(2,1)S(1)} %get-tuple-element.38), channel_id=1, source_target_pairs={{0,6},{2,4},{4,2},{6,0},{8,14},{10,12},{12,10},{14,8},{1,7},{3,5},... | collective-permute-start | bytes 331784 | tf_op jit(solution)/shard_map/ppermute | solution.py:413
  108.5 7.9 %collective-permute-start.23 = (bf16[4,144,384]{2,1,0:T(8,128)(2,1)S(1)}, bf16[4,144,384]{2,1,0:T(8,128)(2,1)S(1)}, u32[]{:S(2)}, u32[]{:S(2)}) collective-permute-start(bf16[4,144,384]{2,1,0:T(8,128)(2,1)S(1)} %pad_maximum_fusion.own_ref.a), channel_id=1, source_target_pairs={{0,1},{1,0},{2,3},{3,2},{4,5},{5,4},{6,7},{7,6},{8,9},{9,8},{10,11... | collective-permute-start | bytes 1327112 | tf_op jit(solution)/shard_map/ppermute | solution.py:24
  108.6 17.4 %collective-permute-start.24 = (bf16[144,384]{1,0:T(8,128)(2,1)S(1)}, bf16[144,384]{1,0:T(8,128)(2,1)S(1)}, u32[]{:S(2)}, u32[]{:S(2)}) collective-permute-start(bf16[144,384]{1,0:T(8,128)(2,1)S(1)} %get-tuple-element.40), channel_id=1, source_target_pairs={{0,8},{2,10},{4,12},{6,14},{8,0},{10,2},{12,4},{14,6},{1,9},{3,11}... | collective-permute-start | bytes 331784 | tf_op jit(solution)/shard_map/ppermute | solution.py:413
  111.2 16.5 %collective-permute-start.25 = (bf16[144,384]{1,0:T(8,128)(2,1)S(1)}, bf16[144,384]{1,0:T(8,128)(2,1)S(1)}, u32[]{:S(2)}, u32[]{:S(2)}) collective-permute-start(bf16[144,384]{1,0:T(8,128)(2,1)S(1)} %get-tuple-element.41), channel_id=1, source_target_pairs={{0,10},{2,8},{4,14},{6,12},{8,2},{10,0},{12,6},{14,4},{1,11},{3,9}... | collective-permute-start | bytes 331784 | tf_op jit(solution)/shard_map/ppermute | solution.py:413
  111.9 15.7 %collective-permute-start.26 = (bf16[144,384]{1,0:T(8,128)(2,1)S(1)}, bf16[144,384]{1,0:T(8,128)(2,1)S(1)}, u32[]{:S(2)}, u32[]{:S(2)}) collective-permute-start(bf16[144,384]{1,0:T(8,128)(2,1)S(1)} %get-tuple-element.42), channel_id=1, source_target_pairs={{0,12},{2,14},{4,8},{6,10},{8,4},{10,6},{12,0},{14,2},{1,13},{3,15... | collective-permute-start | bytes 331784 | tf_op jit(solution)/shard_map/ppermute | solution.py:413
  114.5 13.1 %collective-permute-start.27 = (bf16[144,384]{1,0:T(8,128)(2,1)S(1)}, bf16[144,384]{1,0:T(8,128)(2,1)S(1)}, u32[]{:S(2)}, u32[]{:S(2)}) collective-permute-start(bf16[144,384]{1,0:T(8,128)(2,1)S(1)} %get-tuple-element.43), channel_id=1, source_target_pairs={{0,14},{2,12},{4,10},{6,8},{8,6},{10,4},{12,2},{14,0},{1,15},{3,13... | collective-permute-start | bytes 331784 | tf_op jit(solution)/shard_map/ppermute | solution.py:413
  116.4 5.0 %copy-start.2 = (bf16[3072,2304]{1,0:T(8,128)(2,1)S(1)}, bf16[3072,2304]{1,0:T(8,128)(2,1)}, u32[]{:S(2)}) copy-start(bf16[3072,2304]{1,0:T(8,128)(2,1)} %gate_hbm.1) | copy-start | bytes 42467332
  127.7 10.0 %collective-permute-start.28 = (bf16[4,144,384]{2,1,0:T(8,128)(2,1)S(1)}, bf16[4,144,384]{2,1,0:T(8,128)(2,1)S(1)}, u32[]{:S(2)}, u32[]{:S(2)}) collective-permute-start(bf16[4,144,384]{2,1,0:T(8,128)(2,1)S(1)} %pad_maximum_fusion.1.own_ref.c), channel_id=1, source_target_pairs={{0,1},{1,0},{2,3},{3,2},{4,5},{5,4},{6,7},{7,6},{8,9},{9,8},{10,11... | collective-permute-start | bytes 1327112 | tf_op jit(solution)/shard_map/ppermute | solution.py:24
  127.8 5.0 %copy-start.3 = (bf16[3072,2304]{1,0:T(8,128)(2,1)S(1)}, bf16[3072,2304]{1,0:T(8,128)(2,1)}, u32[]{:S(2)}) copy-start(bf16[3072,2304]{1,0:T(8,128)(2,1)} %up_hbm.1) | copy-start | bytes 42467332
  154.0 2.6 %collective-permute-start.29 = (bf16[288,1536]{1,0:T(8,128)(2,1)S(1)}, bf16[288,1536]{1,0:T(8,128)(2,1)S(1)}, u32[]{:S(2)}, u32[]{:S(2)}) collective-permute-start(bf16[288,1536]{1,0:T(8,128)(2,1)S(1)} %get-tuple-element.52), channel_id=1, source_target_pairs={{0,1},{1,0},{2,3},{3,2},{4,5},{5,4},{6,7},{7,6},{8,9},{9,8},{10,11... | collective-permute-start | bytes 2654216 | tf_op jit(solution)/shard_map/ppermute | solution.py:24
  156.6 27.9 %copy-start.15 = (s32[128,2]{0,1:T(2,128)S(1)}, s32[128,2]{0,1:T(2,128)}, u32[]{:S(2)}) copy-start(s32[128,2]{0,1:T(2,128)} %param.19) | copy-start | bytes 3076
  156.6 30.3 %copy-start.1 = (bf16[2048,384]{1,0:T(8,128)(2,1)S(1)}, bf16[2048,384]{1,0:T(8,128)(2,1)}, u32[]{:S(2)}) copy-start(bf16[2048,384]{1,0:T(8,128)(2,1)} %param.17) | copy-start | bytes 4718596
  158.4 10.1 %collective-permute-start.30 = (bf16[144,384]{1,0:T(8,128)(2,1)S(1)}, bf16[144,384]{1,0:T(8,128)(2,1)S(1)}, u32[]{:S(2)}, u32[]{:S(2)}) collective-permute-start(bf16[144,384]{1,0:T(8,128)(2,1)S(1)} %get-tuple-element.54), channel_id=1, source_target_pairs={{0,2},{2,0},{4,6},{6,4},{8,10},{10,8},{12,14},{14,12},{1,3},{3,1},... | collective-permute-start | bytes 331784 | tf_op jit(solution)/shard_map/ppermute | solution.py:413
  159.6 11.3 %collective-permute-start.31 = (bf16[144,384]{1,0:T(8,128)(2,1)S(1)}, bf16[144,384]{1,0:T(8,128)(2,1)S(1)}, u32[]{:S(2)}, u32[]{:S(2)}) collective-permute-start(bf16[144,384]{1,0:T(8,128)(2,1)S(1)} %get-tuple-element.55), channel_id=1, source_target_pairs={{0,4},{2,6},{4,0},{6,2},{8,12},{10,14},{12,8},{14,10},{1,5},{3,7},... | collective-permute-start | bytes 331784 | tf_op jit(solution)/shard_map/ppermute | solution.py:413
  164.5 9.8 %collective-permute-start.32 = (bf16[144,384]{1,0:T(8,128)(2,1)S(1)}, bf16[144,384]{1,0:T(8,128)(2,1)S(1)}, u32[]{:S(2)}, u32[]{:S(2)}) collective-permute-start(bf16[144,384]{1,0:T(8,128)(2,1)S(1)} %get-tuple-element.56), channel_id=1, source_target_pairs={{0,6},{2,4},{4,2},{6,0},{8,14},{10,12},{12,10},{14,8},{1,7},{3,5},... | collective-permute-start | bytes 331784 | tf_op jit(solution)/shard_map/ppermute | solution.py:413
  165.0 9.3 %collective-permute-start.33 = (bf16[144,384]{1,0:T(8,128)(2,1)S(1)}, bf16[144,384]{1,0:T(8,128)(2,1)S(1)}, u32[]{:S(2)}, u32[]{:S(2)}) collective-permute-start(bf16[144,384]{1,0:T(8,128)(2,1)S(1)} %get-tuple-element.57), channel_id=1, source_target_pairs={{0,8},{2,10},{4,12},{6,14},{8,0},{10,2},{12,4},{14,6},{1,9},{3,11}... | collective-permute-start | bytes 331784 | tf_op jit(solution)/shard_map/ppermute | solution.py:413
  168.0 16.6 %collective-permute-start.34 = (bf16[144,384]{1,0:T(8,128)(2,1)S(1)}, bf16[144,384]{1,0:T(8,128)(2,1)S(1)}, u32[]{:S(2)}, u32[]{:S(2)}) collective-permute-start(bf16[144,384]{1,0:T(8,128)(2,1)S(1)} %get-tuple-element.58), channel_id=1, source_target_pairs={{0,10},{2,8},{4,14},{6,12},{8,2},{10,0},{12,6},{14,4},{1,11},{3,9}... | collective-permute-start | bytes 331784 | tf_op jit(solution)/shard_map/ppermute | solution.py:413
  168.6 16.0 %collective-permute-start.35 = (bf16[144,384]{1,0:T(8,128)(2,1)S(1)}, bf16[144,384]{1,0:T(8,128)(2,1)S(1)}, u32[]{:S(2)}, u32[]{:S(2)}) collective-permute-start(bf16[144,384]{1,0:T(8,128)(2,1)S(1)} %get-tuple-element.59), channel_id=1, source_target_pairs={{0,12},{2,14},{4,8},{6,10},{8,4},{10,6},{12,0},{14,2},{1,13},{3,15... | collective-permute-start | bytes 331784 | tf_op jit(solution)/shard_map/ppermute | solution.py:413
  170.9 13.6 %collective-permute-start.36 = (bf16[144,384]{1,0:T(8,128)(2,1)S(1)}, bf16[144,384]{1,0:T(8,128)(2,1)S(1)}, u32[]{:S(2)}, u32[]{:S(2)}) collective-permute-start(bf16[144,384]{1,0:T(8,128)(2,1)S(1)} %get-tuple-element.60), channel_id=1, source_target_pairs={{0,14},{2,12},{4,10},{6,8},{8,6},{10,4},{12,2},{14,0},{1,15},{3,13... | collective-permute-start | bytes 331784 | tf_op jit(solution)/shard_map/ppermute | solution.py:413
where the time goes:
time: 189 us; the launch traced here: 187 us
  waiting for transfers between devices  71.8 us (38%)
  starting transfers between devices  55.7 us (29%)
  Pallas kernels  35.8 us (19%)
  local copies, waits for them, and re-layouts  15.9 us (8%)
  matrix products  5.85 us (3%)
    ppermute x17, starting transfers between devices, xor_shift(): lax.ppermute(x, 'seq', [(s, s ^ k) for s in range(lax.axis_size('seq'))])  29.5 us
    ppermute x17, waiting for transfers between devices, xor_shift(): lax.ppermute(x, 'seq', [(s, s ^ k) for s in range(lax.axis_size('seq'))])  27.4 us
    ppermute x7, waiting for transfers between devices, ring_project(): back[i] = lax.ppermute(back[i], 'seq', ahead)  17.9 us
    pallas_call x1, Pallas kernels, experts_second(): pl.pallas_call(functools.partial(second_kernel, tile, out_tile), out_shap...  16.3 us
    unnamed x40, local copies, waits for them, and re-layouts  15 us
    all_to_all x1, waiting for transfers between devices, per_device(): lax.all_to_all(states, 'seq', 0, 0, axis_index_groups=groups, tiled=True)  11 us
    pallas_call x7, Pallas kernels, on_chip(): pl.pallas_call(kernel, out_shape=out_shape, in_specs=[smem] * scalars + [...  10 us
    pallas_call x2, Pallas kernels, experts_first(): pl.pallas_call(functools.partial(first_kernel, tile), out_shape=(product,...  9.46 us
  transfers between devices with their start and end apart: 39, of which 20 were waited for; matrix products, arithmetic and copies ran while one was open for 4% of the time, Pallas kernels for 6%

commit v1 on v0

--- a/solution.py
+++ b/solution.py
@@ -75,13 +75,25 @@
     out_ref[width:] = jnp.concatenate(notes, axis=0).astype(BF)
 
 
-def before_kernel(flags_ref, x_ref, far_ref, out_ref):
-    blocks, width, _ = out_ref.shape
+def before_kernel(width, flags_ref, x_ref, far_ref, resid_ref, out_ref):
+    blocks = x_ref.shape[0]
+    tok = resid_ref.shape[-2]
+    split = len(resid_ref.shape) == 3
+    cols = resid_ref.shape[2] if split else resid_ref.shape[1] // blocks
     running = jnp.where(flags_ref[1] == 1, far_ref[:width].astype(F32), 0.0)
     for b in range(blocks):
-        out_ref[b] = running.astype(BF)
+        out_ref[b, :width] = running.astype(BF)
         if b < blocks - 1:
             running = running + x_ref[b, :width].astype(F32)
+        for m in range(0, cols, 128):
+            lanes = min(128, cols - m)
+            lo = width + m // 128 * tok
+            if split:
+                out_ref[b, lo : lo + tok, :lanes] = resid_ref[b, :, m : m + lanes]
+            else:
+                out_ref[b, lo : lo + tok, :lanes] = resid_ref[:, b * cols + m : b * cols + m + lanes]
+            if lanes < 128:
+                out_ref[b, lo : lo + tok, lanes:] = jnp.zeros((tok, 128 - lanes), BF)
 
 
 def attention_kernel(q_ref, k_ref, v_ref, before_ref, gain_ref, out_ref):
@@ -117,10 +129,15 @@
     outs, place_ref = refs[:-1], refs[-1]
     core = flags_ref[0]
     blocks, tok, cols = other_ref.shape
+    base = resid_ref.shape[1] - -(-cols // 128) * tok
     parts = []
     for b in range(blocks):
         own = acc_ref[core * blocks + b] + other_ref[b].astype(F32)
-        parts.append((own + resid_ref[b ^ flags_ref[2]].astype(F32)).astype(BF))
+        pieces = [
+            resid_ref[b, base + m * tok : base + (m + 1) * tok, : min(128, cols - m * 128)]
+            for m in range(-(-cols // 128))
+        ]
+        parts.append((own + jnp.concatenate(pieces, axis=1).astype(F32)).astype(BF))
     hidden = jnp.concatenate(parts, axis=0)
     first = notes_ref.shape[0] - NOTES * blocks
     near = core == flags_ref[1]
@@ -141,8 +158,8 @@
 
 def return_kernel(flags_ref, mine_ref, theirs_ref, x_refs, notes_ref, far_ref, outs, row_ref):
     core, upper, expert, leads = flags_ref[0], flags_ref[1], flags_ref[3], flags_ref[4]
-    near_own, near_other, rest_own, rest_other = x_refs
-    pieces, rows, width = near_own.shape
+    far_own, far_other, near_own, near_other = x_refs
+    pieces, rows, _ = near_own.shape
     blocks = rows // CAP
     tok = notes_ref.shape[1]
     first = notes_ref.shape[0] - NOTES * blocks
@@ -152,10 +169,13 @@
     wanted = expert.astype(F32)
     lead = jnp.where(leads == 1, 1.0, 0.0)
 
-    def hidden_piece(ref, m):
+    def piece_of(ref, m):
         if pieces == 1:
             return ref[0, :, m * piece_width : (m + 1) * piece_width].astype(F32)
         return ref[flags_ref[2] ^ m].astype(F32)
+
+    def hidden_piece(near, far, m):
+        return jnp.where(core == upper, piece_of(near, m), piece_of(far, m))
 
     for half in range(2):
         notes = jnp.where(upper == half, notes_ref[first:].astype(F32), far_ref[first:].astype(F32))
@@ -181,9 +201,9 @@
         parts = []
         for m in range(FOLD):
             lanes = slice(m * piece_width, (m + 1) * piece_width)
-            near = jnp.where(core == half, hidden_piece(near_own, m), hidden_piece(near_other, m))
-            rest = jnp.where(core == half, hidden_piece(rest_own, m), hidden_piece(rest_other, m))
-            hidden = jnp.where(core == upper, near, rest)
+            hidden = jnp.where(
+                core == half, hidden_piece(near_own, far_own, m), hidden_piece(near_other, far_other, m)
+            )
             out = mine_ref[at, lanes].astype(F32) + theirs_ref[at, lanes].astype(F32)
             parts.append(out * row_weight + hidden * row_first)
         for b in range(blocks):
@@ -200,7 +220,7 @@
     )
 
 
-def combine_kernel(per_expert, flags_ref, routes_ref, *refs):
+def combine_kernel(per_expert, order, flags_ref, routes_ref, *refs):
     backs, out_ref, place_ref = refs[:-2], refs[-2], refs[-1]
     folded, width = backs[0].shape
     tok = routes_ref.shape[1]
@@ -210,7 +230,7 @@
     place_ref[...] = jnp.where(hit, ranks_of(jnp.where(hit, 1.0, 0.0)), -float(folded))
     slot = lax.broadcasted_iota(jnp.int32, (folded, tok), 0).astype(F32)
     places = [
-        place_ref[pl.ds((flags_ref[5] ^ k) // per_expert, 1), :] for k in range(len(backs))
+        place_ref[pl.ds((flags_ref[5] ^ k) // per_expert, 1), :] for k in order
     ]
     back = jnp.concatenate([ref[...] for ref in backs], axis=0)
     for m in range(folded // CAP):
@@ -219,65 +239,27 @@
         out_ref[:, m * width : (m + 1) * width] = contract(pick, back, (0, 0)).astype(BF)
 
 
-def place_rows(info_ref, own_ref, other_ref, gain_ref, x_ref):
-    pieces, rows, width = own_ref.shape
-    core = info_ref[0]
-
-    def place(ref, base):
-        total = jnp.zeros((rows, 1), F32)
-        for p in range(pieces):
-            at = 0 if pieces == 1 else pl.multiple_of(info_ref[2 + p] * width, width)
-            wide = ref[p].astype(F32)
-            total = total + jnp.sum(wide * wide, axis=-1, keepdims=True)
-            gain = gain_ref[0:1, pl.ds(at, width)]
-            x_ref[pl.ds(base, rows), pl.ds(at, width)] = (wide * gain).astype(BF)
-        return total
-
-    own_total = place(own_ref, pl.multiple_of(core * rows, rows))
-    other_total = place(other_ref, pl.multiple_of((1 - core) * rows, rows))
-    low = jnp.where(core == 0, own_total, other_total)
-    high = jnp.where(core == 0, other_total, own_total)
-    return jnp.concatenate([low, high], axis=0)
-
-
-def weight_copies(info_ref, sources, buffers, sems, tile):
-    depth = buffers[0].shape[1]
-    base = pl.multiple_of(info_ref[1] * depth, depth)
-    copies = []
-    for i in range(buffers[0].shape[0]):
-        pair = []
-        for n, (source, buffer) in enumerate(zip(sources, buffers)):
-            piece = source.at[pl.ds(base, depth), pl.ds(i * tile, tile)]
-            copy = pltpu.make_async_copy(piece, buffer.at[i], sems.at[n, i])
-            copy.start()
-            pair.append(copy)
-        copies.append(pair)
-    return copies
-
-
-def first_kernel(
-    tile, info_ref, own_ref, other_ref, gain_ref, weight_hbm,
-    out_ref, total_out, x_ref, weight_ref, sems,
-):
-    copies = weight_copies(info_ref, (weight_hbm,), (weight_ref,), sems, tile)
-    total = place_rows(info_ref, own_ref, other_ref, gain_ref, x_ref)
-    total_out[...] = jnp.broadcast_to(total, total_out.shape)
-    x = x_ref[...]
-    for i, (copy,) in enumerate(copies):
-        copy.wait()
-        out_ref[:, i * tile : (i + 1) * tile] = dot(x, weight_ref[i])
-
-
-def second_kernel(
-    tile, out_tile, info_ref, own_ref, other_ref, gain_ref, gate_in, up_in, total_in,
-    gate_hbm, up_hbm, down_hbm,
+def moe_kernel(
+    info_ref, far_own, far_other, near_own, near_other, gain_ref, gate_hbm, up_hbm, down_hbm,
     mine_ref, theirs_ref, x_ref, inner_ref, gate_ref, up_ref, down_ref, sems, down_sems,
 ):
+    pieces, rows, width = near_own.shape
+    tiles, parts, depth, tile = gate_ref.shape
+    outs, _, out_tile = down_ref.shape
+    features = parts * depth
     core = info_ref[0]
-    copies = weight_copies(info_ref, (gate_hbm, up_hbm), (gate_ref, up_ref), sems, tile)
-    half = mine_ref.shape[1]
+    half = features // 2
+
+    copies = {}
+    for i in range(tiles):
+        for k in range(parts):
+            for n, (source, buffer) in enumerate(((gate_hbm, gate_ref), (up_hbm, up_ref))):
+                piece = source.at[pl.ds(k * depth, depth), pl.ds(i * tile, tile)]
+                copy = pltpu.make_async_copy(piece, buffer.at[i, k], sems.at[n, i, k])
+                copy.start()
+                copies[n, i, k] = copy
     downs = []
-    for i in range(2 * half // out_tile):
+    for i in range(outs):
         side = 1 - core if i * out_tile < half else core
         at = pl.multiple_of(side * half + i * out_tile % half, out_tile)
         copy = pltpu.make_async_copy(
@@ -285,24 +267,44 @@
         )
         copy.start()
         downs.append(copy)
-    total = place_rows(info_ref, own_ref, other_ref, gain_ref, x_ref)
-    features = 2 * half
-    scale = lax.rsqrt((total + total_in[:, 0:1]) / features + EPS)
-    x = x_ref[...]
-    for i, pair in enumerate(copies):
-        at = slice(i * tile, (i + 1) * tile)
-        pair[0].wait()
-        gate = (gate_in[:, at] + dot(x, gate_ref[i])) * scale
-        pair[1].wait()
-        upward = (up_in[:, at] + dot(x, up_ref[i])) * scale
-        inner_ref[:, at] = (gate / (1.0 + jnp.exp(-gate)) * upward).astype(BF)
+
+    def lane(p):
+        return pl.ds(pl.multiple_of(info_ref[1 + p] * width, width), width)
+
+    def place(refs, base):
+        total = jnp.zeros((rows, 1), F32)
+        for ref in refs:
+            for p in range(pieces):
+                wide = ref[p].astype(F32)
+                total = total + jnp.sum(wide * wide, axis=-1, keepdims=True)
+        scale = lax.rsqrt(total / features + EPS)
+        for n, ref in enumerate(refs):
+            for p in range(pieces):
+                at = lane(n * pieces + p)
+                value = ref[p].astype(F32) * scale * gain_ref[0:1, at]
+                x_ref[pl.ds(base, rows), at] = value.astype(BF)
+
+    place((far_own, near_own), pl.multiple_of(core * rows, rows))
+    place((far_other, near_other), pl.multiple_of((1 - core) * rows, rows))
+
+    for i in range(tiles):
+        sums = [None, None]
+        for k in range(parts):
+            x = x_ref[:, k * depth : (k + 1) * depth]
+            for n, weight_ref in ((0, gate_ref), (1, up_ref)):
+                copies[n, i, k].wait()
+                value = dot(x, weight_ref[i, k])
+                sums[n] = value if k == 0 else sums[n] + value
+        gate, upward = sums
+        inner_ref[:, i * tile : (i + 1) * tile] = (
+            gate / (1.0 + jnp.exp(-gate)) * upward
+        ).astype(BF)
     inner = inner_ref[...]
     for i, copy in enumerate(downs):
         copy.wait()
-        value = dot(inner, down_ref[i]).astype(BF)
         lo = i * out_tile % half
         out_ref = theirs_ref if i * out_tile < half else mine_ref
-        out_ref[:, lo : lo + out_tile] = value
+        out_ref[:, lo : lo + out_tile] = dot(inner, down_ref[i]).astype(BF)
 
 
 def tile_of(size):
@@ -331,62 +333,34 @@
     return joined
 
 
-def experts_first(name, info, own, other, gain, weight):
-    pieces, rows, width = own.shape
-    depth = pieces * width
-    hidden = weight.shape[1]
-    tile = tile_of(hidden)
-    smem = pl.BlockSpec(memory_space=pltpu.SMEM)
-    vmem = pl.BlockSpec(memory_space=pltpu.VMEM)
-    hbm = pl.BlockSpec(memory_space=pltpu.HBM)
-    product = jax.ShapeDtypeStruct((2 * rows, hidden), F32)
-    return pl.pallas_call(
-        functools.partial(first_kernel, tile),
-        out_shape=(product, jax.ShapeDtypeStruct((2 * rows, 128), F32)),
-        in_specs=[smem] + [vmem] * 3 + [hbm],
-        out_specs=(vmem,) * 2,
-        scratch_shapes=[
-            pltpu.VMEM((2 * rows, depth), BF),
-            pltpu.VMEM((hidden // tile, depth, tile), BF),
-            pltpu.SemaphoreType.DMA((1, hidden // tile)),
-        ],
-        compiler_params=pltpu.CompilerParams(vmem_limit_bytes=16 * MIB),
-        cost_estimate=pl.CostEstimate(
-            flops=4 * rows * depth * hidden, bytes_accessed=2 * depth * hidden, transcendentals=0
-        ),
-        name=name,
-    )(info, own, other, gain, weight)
-
-
-def experts_second(info, own, other, gate, upward, total, gain, w_gate, w_up, w_down):
-    pieces, rows, width = own.shape
-    depth = pieces * width
+def experts(info, far_own, far_other, near_own, near_other, gain, w_gate, w_up, w_down):
+    rows = near_own.shape[1]
     hidden, features = w_down.shape
-    tile, out_tile = tile_of(hidden), tile_of(features // 2)
+    tile, out_tile, parts = tile_of(hidden), tile_of(features // 2), 2
     smem = pl.BlockSpec(memory_space=pltpu.SMEM)
     vmem = pl.BlockSpec(memory_space=pltpu.VMEM)
     hbm = pl.BlockSpec(memory_space=pltpu.HBM)
     out = jax.ShapeDtypeStruct((2 * rows, features // 2), BF)
-    buffer = pltpu.VMEM((hidden // tile, depth, tile), BF)
+    buffer = pltpu.VMEM((hidden // tile, parts, features // parts, tile), BF)
     return pl.pallas_call(
-        functools.partial(second_kernel, tile, out_tile),
+        moe_kernel,
         out_shape=(out, out),
-        in_specs=[smem] + [vmem] * 6 + [hbm] * 3,
+        in_specs=[smem] + [vmem] * 5 + [hbm] * 3,
         out_specs=(vmem, vmem),
         scratch_shapes=[
-            pltpu.VMEM((2 * rows, depth), BF), pltpu.VMEM((2 * rows, hidden), BF), buffer, buffer,
+            pltpu.VMEM((2 * rows, features), BF), pltpu.VMEM((2 * rows, hidden), BF), buffer, buffer,
             pltpu.VMEM((features // out_tile, hidden, out_tile), BF),
-            pltpu.SemaphoreType.DMA((2, hidden // tile)),
+            pltpu.SemaphoreType.DMA((2, hidden // tile, parts)),
             pltpu.SemaphoreType.DMA((features // out_tile,)),
         ],
-        compiler_params=pltpu.CompilerParams(vmem_limit_bytes=40 * MIB),
+        compiler_params=pltpu.CompilerParams(vmem_limit_bytes=51 * MIB),
         cost_estimate=pl.CostEstimate(
-            flops=8 * rows * depth * hidden + 4 * rows * features * hidden,
-            bytes_accessed=4 * depth * hidden + 2 * features * hidden,
+            flops=12 * rows * features * hidden,
+            bytes_accessed=6 * features * hidden,
             transcendentals=2 * rows * hidden,
         ),
-        name="experts_second",
-    )(info, own, other, gain, gate, upward, total, w_gate, w_up, w_down)
+        name="experts",
+    )(info, far_own, far_other, near_own, near_other, gain, w_gate, w_up, w_down)
 
 
 def on_chip(kernel, name, out, *operands, scalars=0, hbm=0, scratch=(), room=1):
@@ -486,17 +460,15 @@
         functools.partial(total_kernel, width), "totals", ((width + half * NOTES, HD), BF), blocks
     )
     far_sum = lax.ppermute(own_sum, "seq", [(s, (s + half) % seq_count) for s in chips])
+    sliced = jnp.where(me // half == core, resid, crossed)
+    if cols % 128:
+        sliced = sliced.reshape(tok, half, cols).transpose(1, 0, 2)
+    chunks = -(-cols // 128)
     sums = on_chip(
-        before_kernel, "sums", ((half, width, HD), BF), flags, blocks, far_sum, scalars=1
+        functools.partial(before_kernel, width), "sums", ((half, width + chunks * tok, HD), BF),
+        flags, blocks, far_sum, sliced, scalars=1,
     )
     sums = lax.all_to_all(sums, "seq", 0, 0, axis_index_groups=groups, tiled=True)
-
-    held = jnp.where(me // half == core, resid, crossed)
-    columns = []
-    for k in range(half):
-        piece = lax.dynamic_slice_in_dim(held, ((me % half) ^ k) * cols, cols, 1)
-        columns.append(xor_shift(piece, k) if k else piece)
-    columns, sums = lax.optimization_barrier((jnp.stack(columns), sums))
     normed = on_chip(
         attention_kernel, "attention", ((tok, heads * HD), BF),
         query, keys, values, sums, attn_gain.reshape(1, heads * HD),
@@ -506,58 +478,40 @@
     other = swap_cores(theirs.astype(BF))
 
     rows = half * CAP
-    pieces = on_chip(
+    pieces = list(on_chip(
         functools.partial(dispatch_kernel, per_expert), "dispatch",
         [((rows, cols), BF)] * seq_count,
-        flags, acc, other, columns, own_sum, far_sum,
+        flags, acc, other, sums, own_sum, far_sum,
         scalars=1, room=half // 4, scratch=[pltpu.VMEM((EXPERTS, half * tok), F32)],
-    )
-    got = [pieces[0]] + [None] * (seq_count - 1)
-    for k in [half] + list(range(1, half)) + list(range(half + 1, seq_count)):
-        got[k] = xor_shift(pieces[k], k)
-
-    def part(ks):
-        own = jnp.stack([got[k] for k in ks])
+    ))
+    got = [None] * seq_count
+    for k in list(range(half, seq_count)) + list(range(half)):
+        got[k] = xor_shift(pieces[k], k) if k else pieces[0]
+    parts, places = [], []
+    for first in (half, 0):
+        turns = me ^ (first + jnp.arange(half))
+        own = jnp.stack(got[first : first + half])
         if cols % 128:
-            order = (me % half) ^ jnp.arange(half)
-            own = jnp.take(own, order, axis=0).transpose(1, 0, 2).reshape(1, rows, half * cols)
-        return own, swap_cores(own)
-
-    turns = (me % half) ^ jnp.arange(half)
-    side = me // half
-    gains = moe_gain.reshape(2, 1, half_width)
-
-    def info_of(which):
-        return jnp.concatenate([jnp.stack([core, which]), turns]).astype(jnp.int32)
-
-    near = part(range(half))
-    near_gain = lax.dynamic_index_in_dim(gains, side, 0, keepdims=False)
-    gate, total = by_rows(
-        functools.partial(experts_first, "near_gate", info_of(side)), rows, near,
-        (near_gain, w_gate),
-    )
-    waiting = lax.optimization_barrier((total, *got[half:]))
-    total, got[half:] = waiting[0], waiting[1:]
-    upward, _ = by_rows(
-        functools.partial(experts_first, "near_up", info_of(side)), rows, near, (near_gain, w_up)
-    )
-    rest = part(range(half, seq_count))
-    rest_gain = lax.dynamic_index_in_dim(gains, 1 - side, 0, keepdims=False)
+            own = jnp.take(own, turns % half, axis=0).transpose(1, 0, 2)
+            own = own.reshape(1, rows, half_width)
+            turns = turns[:1] // half
+        parts += [own, swap_cores(own)]
+        places.append(turns)
+    info = jnp.concatenate([core.reshape(1), *places]).astype(jnp.int32)
     mine, theirs = by_rows(
-        functools.partial(experts_second, info_of(1 - side)), rows,
-        (*rest, gate, upward, total), (rest_gain, w_gate, w_up, w_down),
+        functools.partial(experts, info), rows, parts,
+        (moe_gain.reshape(1, 2 * half_width), w_gate, w_up, w_down),
     )
     piece = half_width // FOLD
     out = on_chip(
         return_entry, "weigh", [((FOLD * CAP, piece), BF)] * seq_count,
-        flags, mine, swap_cores(theirs), *near, *rest, own_sum, far_sum,
+        flags, mine, swap_cores(theirs), *parts, own_sum, far_sum,
         scalars=1, room=half // 4, scratch=[pltpu.VMEM((seq_count, FOLD * CAP, piece), BF)],
     )
-    back = [out[0]] + [None] * (seq_count - 1)
-    for k in list(range(half, seq_count)) + list(range(1, half)):
-        back[k] = xor_shift(out[k], k)
+    order = list(range(half, seq_count)) + list(range(half))
+    back = [xor_shift(out[k], k) if k else out[0] for k in order]
     return on_chip(
-        functools.partial(combine_kernel, per_expert), "combine", ((tok, half_width), BF),
+        functools.partial(combine_kernel, per_expert, order), "combine", ((tok, half_width), BF),
         flags, routes_by_lane, *back,
         scalars=1, room=half // 4, scratch=[pltpu.VMEM((EXPERTS, tok), F32)],
     )

time: 189 us -> 181 us (0.958)
  waiting for transfers between devices: 71.8 us -> 84.5 us
  local copies, waits for them, and re-layouts: 15.9 us -> 5.57 us
  starting transfers between devices: 55.7 us -> 50.5 us
  Pallas kernels: 35.8 us -> 33.3 us
    all_to_all x1, waiting for transfers between devices: 0.01 us -> 12.4 us  [per_device(): lax.all_to_all(sums, 'seq', 0, 0, axis_index_groups=groups, tiled=True)]
    unnamed x40 -> x32, local copies, waits for them, and re-layouts: 15 us -> 5.29 us
    ppermute x17 -> x14, waiting for transfers between devices: 27.4 us -> 21.5 us  [xor_shift(): lax.ppermute(x, 'seq', [(s, s ^ k) for s in range(lax.axis_size('seq'))])]
    ppermute x7, waiting for transfers between devices: 4 us -> 7.76 us  [ring_project(): front[i] = lax.ppermute(front[i], 'seq', behind)]
    ppermute x17 -> x14, starting transfers between devices: 29.5 us -> 26.7 us  [xor_shift(): lax.ppermute(x, 'seq', [(s, s ^ k) for s in range(lax.axis_size('seq'))])]
    pallas_call x3 -> x1, Pallas kernels: 25.8 us -> 23 us  [experts(): pl.pallas_call(moe_kernel, out_shape=(out, out), in_specs=[smem] + [vmem]...]
    ppermute x7, starting transfers between devices: 6.43 us -> 4.27 us  [ring_project(): front[i] = lax.ppermute(front[i], 'seq', behind)]
    ppermute x4, waiting for transfers between devices: 3.77 us -> 5.91 us  [swap_cores(): return lax.ppermute(x, 'head', [(0, 1), (1, 0)])]
  transfers between devices with their start and end apart: 39 -> 36, of which waited for: 20 -> 21; matrix products, arithmetic and copies ran while one was open for 4% -> 3% of each run, Pallas kernels for 6% -> 0%
where the time goes in v1:
time: 181 us
  waiting for transfers between devices  84.5 us (47%)
  starting transfers between devices  50.5 us (28%)
  Pallas kernels  33.3 us (18%)
  matrix products  5.77 us (3%)
  local copies, waits for them, and re-layouts  5.57 us (3%)
    ppermute x14, starting transfers between devices, xor_shift(): lax.ppermute(x, 'seq', [(s, s ^ k) for s in range(lax.axis_size('seq'))])  26.7 us
    pallas_call x1, Pallas kernels, experts(): pl.pallas_call(moe_kernel, out_shape=(out, out), in_specs=[smem] + [vmem]...  23 us
    ppermute x14, waiting for transfers between devices, xor_shift(): lax.ppermute(x, 'seq', [(s, s ^ k) for s in range(lax.axis_size('seq'))])  21.5 us
    ppermute x7, waiting for transfers between devices, ring_project(): back[i] = lax.ppermute(back[i], 'seq', ahead)  17.5 us
    all_to_all x1, waiting for transfers between devices, per_device(): lax.all_to_all(sums, 'seq', 0, 0, axis_index_groups=groups, tiled=True)  12.4 us
    all_to_all x1, waiting for transfers between devices, per_device(): lax.all_to_all(states, 'seq', 0, 0, axis_index_groups=groups, tiled=True)  11.6 us
    pallas_call x7, Pallas kernels, on_chip(): pl.pallas_call(kernel, out_shape=out_shape, in_specs=[smem] * scalars + [...  10.2 us
    ppermute x7, starting transfers between devices, ring_project(): back[i] = lax.ppermute(back[i], 'seq', ahead)  9.53 us
  transfers between devices with their start and end apart: 36, of which 21 were waited for; matrix products, arithmetic and copies ran while one was open for 3% of the time, Pallas kernels for 0%

profile of v1, /device:TPU:0, one launch (start us, length us, event | category | flops | bytes accessed | tf_op | source)
XLA Modules:
  0.0 180.5 jit_solution(15328449504028875074)
XLA Ops:
  0.0 1.2 copy-done.1
  1.2 1.0 copy-done.3
  2.2 0.7 copy-done.11
  2.9 0.7 copy-done.13
  3.6 1.9 %states.1 = bf16[4,528,128]{2,1,0:T(8,128)(2,1)} custom-call(s32[2,128]{1,0:T(2,128)S(1)} %bitcast.112, f32[2,128]{1,0:T(2,128)S(1)} %bitcast.114, bf16[128,2048]{1,0:T(8,128)(2,1)S(1)} %copy-done.1, bf16[128,2048]{1,0:T(8,128)(2,1)S(1)} %copy-done.3), custom_call_target="tpu_custom_call" | custom-call | tf_op jit(solution)/shard_map/states/pallas_call | solution.py:375
  5.5 5.3 %all-to-all-start = ((bf16[4,528,128]{2,1,0:T(8,128)(2,1)}), bf16[4,528,128]{2,1,0:T(8,128)(2,1)S(1)}, u32[]{:S(2)}, u32[]{:S(2)}) async-start(bf16[4,528,128]{2,1,0:T(8,128)(2,1)} %states.1), calls=%async_computation | async-start | bytes 1081344 | tf_op jit(solution)/shard_map/all_to_all | solution.py:458
  10.8 0.7 collective-permute-start.1
  11.6 11.6 %all-to-all-done.x_ref = bf16[4,528,128]{2,1,0:T(8,128)(2,1)S(1)} async-done(((bf16[4,528,128]{2,1,0:T(8,128)(2,1)}), bf16[4,528,128]{2,1,0:T(8,128)(2,1)S(1)}, u32[]{:S(2)}, u32[]{:S(2)}) %all-to-all-start) | async-done | bytes 540704 | tf_op jit(solution)/shard_map/all_to_all | solution.py:458
  23.4 7.8 %collective-permute-done.far_ref = bf16[544,128]{1,0:T(8,128)(2,1)S(1)} collective-permute-done((bf16[544,128]{1,0:T(8,128)(2,1)S(1)}, bf16[544,128]{1,0:T(8,128)(2,1)S(1)}, u32[]{:S(2)}, u32[]{:S(2)}) %collective-permute-start) | collective-permute-done | bytes 139296 | tf_op jit(solution)/shard_map/ppermute | solution.py:462
  31.2 1.6 sums.1
  32.9 0.7 copy-done.5
  33.5 3.6 %all-to-all-start.1 = ((bf16[4,896,128]{2,1,0:T(8,128)(2,1)}), bf16[4,896,128]{2,1,0:T(8,128)(2,1)S(1)}, u32[]{:S(2)}, u32[]{:S(2)}) async-start(bf16[4,896,128]{2,1,0:T(8,128)(2,1)} %sums.1), calls=%async_computation.1 | async-start | bytes 1835008 | tf_op jit(solution)/shard_map/all_to_all | solution.py:471
  37.4 12.4 %all-to-all-done.1.before_ref.resid_ref = bf16[4,896,128]{2,1,0:T(8,128)(2,1)S(1)} async-done(((bf16[4,896,128]{2,1,0:T(8,128)(2,1)}), bf16[4,896,128]{2,1,0:T(8,128)(2,1)S(1)}, u32[]{:S(2)}, u32[]{:S(2)}) %all-to-all-start.1) | async-done | bytes 917536 | tf_op jit(solution)/shard_map/all_to_all | solution.py:471
  49.8 1.0 copy-done.9
  50.8 1.0 attention.1
  51.9 1.5 collective-permute-start.2
  53.3 0.6 collective-permute-start.3
  54.0 1.4 collective-permute-start.4
  55.4 0.6 collective-permute-start.5
  56.1 0.4 fusion.15
  56.5 0.4 fusion.14
  56.8 4.3 %collective-permute-done.2 = bf16[64,2048]{1,0:T(8,128)(2,1)S(1)} collective-permute-done((bf16[64,2048]{1,0:T(8,128)(2,1)S(1)}, bf16[64,2048]{1,0:T(8,128)(2,1)S(1)}, u32[]{:S(2)}, u32[]{:S(2)}) %collective-permute-start.2) | collective-permute-done | bytes 262176 | tf_op jit(solution)/shard_map/ppermute | solution.py:418
  61.2 1.3 collective-permute-start.6
  62.5 0.7 collective-permute-start.7
  63.2 3.6 %collective-permute-done.4 = bf16[64,2048]{1,0:T(8,128)(2,1)S(1)} collective-permute-done((bf16[64,2048]{1,0:T(8,128)(2,1)S(1)}, bf16[64,2048]{1,0:T(8,128)(2,1)S(1)}, u32[]{:S(2)}, u32[]{:S(2)}) %collective-permute-start.4) | collective-permute-done | bytes 262176 | tf_op jit(solution)/shard_map/ppermute | solution.py:418
  66.8 1.3 collective-permute-start.8
  68.5 0.4 fusion.12
  68.9 0.4 fusion.11
  69.2 0.7 collective-permute-start.9
  70.3 2.1 %collective-permute-done.6 = bf16[64,2048]{1,0:T(8,128)(2,1)S(1)} collective-permute-done((bf16[64,2048]{1,0:T(8,128)(2,1)S(1)}, bf16[64,2048]{1,0:T(8,128)(2,1)S(1)}, u32[]{:S(2)}, u32[]{:S(2)}) %collective-permute-start.6) | collective-permute-done | bytes 262176 | tf_op jit(solution)/shard_map/ppermute | solution.py:418
  72.4 1.3 collective-permute-start.10
  73.8 0.7 collective-permute-start.11
  74.4 3.6 %collective-permute-done.8 = bf16[64,2048]{1,0:T(8,128)(2,1)S(1)} collective-permute-done((bf16[64,2048]{1,0:T(8,128)(2,1)S(1)}, bf16[64,2048]{1,0:T(8,128)(2,1)S(1)}, u32[]{:S(2)}, u32[]{:S(2)}) %collective-permute-start.8) | collective-permute-done | bytes 262176 | tf_op jit(solution)/shard_map/ppermute | solution.py:418
  78.0 1.3 collective-permute-start.12
  80.4 0.7 collective-permute-start.13
  81.6 2.1 %collective-permute-done.10 = bf16[64,2048]{1,0:T(8,128)(2,1)S(1)} collective-permute-done((bf16[64,2048]{1,0:T(8,128)(2,1)S(1)}, bf16[64,2048]{1,0:T(8,128)(2,1)S(1)}, u32[]{:S(2)}, u32[]{:S(2)}) %collective-permute-start.10) | collective-permute-done | bytes 262176 | tf_op jit(solution)/shard_map/ppermute | solution.py:418
  83.6 1.3 collective-permute-start.14
  85.0 4.5 %collective-permute-done.13 = bf16[64,2048]{1,0:T(8,128)(2,1)S(1)} collective-permute-done((bf16[64,2048]{1,0:T(8,128)(2,1)S(1)}, bf16[64,2048]{1,0:T(8,128)(2,1)S(1)}, u32[]{:S(2)}, u32[]{:S(2)}) %collective-permute-start.13) | collective-permute-done | bytes 262176 | tf_op jit(solution)/shard_map/ppermute | solution.py:421
  91.2 1.8 %collective-permute-done.14 = bf16[64,2048]{1,0:T(8,128)(2,1)S(1)} collective-permute-done((bf16[64,2048]{1,0:T(8,128)(2,1)S(1)}, bf16[64,2048]{1,0:T(8,128)(2,1)S(1)}, u32[]{:S(2)}, u32[]{:S(2)}) %collective-permute-start.14) | collective-permute-done | bytes 262176 | tf_op jit(solution)/shard_map/ppermute | solution.py:418
  93.4 3.2 %collective-permute-done.15 = bf16[64,2048]{1,0:T(8,128)(2,1)S(1)} collective-permute-done((bf16[64,2048]{1,0:T(8,128)(2,1)S(1)}, bf16[64,2048]{1,0:T(8,128)(2,1)S(1)}, u32[]{:S(2)}, u32[]{:S(2)}) %collective-permute-start.15) | collective-permute-done | bytes 262176 | tf_op jit(solution)/shard_map/ppermute | solution.py:421
  97.1 1.7 collective-permute-done.16.other_ref
  98.8 1.5 dispatch.1
  100.3 3.6 %collective-permute-start.20 = (bf16[144,384]{1,0:T(8,128)(2,1)S(1)}, bf16[144,384]{1,0:T(8,128)(2,1)S(1)}, u32[]{:S(2)}, u32[]{:S(2)}) collective-permute-start(bf16[144,384]{1,0:T(8,128)(2,1)S(1)} %get-tuple-element.26), channel_id=1, source_target_pairs={{0,14},{2,12},{4,10},{6,8},{8,6},{10,4},{12,2},{14,0},{1,15},{3,13... | collective-permute-start | bytes 331784 | tf_op jit(solution)/shard_map/ppermute | solution.py:387
  103.9 2.0 %collective-permute-start.18 = (bf16[144,384]{1,0:T(8,128)(2,1)S(1)}, bf16[144,384]{1,0:T(8,128)(2,1)S(1)}, u32[]{:S(2)}, u32[]{:S(2)}) collective-permute-start(bf16[144,384]{1,0:T(8,128)(2,1)S(1)} %get-tuple-element.24), channel_id=1, source_target_pairs={{0,10},{2,8},{4,14},{6,12},{8,2},{10,0},{12,6},{14,4},{1,11},{3,9}... | collective-permute-start | bytes 331784 | tf_op jit(solution)/shard_map/ppermute | solution.py:387
  105.9 2.1 %collective-permute-start.17 = (bf16[144,384]{1,0:T(8,128)(2,1)S(1)}, bf16[144,384]{1,0:T(8,128)(2,1)S(1)}, u32[]{:S(2)}, u32[]{:S(2)}) collective-permute-start(bf16[144,384]{1,0:T(8,128)(2,1)S(1)} %get-tuple-element.23), channel_id=1, source_target_pairs={{0,8},{2,10},{4,12},{6,14},{8,0},{10,2},{12,4},{14,6},{1,9},{3,11}... | collective-permute-start | bytes 331784 | tf_op jit(solution)/shard_map/ppermute | solution.py:387
  108.0 1.2 collective-permute-start.24
  109.2 9.4 %collective-permute-start.23 = (bf16[144,384]{1,0:T(8,128)(2,1)S(1)}, bf16[144,384]{1,0:T(8,128)(2,1)S(1)}, u32[]{:S(2)}, u32[]{:S(2)}) collective-permute-start(bf16[144,384]{1,0:T(8,128)(2,1)S(1)} %get-tuple-element.29), channel_id=1, source_target_pairs={{0,4},{2,6},{4,0},{6,2},{8,12},{10,14},{12,8},{14,10},{1,5},{3,7},... | collective-permute-start | bytes 331784 | tf_op jit(solution)/shard_map/ppermute | solution.py:387
  118.7 3.9 %collective-permute-done.18 = bf16[144,384]{1,0:T(8,128)(2,1)S(1)} collective-permute-done((bf16[144,384]{1,0:T(8,128)(2,1)S(1)}, bf16[144,384]{1,0:T(8,128)(2,1)S(1)}, u32[]{:S(2)}, u32[]{:S(2)}) %collective-permute-start.18) | collective-permute-done | bytes 110624 | tf_op jit(solution)/shard_map/ppermute | solution.py:387
  122.6 0.4 collective-permute-done.17
  123.2 1.6 collective-permute-done.23
  125.1 1.7 collective-permute-done.25.near_other.d
  126.8 23.0 %experts.1 = (bf16[288,1536]{1,0:T(8,128)(2,1)S(1)}, bf16[288,1536]{1,0:T(8,128)(2,1)}) custom-call(s32[9]{0:T(128)S(1)} %pad_add_fusion.info_ref, bf16[4,144,384]{2,1,0:T(8,128)(2,1)S(1)} %pad_maximum_fusion.far_own.a, bf16[4,144,384]{2,1,0:T(8,128)(2,1)S(1)} %collective-permute-done.21.far_other.b, bf16[4,144,384]{2,1,0:T(8,128)(2,1)S(1)} %pad_maximum_fusion.1.near_own.c, ...), custom_call_target="tpu_custom_call" | custom-call | flops 12230590464 | bytes 42467328 | tf_op jit(solution)/shard_map/experts/pallas_call | solution.py:345
  150.0 2.5 %collective-permute-done.26.theirs_ref = bf16[288,1536]{1,0:T(8,128)(2,1)S(1)} collective-permute-done((bf16[288,1536]{1,0:T(8,128)(2,1)}, bf16[288,1536]{1,0:T(8,128)(2,1)S(1)}, u32[]{:S(2)}, u32[]{:S(2)}) %collective-permute-start.26) | collective-permute-done | bytes 884768 | tf_op jit(solution)/shard_map/ppermute | solution.py:24
  152.5 1.8 %weigh.1 = (bf16[144,384]{1,0:T(8,128)(2,1)S(1)}, bf16[144,384]{1,0:T(8,128)(2,1)S(1)}, bf16[144,384]{1,0:T(8,128)(2,1)S(1)}, bf16[144,384]{1,0:T(8,128)(2,1)S(1...) custom-call(s32[6]{0:T(128)S(1)} %stack.51.flags_ref, ...), custom_call_target="tpu_custom_call" | custom-call | tf_op jit(solution)/shard_map/weigh/pallas_call | solution.py:375
  154.4 0.9 collective-permute-start.27
  155.2 2.2 %collective-permute-start.28 = (bf16[144,384]{1,0:T(8,128)(2,1)S(1)}, bf16[144,384]{1,0:T(8,128)(2,1)S(1)}, u32[]{:S(2)}, u32[]{:S(2)}) collective-permute-start(bf16[144,384]{1,0:T(8,128)(2,1)S(1)} %get-tuple-element.34), channel_id=1, source_target_pairs={{0,10},{2,8},{4,14},{6,12},{8,2},{10,0},{12,6},{14,4},{1,11},{3,9}... | collective-permute-start | bytes 331784 | tf_op jit(solution)/shard_map/ppermute | solution.py:387
  157.4 2.8 %collective-permute-start.29 = (bf16[144,384]{1,0:T(8,128)(2,1)S(1)}, bf16[144,384]{1,0:T(8,128)(2,1)S(1)}, u32[]{:S(2)}, u32[]{:S(2)}) collective-permute-start(bf16[144,384]{1,0:T(8,128)(2,1)S(1)} %get-tuple-element.35), channel_id=1, source_target_pairs={{0,12},{2,14},{4,8},{6,10},{8,4},{10,6},{12,0},{14,2},{1,13},{3,15... | collective-permute-start | bytes 331784 | tf_op jit(solution)/shard_map/ppermute | solution.py:387
  160.2 1.9 %collective-permute-start.30 = (bf16[144,384]{1,0:T(8,128)(2,1)S(1)}, bf16[144,384]{1,0:T(8,128)(2,1)S(1)}, u32[]{:S(2)}, u32[]{:S(2)}) collective-permute-start(bf16[144,384]{1,0:T(8,128)(2,1)S(1)} %get-tuple-element.36), channel_id=1, source_target_pairs={{0,14},{2,12},{4,10},{6,8},{8,6},{10,4},{12,2},{14,0},{1,15},{3,13... | collective-permute-start | bytes 331784 | tf_op jit(solution)/shard_map/ppermute | solution.py:387
  162.1 0.6 collective-permute-start.31
  162.7 6.8 %collective-permute-done.27.refs_0_ = bf16[144,384]{1,0:T(8,128)(2,1)S(1)} collective-permute-done((bf16[144,384]{1,0:T(8,128)(2,1)S(1)}, bf16[144,384]{1,0:T(8,128)(2,1)S(1)}, u32[]{:S(2)}, u32[]{:S(2)}) %collective-permute-start.27) | collective-permute-done | bytes 110624 | tf_op jit(solution)/shard_map/ppermute | solution.py:387
  169.4 3.1 %collective-permute-done.28.refs_1_ = bf16[144,384]{1,0:T(8,128)(2,1)S(1)} collective-permute-done((bf16[144,384]{1,0:T(8,128)(2,1)S(1)}, bf16[144,384]{1,0:T(8,128)(2,1)S(1)}, u32[]{:S(2)}, u32[]{:S(2)}) %collective-permute-start.28) | collective-permute-done | bytes 110624 | tf_op jit(solution)/shard_map/ppermute | solution.py:387
  172.6 1.7 collective-permute-done.32.refs_6_
  174.3 3.9 %collective-permute-done.33.refs_7_ = bf16[144,384]{1,0:T(8,128)(2,1)S(1)} collective-permute-done((bf16[144,384]{1,0:T(8,128)(2,1)S(1)}, bf16[144,384]{1,0:T(8,128)(2,1)S(1)}, u32[]{:S(2)}, u32[]{:S(2)}) %collective-permute-start.33) | collective-permute-done | bytes 110624 | tf_op jit(solution)/shard_map/ppermute | solution.py:387
  178.2 2.3 %combine.1 = bf16[128,1536]{1,0:T(8,128)(2,1)} custom-call(s32[6]{0:T(128)S(1)} %stack.51.flags_ref, s32[2,128]{1,0:T(2,128)S(1)} %bitcast.113, bf16[144,384]{1,0:T(8,128)(2,1)S(1)} %collective-permute-done.27.refs_0_, bf16[144,384]{1,0:T(8,128)(2,1)S(1)} %collective-permute-done.28.refs_1_, bf16[144,384]{1,0:T(8,128)(2,1)S(1)} %collective-permute-done.29.refs_2_, ...), custom_call_target="tpu_custom_call" | custom-call | tf_op jit(solution)/shard_map/combine/pallas_call | solution.py:375
  (73 shorter events, 5.8 us)
Async XLA Ops:
  0.0 56.1 %copy-start = (bf16[2048,384]{1,0:T(8,128)(2,1)S(1)}, bf16[2048,384]{1,0:T(8,128)(2,1)}, u32[]{:S(2)}) copy-start(bf16[2048,384]{1,0:T(8,128)(2,1)} %param.17) | copy-start | bytes 4718596
  0.0 1.2 copy-start.1
  1.2 1.0 copy-start.3
  2.2 0.7 copy-start.11
  2.9 0.7 copy-start.13
  3.6 7.2 %copy-start.15 = (bf16[128,1536]{1,0:T(8,128)(2,1)S(1)}, bf16[128,1536]{1,0:T(8,128)(2,1)}, u32[]{:S(2)}) copy-start(bf16[128,1536]{1,0:T(8,128)(2,1)} %param.15) | copy-start | bytes 1179652
  5.5 17.7 %all-to-all-start = ((bf16[4,528,128]{2,1,0:T(8,128)(2,1)}), bf16[4,528,128]{2,1,0:T(8,128)(2,1)S(1)}, u32[]{:S(2)}, u32[]{:S(2)}) async-start(bf16[4,528,128]{2,1,0:T(8,128)(2,1)} %states.1), calls=%async_computation | async-start | bytes 1081344 | tf_op jit(solution)/shard_map/all_to_all | solution.py:458
  10.8 12.6 %collective-permute-start.1 = (bf16[128,1536]{1,0:T(8,128)(2,1)S(1)}, bf16[128,1536]{1,0:T(8,128)(2,1)S(1)}, u32[]{:S(2)}, u32[]{:S(2)}) collective-permute-start(bf16[128,1536]{1,0:T(8,128)(2,1)S(1)} %copy-done.15), channel_id=1, source_target_pairs={{1,8},{3,10},{5,12},{7,14},{8,1},{10,3},{12,5},{14,7},{17,24},{19,... | collective-permute-start | bytes 1179656 | tf_op jit(solution)/shard_map/ppermute | solution.py:450
  23.2 8.0 %copy-start.7 = (bf16[544,128]{1,0:T(8,128)(2,1)}, bf16[544,128]{1,0:T(8,128)(2,1)S(1)}, u32[]{:S(2)}) copy-start(bf16[544,128]{1,0:T(8,128)(2,1)S(1)} %totals.1.notes_ref) | copy-start | bytes 417796
  23.2 8.0 %collective-permute-start = (bf16[544,128]{1,0:T(8,128)(2,1)S(1)}, bf16[544,128]{1,0:T(8,128)(2,1)S(1)}, u32[]{:S(2)}, u32[]{:S(2)}) collective-permute-start(bf16[544,128]{1,0:T(8,128)(2,1)S(1)} %totals.1.notes_ref), channel_id=1, source_target_pairs={{0,8},{2,10},{4,12},{6,14},{8,0},{10,2},{12,4},{14,6},{1,9},{3,11}... | collective-permute-start | bytes 417800 | tf_op jit(solution)/shard_map/ppermute | solution.py:462
  32.9 0.7 copy-start.5
  33.5 16.3 %copy-start.2 = (bf16[128,2048]{1,0:T(8,128)(2,1)S(1)}, bf16[128,2048]{1,0:T(8,128)(2,1)}, u32[]{:S(2)}) copy-start(bf16[128,2048]{1,0:T(8,128)(2,1)} %k_ref.1) | copy-start | bytes 1572868
  33.5 16.3 %copy-start.4 = (bf16[128,2048]{1,0:T(8,128)(2,1)S(1)}, bf16[128,2048]{1,0:T(8,128)(2,1)}, u32[]{:S(2)}) copy-start(bf16[128,2048]{1,0:T(8,128)(2,1)} %v_ref.1) | copy-start | bytes 1572868
  33.5 16.3 %copy-start.10 = (f32[2048]{0:T(1024)S(1)}, f32[2048]{0:T(1024)}, u32[]{:S(2)}) copy-start(f32[2048]{0:T(1024)} %param.16) | copy-start | bytes 24580
  33.5 16.3 %all-to-all-start.1 = ((bf16[4,896,128]{2,1,0:T(8,128)(2,1)}), bf16[4,896,128]{2,1,0:T(8,128)(2,1)S(1)}, u32[]{:S(2)}, u32[]{:S(2)}) async-start(bf16[4,896,128]{2,1,0:T(8,128)(2,1)} %sums.1), calls=%async_computation.1 | async-start | bytes 1835008 | tf_op jit(solution)/shard_map/all_to_all | solution.py:471
  49.8 1.0 copy-start.9
  51.9 9.3 %collective-permute-start.2 = (bf16[64,2048]{1,0:T(8,128)(2,1)S(1)}, bf16[64,2048]{1,0:T(8,128)(2,1)S(1)}, u32[]{:S(2)}, u32[]{:S(2)}) collective-permute-start(bf16[64,2048]{1,0:T(8,128)(2,1)S(1)} %get-tuple-element.42), channel_id=1, source_target_pairs={{0,4},{4,8},{8,12},{12,14},{14,10},{10,6},{6,2},{2,0},{1,5},{5,9},... | collective-permute-start | bytes 786440 | tf_op jit(solution)/shard_map/ppermute | solution.py:418
  53.3 9.2 %collective-permute-start.3 = (bf16[64,2048]{1,0:T(8,128)(2,1)S(1)}, bf16[64,2048]{1,0:T(8,128)(2,1)S(1)}, u32[]{:S(2)}, u32[]{:S(2)}) collective-permute-start(bf16[64,2048]{1,0:T(8,128)(2,1)S(1)} %get-tuple-element.42), channel_id=1, source_target_pairs={{4,0},{8,4},{12,8},{14,12},{10,14},{6,10},{2,6},{0,2},{5,1},{9,5},... | collective-permute-start | bytes 786440 | tf_op jit(solution)/shard_map/ppermute | solution.py:421
  54.0 12.8 %collective-permute-start.4 = (bf16[64,2048]{1,0:T(8,128)(2,1)S(1)}, bf16[64,2048]{1,0:T(8,128)(2,1)S(1)}, u32[]{:S(2)}, u32[]{:S(2)}) collective-permute-start(bf16[64,2048]{1,0:T(8,128)(2,1)S(1)} %get-tuple-element.41), channel_id=1, source_target_pairs={{0,4},{4,8},{8,12},{12,14},{14,10},{10,6},{6,2},{2,0},{1,5},{5,9},... | collective-permute-start | bytes 786440 | tf_op jit(solution)/shard_map/ppermute | solution.py:418
  55.4 13.9 %collective-permute-start.5 = (bf16[64,2048]{1,0:T(8,128)(2,1)S(1)}, bf16[64,2048]{1,0:T(8,128)(2,1)S(1)}, u32[]{:S(2)}, u32[]{:S(2)}) collective-permute-start(bf16[64,2048]{1,0:T(8,128)(2,1)S(1)} %get-tuple-element.41), channel_id=1, source_target_pairs={{4,0},{8,4},{12,8},{14,12},{10,14},{6,10},{2,6},{0,2},{5,1},{9,5},... | collective-permute-start | bytes 786440 | tf_op jit(solution)/shard_map/ppermute | solution.py:421
  61.2 11.2 %collective-permute-start.6 = (bf16[64,2048]{1,0:T(8,128)(2,1)S(1)}, bf16[64,2048]{1,0:T(8,128)(2,1)S(1)}, u32[]{:S(2)}, u32[]{:S(2)}) collective-permute-start(bf16[64,2048]{1,0:T(8,128)(2,1)S(1)} %collective-permute-done.2), channel_id=1, source_target_pairs={{0,4},{4,8},{8,12},{12,14},{14,10},{10,6},{6,2},{2,0},{1,5},{5,9},... | collective-permute-start | bytes 786440 | tf_op jit(solution)/shard_map/ppermute | solution.py:418
  62.5 11.2 %collective-permute-start.7 = (bf16[64,2048]{1,0:T(8,128)(2,1)S(1)}, bf16[64,2048]{1,0:T(8,128)(2,1)S(1)}, u32[]{:S(2)}, u32[]{:S(2)}) collective-permute-start(bf16[64,2048]{1,0:T(8,128)(2,1)S(1)} %collective-permute-done.3), channel_id=1, source_target_pairs={{4,0},{8,4},{12,8},{14,12},{10,14},{6,10},{2,6},{0,2},{5,1},{9,5},... | collective-permute-start | bytes 786440 | tf_op jit(solution)/shard_map/ppermute | solution.py:421
  66.8 11.2 %collective-permute-start.8 = (bf16[64,2048]{1,0:T(8,128)(2,1)S(1)}, bf16[64,2048]{1,0:T(8,128)(2,1)S(1)}, u32[]{:S(2)}, u32[]{:S(2)}) collective-permute-start(bf16[64,2048]{1,0:T(8,128)(2,1)S(1)} %collective-permute-done.4), channel_id=1, source_target_pairs={{0,4},{4,8},{8,12},{12,14},{14,10},{10,6},{6,2},{2,0},{1,5},{5,9},... | collective-permute-start | bytes 786440 | tf_op jit(solution)/shard_map/ppermute | solution.py:418
  69.2 11.2 %collective-permute-start.9 = (bf16[64,2048]{1,0:T(8,128)(2,1)S(1)}, bf16[64,2048]{1,0:T(8,128)(2,1)S(1)}, u32[]{:S(2)}, u32[]{:S(2)}) collective-permute-start(bf16[64,2048]{1,0:T(8,128)(2,1)S(1)} %collective-permute-done.5), channel_id=1, source_target_pairs={{4,0},{8,4},{12,8},{14,12},{10,14},{6,10},{2,6},{0,2},{5,1},{9,5},... | collective-permute-start | bytes 786440 | tf_op jit(solution)/shard_map/ppermute | solution.py:421
  72.4 11.2 %collective-permute-start.10 = (bf16[64,2048]{1,0:T(8,128)(2,1)S(1)}, bf16[64,2048]{1,0:T(8,128)(2,1)S(1)}, u32[]{:S(2)}, u32[]{:S(2)}) collective-permute-start(bf16[64,2048]{1,0:T(8,128)(2,1)S(1)} %collective-permute-done.6), channel_id=1, source_target_pairs={{0,4},{4,8},{8,12},{12,14},{14,10},{10,6},{6,2},{2,0},{1,5},{5,9},... | collective-permute-start | bytes 786440 | tf_op jit(solution)/shard_map/ppermute | solution.py:418
  73.8 16.2 %collective-permute-start.11 = (bf16[64,2048]{1,0:T(8,128)(2,1)S(1)}, bf16[64,2048]{1,0:T(8,128)(2,1)S(1)}, u32[]{:S(2)}, u32[]{:S(2)}) collective-permute-start(bf16[64,2048]{1,0:T(8,128)(2,1)S(1)} %collective-permute-done.7), channel_id=1, source_target_pairs={{4,0},{8,4},{12,8},{14,12},{10,14},{6,10},{2,6},{0,2},{5,1},{9,5},... | collective-permute-start | bytes 786440 | tf_op jit(solution)/shard_map/ppermute | solution.py:421
  78.0 12.4 %collective-permute-start.12 = (bf16[64,2048]{1,0:T(8,128)(2,1)S(1)}, bf16[64,2048]{1,0:T(8,128)(2,1)S(1)}, u32[]{:S(2)}, u32[]{:S(2)}) collective-permute-start(bf16[64,2048]{1,0:T(8,128)(2,1)S(1)} %collective-permute-done.8), channel_id=1, source_target_pairs={{0,4},{4,8},{8,12},{12,14},{14,10},{10,6},{6,2},{2,0},{1,5},{5,9},... | collective-permute-start | bytes 786440 | tf_op jit(solution)/shard_map/ppermute | solution.py:418
  80.4 9.0 %collective-permute-start.13 = (bf16[64,2048]{1,0:T(8,128)(2,1)S(1)}, bf16[64,2048]{1,0:T(8,128)(2,1)S(1)}, u32[]{:S(2)}, u32[]{:S(2)}) collective-permute-start(bf16[64,2048]{1,0:T(8,128)(2,1)S(1)} %collective-permute-done.9), channel_id=1, source_target_pairs={{4,0},{8,4},{12,8},{14,12},{10,14},{6,10},{2,6},{0,2},{5,1},{9,5},... | collective-permute-start | bytes 786440 | tf_op jit(solution)/shard_map/ppermute | solution.py:421
  83.6 9.4 %collective-permute-start.14 = (bf16[64,2048]{1,0:T(8,128)(2,1)S(1)}, bf16[64,2048]{1,0:T(8,128)(2,1)S(1)}, u32[]{:S(2)}, u32[]{:S(2)}) collective-permute-start(bf16[64,2048]{1,0:T(8,128)(2,1)S(1)} %collective-permute-done.10), channel_id=1, source_target_pairs={{0,4},{4,8},{8,12},{12,14},{14,10},{10,6},{6,2},{2,0},{1,5},{5,9},... | collective-permute-start | bytes 786440 | tf_op jit(solution)/shard_map/ppermute | solution.py:418
  89.4 7.2 %collective-permute-start.15 = (bf16[64,2048]{1,0:T(8,128)(2,1)S(1)}, bf16[64,2048]{1,0:T(8,128)(2,1)S(1)}, u32[]{:S(2)}, u32[]{:S(2)}) collective-permute-start(bf16[64,2048]{1,0:T(8,128)(2,1)S(1)} %collective-permute-done.13), channel_id=1, source_target_pairs={{4,0},{8,4},{12,8},{14,12},{10,14},{6,10},{2,6},{0,2},{5,1},{9,5},... | collective-permute-start | bytes 786440 | tf_op jit(solution)/shard_map/ppermute | solution.py:421
  93.4 5.5 %copy-start.6 = (bf16[544,128]{1,0:T(8,128)(2,1)S(1)}, bf16[544,128]{1,0:T(8,128)(2,1)}, u32[]{:S(2)}) copy-start(bf16[544,128]{1,0:T(8,128)(2,1)} %copy-done.5) | copy-start | bytes 417796
  93.4 5.5 %copy-start.8 = (bf16[544,128]{1,0:T(8,128)(2,1)S(1)}, bf16[544,128]{1,0:T(8,128)(2,1)}, u32[]{:S(2)}) copy-start(bf16[544,128]{1,0:T(8,128)(2,1)} %copy-done.7) | copy-start | bytes 417796
  97.0 1.8 collective-permute-start.16
  100.3 26.5 %copy-start.14 = (f32[3072]{0:T(1024)S(1)}, f32[3072]{0:T(1024)}, u32[]{:S(2)}) copy-start(f32[3072]{0:T(1024)} %param.18) | copy-start | bytes 36868
  100.3 8.9 %collective-permute-start.20 = (bf16[144,384]{1,0:T(8,128)(2,1)S(1)}, bf16[144,384]{1,0:T(8,128)(2,1)S(1)}, u32[]{:S(2)}, u32[]{:S(2)}) collective-permute-start(bf16[144,384]{1,0:T(8,128)(2,1)S(1)} %get-tuple-element.26), channel_id=1, source_target_pairs={{0,14},{2,12},{4,10},{6,8},{8,6},{10,4},{12,2},{14,0},{1,15},{3,13... | collective-permute-start | bytes 331784 | tf_op jit(solution)/shard_map/ppermute | solution.py:387
  103.9 14.7 %collective-permute-start.19 = (bf16[144,384]{1,0:T(8,128)(2,1)S(1)}, bf16[144,384]{1,0:T(8,128)(2,1)S(1)}, u32[]{:S(2)}, u32[]{:S(2)}) collective-permute-start(bf16[144,384]{1,0:T(8,128)(2,1)S(1)} %get-tuple-element.25), channel_id=1, source_target_pairs={{0,12},{2,14},{4,8},{6,10},{8,4},{10,6},{12,0},{14,2},{1,13},{3,15... | collective-permute-start | bytes 331784 | tf_op jit(solution)/shard_map/ppermute | solution.py:387
  103.9 18.6 %collective-permute-start.18 = (bf16[144,384]{1,0:T(8,128)(2,1)S(1)}, bf16[144,384]{1,0:T(8,128)(2,1)S(1)}, u32[]{:S(2)}, u32[]{:S(2)}) collective-permute-start(bf16[144,384]{1,0:T(8,128)(2,1)S(1)} %get-tuple-element.24), channel_id=1, source_target_pairs={{0,10},{2,8},{4,14},{6,12},{8,2},{10,0},{12,6},{14,4},{1,11},{3,9}... | collective-permute-start | bytes 331784 | tf_op jit(solution)/shard_map/ppermute | solution.py:387
  105.9 17.1 %collective-permute-start.17 = (bf16[144,384]{1,0:T(8,128)(2,1)S(1)}, bf16[144,384]{1,0:T(8,128)(2,1)S(1)}, u32[]{:S(2)}, u32[]{:S(2)}) collective-permute-start(bf16[144,384]{1,0:T(8,128)(2,1)S(1)} %get-tuple-element.23), channel_id=1, source_target_pairs={{0,8},{2,10},{4,12},{6,14},{8,0},{10,2},{12,4},{14,6},{1,9},{3,11}... | collective-permute-start | bytes 331784 | tf_op jit(solution)/shard_map/ppermute | solution.py:387
  108.0 15.1 %collective-permute-start.24 = (bf16[144,384]{1,0:T(8,128)(2,1)S(1)}, bf16[144,384]{1,0:T(8,128)(2,1)S(1)}, u32[]{:S(2)}, u32[]{:S(2)}) collective-permute-start(bf16[144,384]{1,0:T(8,128)(2,1)S(1)} %get-tuple-element.30), channel_id=1, source_target_pairs={{0,6},{2,4},{4,2},{6,0},{8,14},{10,12},{12,10},{14,8},{1,7},{3,5},... | collective-permute-start | bytes 331784 | tf_op jit(solution)/shard_map/ppermute | solution.py:387
  109.2 15.6 %collective-permute-start.23 = (bf16[144,384]{1,0:T(8,128)(2,1)S(1)}, bf16[144,384]{1,0:T(8,128)(2,1)S(1)}, u32[]{:S(2)}, u32[]{:S(2)}) collective-permute-start(bf16[144,384]{1,0:T(8,128)(2,1)S(1)} %get-tuple-element.29), channel_id=1, source_target_pairs={{0,4},{2,6},{4,0},{6,2},{8,12},{10,14},{12,8},{14,10},{1,5},{3,7},... | collective-permute-start | bytes 331784 | tf_op jit(solution)/shard_map/ppermute | solution.py:387
  118.7 6.2 %collective-permute-start.22 = (bf16[144,384]{1,0:T(8,128)(2,1)S(1)}, bf16[144,384]{1,0:T(8,128)(2,1)S(1)}, u32[]{:S(2)}, u32[]{:S(2)}) collective-permute-start(bf16[144,384]{1,0:T(8,128)(2,1)S(1)} %get-tuple-element.28), channel_id=1, source_target_pairs={{0,2},{2,0},{4,6},{6,4},{8,10},{10,8},{12,14},{14,12},{1,3},{3,1},... | collective-permute-start | bytes 331784 | tf_op jit(solution)/shard_map/ppermute | solution.py:387
  123.1 2.0 %collective-permute-start.21 = (bf16[4,144,384]{2,1,0:T(8,128)(2,1)S(1)}, bf16[4,144,384]{2,1,0:T(8,128)(2,1)S(1)}, u32[]{:S(2)}, u32[]{:S(2)}) collective-permute-start(bf16[4,144,384]{2,1,0:T(8,128)(2,1)S(1)} %pad_maximum_fusion.far_own.a), channel_id=1, source_target_pairs={{0,1},{1,0},{2,3},{3,2},{4,5},{5,4},{6,7},{7,6},{8,9},{9,8},{10,11... | collective-permute-start | bytes 1327112 | tf_op jit(solution)/shard_map/ppermute | solution.py:24
  124.9 1.9 %collective-permute-start.25 = (bf16[4,144,384]{2,1,0:T(8,128)(2,1)S(1)}, bf16[4,144,384]{2,1,0:T(8,128)(2,1)S(1)}, u32[]{:S(2)}, u32[]{:S(2)}) collective-permute-start(bf16[4,144,384]{2,1,0:T(8,128)(2,1)S(1)} %pad_maximum_fusion.1.near_own.c), channel_id=1, source_target_pairs={{0,1},{1,0},{2,3},{3,2},{4,5},{5,4},{6,7},{7,6},{8,9},{9,8},{10,11... | collective-permute-start | bytes 1327112 | tf_op jit(solution)/shard_map/ppermute | solution.py:24
  149.8 2.7 %collective-permute-start.26 = (bf16[288,1536]{1,0:T(8,128)(2,1)}, bf16[288,1536]{1,0:T(8,128)(2,1)S(1)}, u32[]{:S(2)}, u32[]{:S(2)}) collective-permute-start(bf16[288,1536]{1,0:T(8,128)(2,1)} %get-tuple-element.32), channel_id=1, source_target_pairs={{0,1},{1,0},{2,3},{3,2},{4,5},{5,4},{6,7},{7,6},{8,9},{9,8},{10,11... | collective-permute-start | bytes 2654216 | tf_op jit(solution)/shard_map/ppermute | solution.py:24
  152.5 25.7 %copy-start.12 = (s32[128,2]{0,1:T(2,128)S(1)}, s32[128,2]{0,1:T(2,128)}, u32[]{:S(2)}) copy-start(s32[128,2]{0,1:T(2,128)} %param.19) | copy-start | bytes 3076
  154.4 15.1 %collective-permute-start.27 = (bf16[144,384]{1,0:T(8,128)(2,1)S(1)}, bf16[144,384]{1,0:T(8,128)(2,1)S(1)}, u32[]{:S(2)}, u32[]{:S(2)}) collective-permute-start(bf16[144,384]{1,0:T(8,128)(2,1)S(1)} %get-tuple-element.33), channel_id=1, source_target_pairs={{0,8},{2,10},{4,12},{6,14},{8,0},{10,2},{12,4},{14,6},{1,9},{3,11}... | collective-permute-start | bytes 331784 | tf_op jit(solution)/shard_map/ppermute | solution.py:387
  155.2 17.3 %collective-permute-start.28 = (bf16[144,384]{1,0:T(8,128)(2,1)S(1)}, bf16[144,384]{1,0:T(8,128)(2,1)S(1)}, u32[]{:S(2)}, u32[]{:S(2)}) collective-permute-start(bf16[144,384]{1,0:T(8,128)(2,1)S(1)} %get-tuple-element.34), channel_id=1, source_target_pairs={{0,10},{2,8},{4,14},{6,12},{8,2},{10,0},{12,6},{14,4},{1,11},{3,9}... | collective-permute-start | bytes 331784 | tf_op jit(solution)/shard_map/ppermute | solution.py:387
  157.4 15.2 %collective-permute-start.29 = (bf16[144,384]{1,0:T(8,128)(2,1)S(1)}, bf16[144,384]{1,0:T(8,128)(2,1)S(1)}, u32[]{:S(2)}, u32[]{:S(2)}) collective-permute-start(bf16[144,384]{1,0:T(8,128)(2,1)S(1)} %get-tuple-element.35), channel_id=1, source_target_pairs={{0,12},{2,14},{4,8},{6,10},{8,4},{10,6},{12,0},{14,2},{1,13},{3,15... | collective-permute-start | bytes 331784 | tf_op jit(solution)/shard_map/ppermute | solution.py:387
  160.2 12.4 %collective-permute-start.30 = (bf16[144,384]{1,0:T(8,128)(2,1)S(1)}, bf16[144,384]{1,0:T(8,128)(2,1)S(1)}, u32[]{:S(2)}, u32[]{:S(2)}) collective-permute-start(bf16[144,384]{1,0:T(8,128)(2,1)S(1)} %get-tuple-element.36), channel_id=1, source_target_pairs={{0,14},{2,12},{4,10},{6,8},{8,6},{10,4},{12,2},{14,0},{1,15},{3,13... | collective-permute-start | bytes 331784 | tf_op jit(solution)/shard_map/ppermute | solution.py:387
  162.1 10.5 %collective-permute-start.31 = (bf16[144,384]{1,0:T(8,128)(2,1)S(1)}, bf16[144,384]{1,0:T(8,128)(2,1)S(1)}, u32[]{:S(2)}, u32[]{:S(2)}) collective-permute-start(bf16[144,384]{1,0:T(8,128)(2,1)S(1)} %get-tuple-element.38), channel_id=1, source_target_pairs={{0,2},{2,0},{4,6},{6,4},{8,10},{10,8},{12,14},{14,12},{1,3},{3,1},... | collective-permute-start | bytes 331784 | tf_op jit(solution)/shard_map/ppermute | solution.py:387
  169.4 4.9 %collective-permute-start.32 = (bf16[144,384]{1,0:T(8,128)(2,1)S(1)}, bf16[144,384]{1,0:T(8,128)(2,1)S(1)}, u32[]{:S(2)}, u32[]{:S(2)}) collective-permute-start(bf16[144,384]{1,0:T(8,128)(2,1)S(1)} %get-tuple-element.39), channel_id=1, source_target_pairs={{0,4},{2,6},{4,0},{6,2},{8,12},{10,14},{12,8},{14,10},{1,5},{3,7},... | collective-permute-start | bytes 331784 | tf_op jit(solution)/shard_map/ppermute | solution.py:387
  172.6 5.6 %collective-permute-start.33 = (bf16[144,384]{1,0:T(8,128)(2,1)S(1)}, bf16[144,384]{1,0:T(8,128)(2,1)S(1)}, u32[]{:S(2)}, u32[]{:S(2)}) collective-permute-start(bf16[144,384]{1,0:T(8,128)(2,1)S(1)} %get-tuple-element.40), channel_id=1, source_target_pairs={{0,6},{2,4},{4,2},{6,0},{8,14},{10,12},{12,10},{14,8},{1,7},{3,5},... | collective-permute-start | bytes 331784 | tf_op jit(solution)/shard_map/ppermute | solution.py:387

commit v2 on v1

--- a/solution.py
+++ b/solution.py
@@ -239,12 +239,18 @@
         out_ref[:, m * width : (m + 1) * width] = contract(pick, back, (0, 0)).astype(BF)
 
 
+def load_kernel(source, out_ref, sem):
+    copy = pltpu.make_async_copy(source, out_ref, sem)
+    copy.start()
+    copy.wait()
+
+
 def moe_kernel(
-    info_ref, far_own, far_other, near_own, near_other, gain_ref, gate_hbm, up_hbm, down_hbm,
-    mine_ref, theirs_ref, x_ref, inner_ref, gate_ref, up_ref, down_ref, sems, down_sems,
+    info_ref, far_own, far_other, near_own, near_other, gain_ref, gate_ref, up_hbm, down_hbm,
+    mine_ref, theirs_ref, x_ref, inner_ref, up_ref, down_ref, sems, down_sems,
 ):
     pieces, rows, width = near_own.shape
-    tiles, parts, depth, tile = gate_ref.shape
+    tiles, parts, depth, tile = up_ref.shape
     outs, _, out_tile = down_ref.shape
     features = parts * depth
     core = info_ref[0]
@@ -253,11 +259,10 @@
     copies = {}
     for i in range(tiles):
         for k in range(parts):
-            for n, (source, buffer) in enumerate(((gate_hbm, gate_ref), (up_hbm, up_ref))):
-                piece = source.at[pl.ds(k * depth, depth), pl.ds(i * tile, tile)]
-                copy = pltpu.make_async_copy(piece, buffer.at[i, k], sems.at[n, i, k])
-                copy.start()
-                copies[n, i, k] = copy
+            piece = up_hbm.at[pl.ds(k * depth, depth), pl.ds(i * tile, tile)]
+            copy = pltpu.make_async_copy(piece, up_ref.at[i, k], sems.at[i, k])
+            copy.start()
+            copies[i, k] = copy
     downs = []
     for i in range(outs):
         side = 1 - core if i * out_tile < half else core
@@ -288,17 +293,14 @@
     place((far_other, near_other), pl.multiple_of((1 - core) * rows, rows))
 
     for i in range(tiles):
-        sums = [None, None]
+        at = slice(i * tile, (i + 1) * tile)
+        gate = dot(x_ref[...], gate_ref[:, at])
+        upward = None
         for k in range(parts):
-            x = x_ref[:, k * depth : (k + 1) * depth]
-            for n, weight_ref in ((0, gate_ref), (1, up_ref)):
-                copies[n, i, k].wait()
-                value = dot(x, weight_ref[i, k])
-                sums[n] = value if k == 0 else sums[n] + value
-        gate, upward = sums
-        inner_ref[:, i * tile : (i + 1) * tile] = (
-            gate / (1.0 + jnp.exp(-gate)) * upward
-        ).astype(BF)
+            copies[i, k].wait()
+            value = dot(x_ref[:, k * depth : (k + 1) * depth], up_ref[i, k])
+            upward = value if k == 0 else upward + value
+        inner_ref[:, at] = (gate / (1.0 + jnp.exp(-gate)) * upward).astype(BF)
     inner = inner_ref[...]
     for i, copy in enumerate(downs):
         copy.wait()
@@ -345,15 +347,15 @@
     return pl.pallas_call(
         moe_kernel,
         out_shape=(out, out),
-        in_specs=[smem] + [vmem] * 5 + [hbm] * 3,
+        in_specs=[smem] + [vmem] * 6 + [hbm] * 2,
         out_specs=(vmem, vmem),
         scratch_shapes=[
-            pltpu.VMEM((2 * rows, features), BF), pltpu.VMEM((2 * rows, hidden), BF), buffer, buffer,
+            pltpu.VMEM((2 * rows, features), BF), pltpu.VMEM((2 * rows, hidden), BF), buffer,
             pltpu.VMEM((features // out_tile, hidden, out_tile), BF),
-            pltpu.SemaphoreType.DMA((2, hidden // tile, parts)),
+            pltpu.SemaphoreType.DMA((hidden // tile, parts)),
             pltpu.SemaphoreType.DMA((features // out_tile,)),
         ],
-        compiler_params=pltpu.CompilerParams(vmem_limit_bytes=51 * MIB),
+        compiler_params=pltpu.CompilerParams(vmem_limit_bytes=35 * MIB),
         cost_estimate=pl.CostEstimate(
             flops=12 * rows * features * hidden,
             bytes_accessed=6 * features * hidden,
@@ -381,6 +383,19 @@
         compiler_params=pltpu.CompilerParams(vmem_limit_bytes=room * VMEM_BYTES),
         name=name,
     )(*operands)
+
+
+def load(weight, name):
+    return pl.pallas_call(
+        load_kernel,
+        out_shape=jax.ShapeDtypeStruct(weight.shape, weight.dtype),
+        in_specs=[pl.BlockSpec(memory_space=pltpu.HBM)],
+        out_specs=pl.BlockSpec(memory_space=pltpu.VMEM),
+        scratch_shapes=[pltpu.SemaphoreType.DMA],
+        compiler_params=pltpu.CompilerParams(vmem_limit_bytes=30 * MIB),
+        cost_estimate=pl.CostEstimate(flops=0, bytes_accessed=2 * weight.size, transcendentals=0),
+        name=name,
+    )(weight)
 
 
 def xor_shift(x, k):
@@ -487,6 +502,7 @@
     got = [None] * seq_count
     for k in list(range(half, seq_count)) + list(range(half)):
         got[k] = xor_shift(pieces[k], k) if k else pieces[0]
+    gate_here, got = lax.optimization_barrier((load(w_gate, "load_gate"), got))
     parts, places = [], []
     for first in (half, 0):
         turns = me ^ (first + jnp.arange(half))
@@ -500,7 +516,7 @@
     info = jnp.concatenate([core.reshape(1), *places]).astype(jnp.int32)
     mine, theirs = by_rows(
         functools.partial(experts, info), rows, parts,
-        (moe_gain.reshape(1, 2 * half_width), w_gate, w_up, w_down),
+        (moe_gain.reshape(1, 2 * half_width), gate_here, w_up, w_down),
     )
     piece = half_width // FOLD
     out = on_chip(

time: 181 us -> 179 us (0.989)
  waiting for transfers between devices: 84.5 us -> 80.5 us
    pallas_call x0 -> x1, Pallas kernels: none -> 5.03 us  [load(): pl.pallas_call(load_kernel, out_shape=jax.ShapeDtypeStruct(weight.shape,...]
    pallas_call x1, Pallas kernels: 23 us -> 19.4 us  [experts(): pl.pallas_call(moe_kernel, out_shape=(out, out), in_specs=[smem] + [vmem]...]
    ppermute x7, waiting for transfers between devices: 7.76 us -> 4.36 us  [ring_project(): front[i] = lax.ppermute(front[i], 'seq', behind)]
    unnamed x32 -> x34, local copies, waits for them, and re-layouts: 5.29 us -> 5.31 us
  transfers between devices with their start and end apart: 36 -> 36, of which waited for: 21 -> 22; matrix products, arithmetic and copies ran while one was open for 3% -> 3% of each run, Pallas kernels for 0% -> 3%
where the time goes in v2:
time: 179 us
  waiting for transfers between devices  80.5 us (45%)
  starting transfers between devices  51.4 us (29%)
  Pallas kernels  34.7 us (19%)
  matrix products  5.79 us (3%)
  local copies, waits for them, and re-layouts  5.59 us (3%)
    ppermute x14, starting transfers between devices, xor_shift(): lax.ppermute(x, 'seq', [(s, s ^ k) for s in range(lax.axis_size('seq'))])  25.9 us
    ppermute x14, waiting for transfers between devices, xor_shift(): lax.ppermute(x, 'seq', [(s, s ^ k) for s in range(lax.axis_size('seq'))])  20.4 us
    pallas_call x1, Pallas kernels, experts(): pl.pallas_call(moe_kernel, out_shape=(out, out), in_specs=[smem] + [vmem]...  19.4 us
    ppermute x7, waiting for transfers between devices, ring_project(): back[i] = lax.ppermute(back[i], 'seq', ahead)  18.2 us
    all_to_all x1, waiting for transfers between devices, per_device(): lax.all_to_all(sums, 'seq', 0, 0, axis_index_groups=groups, tiled=True)  12.4 us
    all_to_all x1, waiting for transfers between devices, per_device(): lax.all_to_all(states, 'seq', 0, 0, axis_index_groups=groups, tiled=True)  11.6 us
    ppermute x7, starting transfers between devices, ring_project(): back[i] = lax.ppermute(back[i], 'seq', ahead)  10.5 us
    pallas_call x7, Pallas kernels, on_chip(): pl.pallas_call(kernel, out_shape=out_shape, in_specs=[smem] * scalars + [...  10.2 us
  transfers between devices with their start and end apart: 36, of which 22 were waited for; matrix products, arithmetic and copies ran while one was open for 3% of the time, Pallas kernels for 3%

profile of v2, /device:TPU:0, one launch (start us, length us, event | category | flops | bytes accessed | tf_op | source)
XLA Modules:
  0.0 178.8 jit_solution(1431364395372602423)
XLA Ops:
  0.0 1.2 copy-done.2
  1.2 1.0 copy-done.4
  2.2 0.7 copy-done.12
  2.9 0.7 copy-done.14
  3.6 1.9 %states.1 = bf16[4,528,128]{2,1,0:T(8,128)(2,1)} custom-call(s32[2,128]{1,0:T(2,128)S(1)} %bitcast.112, f32[2,128]{1,0:T(2,128)S(1)} %bitcast.114, bf16[128,2048]{1,0:T(8,128)(2,1)S(1)} %copy-done.2, bf16[128,2048]{1,0:T(8,128)(2,1)S(1)} %copy-done.4), custom_call_target="tpu_custom_call" | custom-call | tf_op jit(solution)/shard_map/states/pallas_call | solution.py:377
  5.5 5.3 %all-to-all-start = ((bf16[4,528,128]{2,1,0:T(8,128)(2,1)}), bf16[4,528,128]{2,1,0:T(8,128)(2,1)S(1)}, u32[]{:S(2)}, u32[]{:S(2)}) async-start(bf16[4,528,128]{2,1,0:T(8,128)(2,1)} %states.1), calls=%async_computation | async-start | bytes 1081344 | tf_op jit(solution)/shard_map/all_to_all | solution.py:473
  10.8 0.7 collective-permute-start.1
  11.6 11.6 %all-to-all-done.x_ref = bf16[4,528,128]{2,1,0:T(8,128)(2,1)S(1)} async-done(((bf16[4,528,128]{2,1,0:T(8,128)(2,1)}), bf16[4,528,128]{2,1,0:T(8,128)(2,1)S(1)}, u32[]{:S(2)}, u32[]{:S(2)}) %all-to-all-start) | async-done | bytes 540704 | tf_op jit(solution)/shard_map/all_to_all | solution.py:473
  23.4 7.8 %collective-permute-done.far_ref = bf16[544,128]{1,0:T(8,128)(2,1)S(1)} collective-permute-done((bf16[544,128]{1,0:T(8,128)(2,1)S(1)}, bf16[544,128]{1,0:T(8,128)(2,1)S(1)}, u32[]{:S(2)}, u32[]{:S(2)}) %collective-permute-start) | collective-permute-done | bytes 139296 | tf_op jit(solution)/shard_map/ppermute | solution.py:477
  31.2 1.6 sums.1
  32.9 0.7 copy-done.6
  33.5 3.6 %all-to-all-start.1 = ((bf16[4,896,128]{2,1,0:T(8,128)(2,1)}), bf16[4,896,128]{2,1,0:T(8,128)(2,1)S(1)}, u32[]{:S(2)}, u32[]{:S(2)}) async-start(bf16[4,896,128]{2,1,0:T(8,128)(2,1)} %sums.1), calls=%async_computation.1 | async-start | bytes 1835008 | tf_op jit(solution)/shard_map/all_to_all | solution.py:486
  37.4 12.4 %all-to-all-done.1.before_ref.resid_ref = bf16[4,896,128]{2,1,0:T(8,128)(2,1)S(1)} async-done(((bf16[4,896,128]{2,1,0:T(8,128)(2,1)}), bf16[4,896,128]{2,1,0:T(8,128)(2,1)S(1)}, u32[]{:S(2)}, u32[]{:S(2)}) %all-to-all-start.1) | async-done | bytes 917536 | tf_op jit(solution)/shard_map/all_to_all | solution.py:486
  49.8 1.0 copy-done.10
  50.9 1.0 attention.1
  51.9 1.5 collective-permute-start.4
  53.4 0.6 collective-permute-start.5
  54.0 1.4 collective-permute-start.2
  55.4 0.6 collective-permute-start.3
  56.9 4.3 %collective-permute-done.4 = bf16[64,2048]{1,0:T(8,128)(2,1)S(1)} collective-permute-done((bf16[64,2048]{1,0:T(8,128)(2,1)S(1)}, bf16[64,2048]{1,0:T(8,128)(2,1)S(1)}, u32[]{:S(2)}, u32[]{:S(2)}) %collective-permute-start.4) | collective-permute-done | bytes 262176 | tf_op jit(solution)/shard_map/ppermute | solution.py:433
  61.2 1.3 collective-permute-start.8
  62.6 0.7 collective-permute-start.9
  63.2 3.6 %collective-permute-done.2 = bf16[64,2048]{1,0:T(8,128)(2,1)S(1)} collective-permute-done((bf16[64,2048]{1,0:T(8,128)(2,1)S(1)}, bf16[64,2048]{1,0:T(8,128)(2,1)S(1)}, u32[]{:S(2)}, u32[]{:S(2)}) %collective-permute-start.2) | collective-permute-done | bytes 262176 | tf_op jit(solution)/shard_map/ppermute | solution.py:433
  66.8 1.3 collective-permute-start.6
  68.2 0.7 collective-permute-start.7
  70.3 2.1 %collective-permute-done.8 = bf16[64,2048]{1,0:T(8,128)(2,1)S(1)} collective-permute-done((bf16[64,2048]{1,0:T(8,128)(2,1)S(1)}, bf16[64,2048]{1,0:T(8,128)(2,1)S(1)}, u32[]{:S(2)}, u32[]{:S(2)}) %collective-permute-start.8) | collective-permute-done | bytes 262176 | tf_op jit(solution)/shard_map/ppermute | solution.py:433
  72.4 1.3 collective-permute-start.12
  73.8 0.7 collective-permute-start.13
  74.4 3.6 %collective-permute-done.6 = bf16[64,2048]{1,0:T(8,128)(2,1)S(1)} collective-permute-done((bf16[64,2048]{1,0:T(8,128)(2,1)S(1)}, bf16[64,2048]{1,0:T(8,128)(2,1)S(1)}, u32[]{:S(2)}, u32[]{:S(2)}) %collective-permute-start.6) | collective-permute-done | bytes 262176 | tf_op jit(solution)/shard_map/ppermute | solution.py:433
  78.0 1.3 collective-permute-start.10
  79.4 0.7 collective-permute-start.11
  81.5 3.5 %collective-permute-done.13 = bf16[64,2048]{1,0:T(8,128)(2,1)S(1)} collective-permute-done((bf16[64,2048]{1,0:T(8,128)(2,1)S(1)}, bf16[64,2048]{1,0:T(8,128)(2,1)S(1)}, u32[]{:S(2)}, u32[]{:S(2)}) %collective-permute-start.13) | collective-permute-done | bytes 262176 | tf_op jit(solution)/shard_map/ppermute | solution.py:436
  85.0 0.7 collective-permute-start.15
  85.7 1.7 collective-permute-done.10
  87.4 2.3 %collective-permute-start.14 = (bf16[64,2048]{1,0:T(8,128)(2,1)S(1)}, bf16[64,2048]{1,0:T(8,128)(2,1)S(1)}, u32[]{:S(2)}, u32[]{:S(2)}) collective-permute-start(bf16[64,2048]{1,0:T(8,128)(2,1)S(1)} %collective-permute-done.10), channel_id=1, source_target_pairs={{0,4},{4,8},{8,12},{12,14},{14,10},{10,6},{6,2},{2,0},{1,5},{5,9},... | collective-permute-start | bytes 786440 | tf_op jit(solution)/shard_map/ppermute | solution.py:433
  90.0 0.6 collective-permute-done.11
  91.0 0.4 fusion.3
  91.8 2.8 %collective-permute-done.14 = bf16[64,2048]{1,0:T(8,128)(2,1)S(1)} collective-permute-done((bf16[64,2048]{1,0:T(8,128)(2,1)S(1)}, bf16[64,2048]{1,0:T(8,128)(2,1)S(1)}, u32[]{:S(2)}, u32[]{:S(2)}) %collective-permute-start.14) | collective-permute-done | bytes 262176 | tf_op jit(solution)/shard_map/ppermute | solution.py:433
  95.6 1.7 collective-permute-done.16.other_ref
  97.3 1.5 dispatch.1
  98.8 2.7 %collective-permute-start.17 = (bf16[144,384]{1,0:T(8,128)(2,1)S(1)}, bf16[144,384]{1,0:T(8,128)(2,1)S(1)}, u32[]{:S(2)}, u32[]{:S(2)}) collective-permute-start(bf16[144,384]{1,0:T(8,128)(2,1)S(1)} %get-tuple-element.33), channel_id=1, source_target_pairs={{0,2},{2,0},{4,6},{6,4},{8,10},{10,8},{12,14},{14,12},{1,3},{3,1},... | collective-permute-start | bytes 331784 | tf_op jit(solution)/shard_map/ppermute | solution.py:402
  101.4 1.7 collective-permute-start.18
  103.2 2.9 %collective-permute-start.20 = (bf16[144,384]{1,0:T(8,128)(2,1)S(1)}, bf16[144,384]{1,0:T(8,128)(2,1)S(1)}, u32[]{:S(2)}, u32[]{:S(2)}) collective-permute-start(bf16[144,384]{1,0:T(8,128)(2,1)S(1)} %get-tuple-element.36), channel_id=1, source_target_pairs={{0,8},{2,10},{4,12},{6,14},{8,0},{10,2},{12,4},{14,6},{1,9},{3,11}... | collective-permute-start | bytes 331784 | tf_op jit(solution)/shard_map/ppermute | solution.py:402
  106.1 1.2 collective-permute-start.21
  107.3 2.6 %collective-permute-start.22 = (bf16[144,384]{1,0:T(8,128)(2,1)S(1)}, bf16[144,384]{1,0:T(8,128)(2,1)S(1)}, u32[]{:S(2)}, u32[]{:S(2)}) collective-permute-start(bf16[144,384]{1,0:T(8,128)(2,1)S(1)} %get-tuple-element.38), channel_id=1, source_target_pairs={{0,12},{2,14},{4,8},{6,10},{8,4},{10,6},{12,0},{14,2},{1,13},{3,15... | collective-permute-start | bytes 331784 | tf_op jit(solution)/shard_map/ppermute | solution.py:402
  110.1 3.0 %collective-permute-start.23 = (bf16[144,384]{1,0:T(8,128)(2,1)S(1)}, bf16[144,384]{1,0:T(8,128)(2,1)S(1)}, u32[]{:S(2)}, u32[]{:S(2)}) collective-permute-start(bf16[144,384]{1,0:T(8,128)(2,1)S(1)} %get-tuple-element.39), channel_id=1, source_target_pairs={{0,14},{2,12},{4,10},{6,8},{8,6},{10,4},{12,2},{14,0},{1,15},{3,13... | collective-permute-start | bytes 331784 | tf_op jit(solution)/shard_map/ppermute | solution.py:402
  113.1 5.0 %load_gate.1.gate_ref = bf16[3072,2304]{1,0:T(8,128)(2,1)S(1)} custom-call(bf16[3072,2304]{1,0:T(8,128)(2,1)} %source.1), custom_call_target="tpu_custom_call" | custom-call | bytes 14155776 | tf_op jit(solution)/shard_map/load_gate/pallas_call | solution.py:389
  118.2 4.2 %collective-permute-done.21 = bf16[144,384]{1,0:T(8,128)(2,1)S(1)} collective-permute-done((bf16[144,384]{1,0:T(8,128)(2,1)S(1)}, bf16[144,384]{1,0:T(8,128)(2,1)S(1)}, u32[]{:S(2)}, u32[]{:S(2)}) %collective-permute-start.21) | collective-permute-done | bytes 110624 | tf_op jit(solution)/shard_map/ppermute | solution.py:402
  122.7 0.6 collective-permute-start.24
  123.3 1.1 collective-permute-done.25.near_other.d
  124.4 0.6 collective-permute-done.24.far_other.b
  125.0 19.4 %experts.1 = (bf16[288,1536]{1,0:T(8,128)(2,1)S(1)}, bf16[288,1536]{1,0:T(8,128)(2,1)S(1)}) custom-call(s32[9]{0:T(128)S(1)} %pad_add_fusion.info_ref, bf16[4,144,384]{2,1,0:T(8,128)(2,1)S(1)} %pad_maximum_fusion.far_own.a, bf16[4,144,384]{2,1,0:T(8,128)(2,1)S(1)} %collective-permute-done.24.far_other.b, ...), custom_call_target="tpu_custom_call" | custom-call | flops 12230590464 | bytes 42467328 | tf_op jit(solution)/shard_map/experts/pallas_call | solution.py:347
  144.6 2.3 %collective-permute-done.26.theirs_ref = bf16[288,1536]{1,0:T(8,128)(2,1)S(1)} collective-permute-done((bf16[288,1536]{1,0:T(8,128)(2,1)S(1)}, bf16[288,1536]{1,0:T(8,128)(2,1)S(1)}, u32[]{:S(2)}, u32[]{:S(2)}) %collective-permute-start.26) | collective-permute-done | bytes 884768 | tf_op jit(solution)/shard_map/ppermute | solution.py:24
  146.9 1.8 %weigh.1 = (bf16[144,384]{1,0:T(8,128)(2,1)S(1)}, bf16[144,384]{1,0:T(8,128)(2,1)S(1)}, bf16[144,384]{1,0:T(8,128)(2,1)S(1)}, bf16[144,384]{1,0:T(8,128)(2,1)S(1...) custom-call(s32[6]{0:T(128)S(1)} %stack.51.flags_ref, ...), custom_call_target="tpu_custom_call" | custom-call | tf_op jit(solution)/shard_map/weigh/pallas_call | solution.py:377
  148.7 5.5 %collective-permute-start.27 = (bf16[144,384]{1,0:T(8,128)(2,1)S(1)}, bf16[144,384]{1,0:T(8,128)(2,1)S(1)}, u32[]{:S(2)}, u32[]{:S(2)}) collective-permute-start(bf16[144,384]{1,0:T(8,128)(2,1)S(1)} %get-tuple-element.51), channel_id=1, source_target_pairs={{0,8},{2,10},{4,12},{6,14},{8,0},{10,2},{12,4},{14,6},{1,9},{3,11}... | collective-permute-start | bytes 331784 | tf_op jit(solution)/shard_map/ppermute | solution.py:402
  154.2 1.0 collective-permute-start.28
  155.2 1.2 collective-permute-start.29
  156.3 2.7 %collective-permute-start.30 = (bf16[144,384]{1,0:T(8,128)(2,1)S(1)}, bf16[144,384]{1,0:T(8,128)(2,1)S(1)}, u32[]{:S(2)}, u32[]{:S(2)}) collective-permute-start(bf16[144,384]{1,0:T(8,128)(2,1)S(1)} %get-tuple-element.54), channel_id=1, source_target_pairs={{0,14},{2,12},{4,10},{6,8},{8,6},{10,4},{12,2},{14,0},{1,15},{3,13... | collective-permute-start | bytes 331784 | tf_op jit(solution)/shard_map/ppermute | solution.py:402
  159.0 1.5 collective-permute-start.31
  160.5 7.1 %collective-permute-done.27.refs_0_ = bf16[144,384]{1,0:T(8,128)(2,1)S(1)} collective-permute-done((bf16[144,384]{1,0:T(8,128)(2,1)S(1)}, bf16[144,384]{1,0:T(8,128)(2,1)S(1)}, u32[]{:S(2)}, u32[]{:S(2)}) %collective-permute-start.27) | collective-permute-done | bytes 110624 | tf_op jit(solution)/shard_map/ppermute | solution.py:402
  167.5 3.3 %collective-permute-done.28.refs_1_ = bf16[144,384]{1,0:T(8,128)(2,1)S(1)} collective-permute-done((bf16[144,384]{1,0:T(8,128)(2,1)S(1)}, bf16[144,384]{1,0:T(8,128)(2,1)S(1)}, u32[]{:S(2)}, u32[]{:S(2)}) %collective-permute-start.28) | collective-permute-done | bytes 110624 | tf_op jit(solution)/shard_map/ppermute | solution.py:402
  170.8 1.5 collective-permute-done.32.refs_6_
  172.3 4.2 %collective-permute-done.33.refs_7_ = bf16[144,384]{1,0:T(8,128)(2,1)S(1)} collective-permute-done((bf16[144,384]{1,0:T(8,128)(2,1)S(1)}, bf16[144,384]{1,0:T(8,128)(2,1)S(1)}, u32[]{:S(2)}, u32[]{:S(2)}) %collective-permute-start.33) | collective-permute-done | bytes 110624 | tf_op jit(solution)/shard_map/ppermute | solution.py:402
  176.4 2.3 %combine.1 = bf16[128,1536]{1,0:T(8,128)(2,1)} custom-call(s32[6]{0:T(128)S(1)} %stack.51.flags_ref, s32[2,128]{1,0:T(2,128)S(1)} %bitcast.113, bf16[144,384]{1,0:T(8,128)(2,1)S(1)} %collective-permute-done.27.refs_0_, bf16[144,384]{1,0:T(8,128)(2,1)S(1)} %collective-permute-done.28.refs_1_, bf16[144,384]{1,0:T(8,128)(2,1)S(1)} %collective-permute-done.29.refs_2_, ...), custom_call_target="tpu_custom_call" | custom-call | tf_op jit(solution)/shard_map/combine/pallas_call | solution.py:377
  (76 shorter events, 6.9 us)
Async XLA Ops:
  0.0 56.1 %copy-start = (bf16[2048,384]{1,0:T(8,128)(2,1)S(1)}, bf16[2048,384]{1,0:T(8,128)(2,1)}, u32[]{:S(2)}) copy-start(bf16[2048,384]{1,0:T(8,128)(2,1)} %param.17) | copy-start | bytes 4718596
  0.0 1.2 copy-start.2
  1.2 1.0 copy-start.4
  2.2 0.7 copy-start.12
  2.9 0.7 copy-start.14
  3.6 7.2 %copy-start.16 = (bf16[128,1536]{1,0:T(8,128)(2,1)S(1)}, bf16[128,1536]{1,0:T(8,128)(2,1)}, u32[]{:S(2)}) copy-start(bf16[128,1536]{1,0:T(8,128)(2,1)} %param.15) | copy-start | bytes 1179652
  5.5 17.7 %all-to-all-start = ((bf16[4,528,128]{2,1,0:T(8,128)(2,1)}), bf16[4,528,128]{2,1,0:T(8,128)(2,1)S(1)}, u32[]{:S(2)}, u32[]{:S(2)}) async-start(bf16[4,528,128]{2,1,0:T(8,128)(2,1)} %states.1), calls=%async_computation | async-start | bytes 1081344 | tf_op jit(solution)/shard_map/all_to_all | solution.py:473
  10.8 12.6 %collective-permute-start.1 = (bf16[128,1536]{1,0:T(8,128)(2,1)S(1)}, bf16[128,1536]{1,0:T(8,128)(2,1)S(1)}, u32[]{:S(2)}, u32[]{:S(2)}) collective-permute-start(bf16[128,1536]{1,0:T(8,128)(2,1)S(1)} %copy-done.16), channel_id=1, source_target_pairs={{1,8},{3,10},{5,12},{7,14},{8,1},{10,3},{12,5},{14,7},{17,24},{19,... | collective-permute-start | bytes 1179656 | tf_op jit(solution)/shard_map/ppermute | solution.py:465
  23.2 8.0 %copy-start.8 = (bf16[544,128]{1,0:T(8,128)(2,1)}, bf16[544,128]{1,0:T(8,128)(2,1)S(1)}, u32[]{:S(2)}) copy-start(bf16[544,128]{1,0:T(8,128)(2,1)S(1)} %totals.1.notes_ref) | copy-start | bytes 417796
  23.3 8.0 %collective-permute-start = (bf16[544,128]{1,0:T(8,128)(2,1)S(1)}, bf16[544,128]{1,0:T(8,128)(2,1)S(1)}, u32[]{:S(2)}, u32[]{:S(2)}) collective-permute-start(bf16[544,128]{1,0:T(8,128)(2,1)S(1)} %totals.1.notes_ref), channel_id=1, source_target_pairs={{0,8},{2,10},{4,12},{6,14},{8,0},{10,2},{12,4},{14,6},{1,9},{3,11}... | collective-permute-start | bytes 417800 | tf_op jit(solution)/shard_map/ppermute | solution.py:477
  32.9 0.7 copy-start.6
  33.5 16.3 %copy-start.3 = (bf16[128,2048]{1,0:T(8,128)(2,1)S(1)}, bf16[128,2048]{1,0:T(8,128)(2,1)}, u32[]{:S(2)}) copy-start(bf16[128,2048]{1,0:T(8,128)(2,1)} %k_ref.1) | copy-start | bytes 1572868
  33.5 16.3 %copy-start.5 = (bf16[128,2048]{1,0:T(8,128)(2,1)S(1)}, bf16[128,2048]{1,0:T(8,128)(2,1)}, u32[]{:S(2)}) copy-start(bf16[128,2048]{1,0:T(8,128)(2,1)} %v_ref.1) | copy-start | bytes 1572868
  33.5 16.3 %copy-start.11 = (f32[2048]{0:T(1024)S(1)}, f32[2048]{0:T(1024)}, u32[]{:S(2)}) copy-start(f32[2048]{0:T(1024)} %param.16) | copy-start | bytes 24580
  33.5 16.3 %all-to-all-start.1 = ((bf16[4,896,128]{2,1,0:T(8,128)(2,1)}), bf16[4,896,128]{2,1,0:T(8,128)(2,1)S(1)}, u32[]{:S(2)}, u32[]{:S(2)}) async-start(bf16[4,896,128]{2,1,0:T(8,128)(2,1)} %sums.1), calls=%async_computation.1 | async-start | bytes 1835008 | tf_op jit(solution)/shard_map/all_to_all | solution.py:486
  49.8 1.0 copy-start.10
  51.9 9.3 %collective-permute-start.4 = (bf16[64,2048]{1,0:T(8,128)(2,1)S(1)}, bf16[64,2048]{1,0:T(8,128)(2,1)S(1)}, u32[]{:S(2)}, u32[]{:S(2)}) collective-permute-start(bf16[64,2048]{1,0:T(8,128)(2,1)S(1)} %get-tuple-element.59), channel_id=1, source_target_pairs={{0,4},{4,8},{8,12},{12,14},{14,10},{10,6},{6,2},{2,0},{1,5},{5,9},... | collective-permute-start | bytes 786440 | tf_op jit(solution)/shard_map/ppermute | solution.py:433
  53.4 9.2 %collective-permute-start.5 = (bf16[64,2048]{1,0:T(8,128)(2,1)S(1)}, bf16[64,2048]{1,0:T(8,128)(2,1)S(1)}, u32[]{:S(2)}, u32[]{:S(2)}) collective-permute-start(bf16[64,2048]{1,0:T(8,128)(2,1)S(1)} %get-tuple-element.59), channel_id=1, source_target_pairs={{4,0},{8,4},{12,8},{14,12},{10,14},{6,10},{2,6},{0,2},{5,1},{9,5},... | collective-permute-start | bytes 786440 | tf_op jit(solution)/shard_map/ppermute | solution.py:436
  54.0 12.8 %collective-permute-start.2 = (bf16[64,2048]{1,0:T(8,128)(2,1)S(1)}, bf16[64,2048]{1,0:T(8,128)(2,1)S(1)}, u32[]{:S(2)}, u32[]{:S(2)}) collective-permute-start(bf16[64,2048]{1,0:T(8,128)(2,1)S(1)} %get-tuple-element.60), channel_id=1, source_target_pairs={{0,4},{4,8},{8,12},{12,14},{14,10},{10,6},{6,2},{2,0},{1,5},{5,9},... | collective-permute-start | bytes 786440 | tf_op jit(solution)/shard_map/ppermute | solution.py:433
  55.4 12.8 %collective-permute-start.3 = (bf16[64,2048]{1,0:T(8,128)(2,1)S(1)}, bf16[64,2048]{1,0:T(8,128)(2,1)S(1)}, u32[]{:S(2)}, u32[]{:S(2)}) collective-permute-start(bf16[64,2048]{1,0:T(8,128)(2,1)S(1)} %get-tuple-element.60), channel_id=1, source_target_pairs={{4,0},{8,4},{12,8},{14,12},{10,14},{6,10},{2,6},{0,2},{5,1},{9,5},... | collective-permute-start | bytes 786440 | tf_op jit(solution)/shard_map/ppermute | solution.py:436
  61.2 11.2 %collective-permute-start.8 = (bf16[64,2048]{1,0:T(8,128)(2,1)S(1)}, bf16[64,2048]{1,0:T(8,128)(2,1)S(1)}, u32[]{:S(2)}, u32[]{:S(2)}) collective-permute-start(bf16[64,2048]{1,0:T(8,128)(2,1)S(1)} %collective-permute-done.4), channel_id=1, source_target_pairs={{0,4},{4,8},{8,12},{12,14},{14,10},{10,6},{6,2},{2,0},{1,5},{5,9},... | collective-permute-start | bytes 786440 | tf_op jit(solution)/shard_map/ppermute | solution.py:433
  62.6 11.2 %collective-permute-start.9 = (bf16[64,2048]{1,0:T(8,128)(2,1)S(1)}, bf16[64,2048]{1,0:T(8,128)(2,1)S(1)}, u32[]{:S(2)}, u32[]{:S(2)}) collective-permute-start(bf16[64,2048]{1,0:T(8,128)(2,1)S(1)} %collective-permute-done.5), channel_id=1, source_target_pairs={{4,0},{8,4},{12,8},{14,12},{10,14},{6,10},{2,6},{0,2},{5,1},{9,5},... | collective-permute-start | bytes 786440 | tf_op jit(solution)/shard_map/ppermute | solution.py:436
  66.8 11.2 %collective-permute-start.6 = (bf16[64,2048]{1,0:T(8,128)(2,1)S(1)}, bf16[64,2048]{1,0:T(8,128)(2,1)S(1)}, u32[]{:S(2)}, u32[]{:S(2)}) collective-permute-start(bf16[64,2048]{1,0:T(8,128)(2,1)S(1)} %collective-permute-done.2), channel_id=1, source_target_pairs={{0,4},{4,8},{8,12},{12,14},{14,10},{10,6},{6,2},{2,0},{1,5},{5,9},... | collective-permute-start | bytes 786440 | tf_op jit(solution)/shard_map/ppermute | solution.py:433
  68.2 11.2 %collective-permute-start.7 = (bf16[64,2048]{1,0:T(8,128)(2,1)S(1)}, bf16[64,2048]{1,0:T(8,128)(2,1)S(1)}, u32[]{:S(2)}, u32[]{:S(2)}) collective-permute-start(bf16[64,2048]{1,0:T(8,128)(2,1)S(1)} %collective-permute-done.3), channel_id=1, source_target_pairs={{4,0},{8,4},{12,8},{14,12},{10,14},{6,10},{2,6},{0,2},{5,1},{9,5},... | collective-permute-start | bytes 786440 | tf_op jit(solution)/shard_map/ppermute | solution.py:436
  72.4 18.6 %collective-permute-start.12 = (bf16[64,2048]{1,0:T(8,128)(2,1)S(1)}, bf16[64,2048]{1,0:T(8,128)(2,1)S(1)}, u32[]{:S(2)}, u32[]{:S(2)}) collective-permute-start(bf16[64,2048]{1,0:T(8,128)(2,1)S(1)} %collective-permute-done.8), channel_id=1, source_target_pairs={{0,4},{4,8},{8,12},{12,14},{14,10},{10,6},{6,2},{2,0},{1,5},{5,9},... | collective-permute-start | bytes 786440 | tf_op jit(solution)/shard_map/ppermute | solution.py:433
  73.8 11.2 %collective-permute-start.13 = (bf16[64,2048]{1,0:T(8,128)(2,1)S(1)}, bf16[64,2048]{1,0:T(8,128)(2,1)S(1)}, u32[]{:S(2)}, u32[]{:S(2)}) collective-permute-start(bf16[64,2048]{1,0:T(8,128)(2,1)S(1)} %collective-permute-done.9), channel_id=1, source_target_pairs={{4,0},{8,4},{12,8},{14,12},{10,14},{6,10},{2,6},{0,2},{5,1},{9,5},... | collective-permute-start | bytes 786440 | tf_op jit(solution)/shard_map/ppermute | solution.py:436
  78.0 9.4 %collective-permute-start.10 = (bf16[64,2048]{1,0:T(8,128)(2,1)S(1)}, bf16[64,2048]{1,0:T(8,128)(2,1)S(1)}, u32[]{:S(2)}, u32[]{:S(2)}) collective-permute-start(bf16[64,2048]{1,0:T(8,128)(2,1)S(1)} %collective-permute-done.6), channel_id=1, source_target_pairs={{0,4},{4,8},{8,12},{12,14},{14,10},{10,6},{6,2},{2,0},{1,5},{5,9},... | collective-permute-start | bytes 786440 | tf_op jit(solution)/shard_map/ppermute | solution.py:433
  79.4 11.2 %collective-permute-start.11 = (bf16[64,2048]{1,0:T(8,128)(2,1)S(1)}, bf16[64,2048]{1,0:T(8,128)(2,1)S(1)}, u32[]{:S(2)}, u32[]{:S(2)}) collective-permute-start(bf16[64,2048]{1,0:T(8,128)(2,1)S(1)} %collective-permute-done.7), channel_id=1, source_target_pairs={{4,0},{8,4},{12,8},{14,12},{10,14},{6,10},{2,6},{0,2},{5,1},{9,5},... | collective-permute-start | bytes 786440 | tf_op jit(solution)/shard_map/ppermute | solution.py:436
  85.0 10.0 %collective-permute-start.15 = (bf16[64,2048]{1,0:T(8,128)(2,1)S(1)}, bf16[64,2048]{1,0:T(8,128)(2,1)S(1)}, u32[]{:S(2)}, u32[]{:S(2)}) collective-permute-start(bf16[64,2048]{1,0:T(8,128)(2,1)S(1)} %collective-permute-done.13), channel_id=1, source_target_pairs={{4,0},{8,4},{12,8},{14,12},{10,14},{6,10},{2,6},{0,2},{5,1},{9,5},... | collective-permute-start | bytes 786440 | tf_op jit(solution)/shard_map/ppermute | solution.py:436
  87.4 7.2 %collective-permute-start.14 = (bf16[64,2048]{1,0:T(8,128)(2,1)S(1)}, bf16[64,2048]{1,0:T(8,128)(2,1)S(1)}, u32[]{:S(2)}, u32[]{:S(2)}) collective-permute-start(bf16[64,2048]{1,0:T(8,128)(2,1)S(1)} %collective-permute-done.10), channel_id=1, source_target_pairs={{0,4},{4,8},{8,12},{12,14},{14,10},{10,6},{6,2},{2,0},{1,5},{5,9},... | collective-permute-start | bytes 786440 | tf_op jit(solution)/shard_map/ppermute | solution.py:433
  95.0 2.3 %copy-start.7 = (bf16[544,128]{1,0:T(8,128)(2,1)S(1)}, bf16[544,128]{1,0:T(8,128)(2,1)}, u32[]{:S(2)}) copy-start(bf16[544,128]{1,0:T(8,128)(2,1)} %copy-done.6) | copy-start | bytes 417796
  95.0 2.3 %copy-start.9 = (bf16[544,128]{1,0:T(8,128)(2,1)S(1)}, bf16[544,128]{1,0:T(8,128)(2,1)}, u32[]{:S(2)}) copy-start(bf16[544,128]{1,0:T(8,128)(2,1)} %copy-done.8) | copy-start | bytes 417796
  95.5 1.8 %collective-permute-start.16 = (bf16[4,128,384]{2,1,0:T(8,128)(2,1)S(1)}, bf16[4,128,384]{2,1,0:T(8,128)(2,1)S(1)}, u32[]{:S(2)}, u32[]{:S(2)}) collective-permute-start(bf16[4,128,384]{2,1,0:T(8,128)(2,1)S(1)} %dynamic-slice_convert_fusion), channel_id=1, source_target_pairs={{0,1},{1,0},{2,3},{3,2},{4,5},{5,4},{6,7},{7,6},{8,9},{9,8},{10,11... | collective-permute-start | bytes 1179656 | tf_op jit(solution)/shard_map/ppermute | solution.py:24
  98.8 8.5 %collective-permute-start.17 = (bf16[144,384]{1,0:T(8,128)(2,1)S(1)}, bf16[144,384]{1,0:T(8,128)(2,1)S(1)}, u32[]{:S(2)}, u32[]{:S(2)}) collective-permute-start(bf16[144,384]{1,0:T(8,128)(2,1)S(1)} %get-tuple-element.33), channel_id=1, source_target_pairs={{0,2},{2,0},{4,6},{6,4},{8,10},{10,8},{12,14},{14,12},{1,3},{3,1},... | collective-permute-start | bytes 331784 | tf_op jit(solution)/shard_map/ppermute | solution.py:402
  101.4 8.6 %collective-permute-start.18 = (bf16[144,384]{1,0:T(8,128)(2,1)S(1)}, bf16[144,384]{1,0:T(8,128)(2,1)S(1)}, u32[]{:S(2)}, u32[]{:S(2)}) collective-permute-start(bf16[144,384]{1,0:T(8,128)(2,1)S(1)} %get-tuple-element.34), channel_id=1, source_target_pairs={{0,4},{2,6},{4,0},{6,2},{8,12},{10,14},{12,8},{14,10},{1,5},{3,7},... | collective-permute-start | bytes 331784 | tf_op jit(solution)/shard_map/ppermute | solution.py:402
  103.2 15.0 %collective-permute-start.19 = (bf16[144,384]{1,0:T(8,128)(2,1)S(1)}, bf16[144,384]{1,0:T(8,128)(2,1)S(1)}, u32[]{:S(2)}, u32[]{:S(2)}) collective-permute-start(bf16[144,384]{1,0:T(8,128)(2,1)S(1)} %get-tuple-element.35), channel_id=1, source_target_pairs={{0,6},{2,4},{4,2},{6,0},{8,14},{10,12},{12,10},{14,8},{1,7},{3,5},... | collective-permute-start | bytes 331784 | tf_op jit(solution)/shard_map/ppermute | solution.py:402
  103.2 15.0 %collective-permute-start.20 = (bf16[144,384]{1,0:T(8,128)(2,1)S(1)}, bf16[144,384]{1,0:T(8,128)(2,1)S(1)}, u32[]{:S(2)}, u32[]{:S(2)}) collective-permute-start(bf16[144,384]{1,0:T(8,128)(2,1)S(1)} %get-tuple-element.36), channel_id=1, source_target_pairs={{0,8},{2,10},{4,12},{6,14},{8,0},{10,2},{12,4},{14,6},{1,9},{3,11}... | collective-permute-start | bytes 331784 | tf_op jit(solution)/shard_map/ppermute | solution.py:402
  106.1 16.3 %collective-permute-start.21 = (bf16[144,384]{1,0:T(8,128)(2,1)S(1)}, bf16[144,384]{1,0:T(8,128)(2,1)S(1)}, u32[]{:S(2)}, u32[]{:S(2)}) collective-permute-start(bf16[144,384]{1,0:T(8,128)(2,1)S(1)} %get-tuple-element.37), channel_id=1, source_target_pairs={{0,10},{2,8},{4,14},{6,12},{8,2},{10,0},{12,6},{14,4},{1,11},{3,9}... | collective-permute-start | bytes 331784 | tf_op jit(solution)/shard_map/ppermute | solution.py:402
  107.3 15.1 %collective-permute-start.22 = (bf16[144,384]{1,0:T(8,128)(2,1)S(1)}, bf16[144,384]{1,0:T(8,128)(2,1)S(1)}, u32[]{:S(2)}, u32[]{:S(2)}) collective-permute-start(bf16[144,384]{1,0:T(8,128)(2,1)S(1)} %get-tuple-element.38), channel_id=1, source_target_pairs={{0,12},{2,14},{4,8},{6,10},{8,4},{10,6},{12,0},{14,2},{1,13},{3,15... | collective-permute-start | bytes 331784 | tf_op jit(solution)/shard_map/ppermute | solution.py:402
  110.1 12.4 %collective-permute-start.23 = (bf16[144,384]{1,0:T(8,128)(2,1)S(1)}, bf16[144,384]{1,0:T(8,128)(2,1)S(1)}, u32[]{:S(2)}, u32[]{:S(2)}) collective-permute-start(bf16[144,384]{1,0:T(8,128)(2,1)S(1)} %get-tuple-element.39), channel_id=1, source_target_pairs={{0,14},{2,12},{4,10},{6,8},{8,6},{10,4},{12,2},{14,0},{1,15},{3,13... | collective-permute-start | bytes 331784 | tf_op jit(solution)/shard_map/ppermute | solution.py:402
  118.1 6.9 %copy-start.15 = (f32[3072]{0:T(1024)S(1)}, f32[3072]{0:T(1024)}, u32[]{:S(2)}) copy-start(f32[3072]{0:T(1024)} %param.18) | copy-start | bytes 36868
  122.5 1.9 %collective-permute-start.25 = (bf16[4,144,384]{2,1,0:T(8,128)(2,1)S(1)}, bf16[4,144,384]{2,1,0:T(8,128)(2,1)S(1)}, u32[]{:S(2)}, u32[]{:S(2)}) collective-permute-start(bf16[4,144,384]{2,1,0:T(8,128)(2,1)S(1)} %pad_maximum_fusion.1.near_own.c), channel_id=1, source_target_pairs={{0,1},{1,0},{2,3},{3,2},{4,5},{5,4},{6,7},{7,6},{8,9},{9,8},{10,11... | collective-permute-start | bytes 1327112 | tf_op jit(solution)/shard_map/ppermute | solution.py:24
  122.7 2.3 %collective-permute-start.24 = (bf16[4,144,384]{2,1,0:T(8,128)(2,1)S(1)}, bf16[4,144,384]{2,1,0:T(8,128)(2,1)S(1)}, u32[]{:S(2)}, u32[]{:S(2)}) collective-permute-start(bf16[4,144,384]{2,1,0:T(8,128)(2,1)S(1)} %pad_maximum_fusion.far_own.a), channel_id=1, source_target_pairs={{0,1},{1,0},{2,3},{3,2},{4,5},{5,4},{6,7},{7,6},{8,9},{9,8},{10,11... | collective-permute-start | bytes 1327112 | tf_op jit(solution)/shard_map/ppermute | solution.py:24
  144.4 2.5 %collective-permute-start.26 = (bf16[288,1536]{1,0:T(8,128)(2,1)S(1)}, bf16[288,1536]{1,0:T(8,128)(2,1)S(1)}, u32[]{:S(2)}, u32[]{:S(2)}) collective-permute-start(bf16[288,1536]{1,0:T(8,128)(2,1)S(1)} %get-tuple-element.50), channel_id=1, source_target_pairs={{0,1},{1,0},{2,3},{3,2},{4,5},{5,4},{6,7},{7,6},{8,9},{9,8},{10,11... | collective-permute-start | bytes 2654216 | tf_op jit(solution)/shard_map/ppermute | solution.py:24
  146.9 29.5 %copy-start.13 = (s32[128,2]{0,1:T(2,128)S(1)}, s32[128,2]{0,1:T(2,128)}, u32[]{:S(2)}) copy-start(s32[128,2]{0,1:T(2,128)} %param.19) | copy-start | bytes 3076
  146.9 31.9 %copy-start.1 = (bf16[2048,384]{1,0:T(8,128)(2,1)S(1)}, bf16[2048,384]{1,0:T(8,128)(2,1)}, u32[]{:S(2)}) copy-start(bf16[2048,384]{1,0:T(8,128)(2,1)} %param.17) | copy-start | bytes 4718596
  148.7 18.8 %collective-permute-start.27 = (bf16[144,384]{1,0:T(8,128)(2,1)S(1)}, bf16[144,384]{1,0:T(8,128)(2,1)S(1)}, u32[]{:S(2)}, u32[]{:S(2)}) collective-permute-start(bf16[144,384]{1,0:T(8,128)(2,1)S(1)} %get-tuple-element.51), channel_id=1, source_target_pairs={{0,8},{2,10},{4,12},{6,14},{8,0},{10,2},{12,4},{14,6},{1,9},{3,11}... | collective-permute-start | bytes 331784 | tf_op jit(solution)/shard_map/ppermute | solution.py:402
  154.2 16.6 %collective-permute-start.28 = (bf16[144,384]{1,0:T(8,128)(2,1)S(1)}, bf16[144,384]{1,0:T(8,128)(2,1)S(1)}, u32[]{:S(2)}, u32[]{:S(2)}) collective-permute-start(bf16[144,384]{1,0:T(8,128)(2,1)S(1)} %get-tuple-element.52), channel_id=1, source_target_pairs={{0,10},{2,8},{4,14},{6,12},{8,2},{10,0},{12,6},{14,4},{1,11},{3,9}... | collective-permute-start | bytes 331784 | tf_op jit(solution)/shard_map/ppermute | solution.py:402
  155.2 15.6 %collective-permute-start.29 = (bf16[144,384]{1,0:T(8,128)(2,1)S(1)}, bf16[144,384]{1,0:T(8,128)(2,1)S(1)}, u32[]{:S(2)}, u32[]{:S(2)}) collective-permute-start(bf16[144,384]{1,0:T(8,128)(2,1)S(1)} %get-tuple-element.53), channel_id=1, source_target_pairs={{0,12},{2,14},{4,8},{6,10},{8,4},{10,6},{12,0},{14,2},{1,13},{3,15... | collective-permute-start | bytes 331784 | tf_op jit(solution)/shard_map/ppermute | solution.py:402
  156.3 14.5 %collective-permute-start.30 = (bf16[144,384]{1,0:T(8,128)(2,1)S(1)}, bf16[144,384]{1,0:T(8,128)(2,1)S(1)}, u32[]{:S(2)}, u32[]{:S(2)}) collective-permute-start(bf16[144,384]{1,0:T(8,128)(2,1)S(1)} %get-tuple-element.54), channel_id=1, source_target_pairs={{0,14},{2,12},{4,10},{6,8},{8,6},{10,4},{12,2},{14,0},{1,15},{3,13... | collective-permute-start | bytes 331784 | tf_op jit(solution)/shard_map/ppermute | solution.py:402
  159.0 11.8 %collective-permute-start.31 = (bf16[144,384]{1,0:T(8,128)(2,1)S(1)}, bf16[144,384]{1,0:T(8,128)(2,1)S(1)}, u32[]{:S(2)}, u32[]{:S(2)}) collective-permute-start(bf16[144,384]{1,0:T(8,128)(2,1)S(1)} %get-tuple-element.56), channel_id=1, source_target_pairs={{0,2},{2,0},{4,6},{6,4},{8,10},{10,8},{12,14},{14,12},{1,3},{3,1},... | collective-permute-start | bytes 331784 | tf_op jit(solution)/shard_map/ppermute | solution.py:402
  167.5 4.7 %collective-permute-start.32 = (bf16[144,384]{1,0:T(8,128)(2,1)S(1)}, bf16[144,384]{1,0:T(8,128)(2,1)S(1)}, u32[]{:S(2)}, u32[]{:S(2)}) collective-permute-start(bf16[144,384]{1,0:T(8,128)(2,1)S(1)} %get-tuple-element.57), channel_id=1, source_target_pairs={{0,4},{2,6},{4,0},{6,2},{8,12},{10,14},{12,8},{14,10},{1,5},{3,7},... | collective-permute-start | bytes 331784 | tf_op jit(solution)/shard_map/ppermute | solution.py:402
  170.8 5.6 %collective-permute-start.33 = (bf16[144,384]{1,0:T(8,128)(2,1)S(1)}, bf16[144,384]{1,0:T(8,128)(2,1)S(1)}, u32[]{:S(2)}, u32[]{:S(2)}) collective-permute-start(bf16[144,384]{1,0:T(8,128)(2,1)S(1)} %get-tuple-element.58), channel_id=1, source_target_pairs={{0,6},{2,4},{4,2},{6,0},{8,14},{10,12},{12,10},{14,8},{1,7},{3,5},... | collective-permute-start | bytes 331784 | tf_op jit(solution)/shard_map/ppermute | solution.py:402

commit v3 on v2

--- a/solution.py
+++ b/solution.py
@@ -18,6 +18,7 @@
 F32 = jnp.float32
 MIB = 1024 * 1024
 VMEM_BYTES = 10 * MIB
+ROOM_ALL = 6.2
 
 
 def swap_cores(x):
@@ -32,7 +33,7 @@
     return lax.dot_general(a, b, ((dims[:1], dims[1:]), ((), ())), preferred_element_type=F32)
 
 
-def state_kernel(heads, half, routes_ref, weights_ref, k_hbm, v_hbm, out_ref, k_ref, v_ref, sems):
+def state_kernel(heads, half, k_hbm, v_hbm, out_ref, k_ref, v_ref, sems):
     width = heads * HD
     copies = []
     for j in range(half):
@@ -44,6 +45,21 @@
         for copy in pair:
             copy.start()
         copies.append(pair)
+    for j in range(half):
+        for copy in copies[j]:
+            copy.wait()
+        for n in range(heads):
+            lo = n * HD
+            state = contract(k_ref[j, :, lo : lo + HD], v_ref[j, :, lo : lo + HD], (0, 0))
+            out_ref[j, lo : lo + HD] = state.astype(BF)
+
+
+def total_kernel(routes_ref, weights_ref, x_ref, out_ref):
+    blocks, width, _ = x_ref.shape
+    total = x_ref[0].astype(F32)
+    for b in range(1, blocks):
+        total = total + x_ref[b].astype(F32)
+    out_ref[:width] = total.astype(BF)
     routes = routes_ref[...].astype(F32)
     weights = weights_ref[...]
     rows = [routes[0:1], routes[1:2]]
@@ -53,38 +69,26 @@
             piece = rest.astype(BF).astype(F32)
             rows.append(piece)
             rest = rest - piece
-    spare = jnp.zeros((out_ref.shape[1] - width - NOTES, routes.shape[1]), F32)
-    notes = jnp.concatenate(rows + [spare], axis=0).astype(BF)
-    for j in range(half):
-        for copy in copies[j]:
-            copy.wait()
-        for n in range(heads):
-            lo = n * HD
-            state = contract(k_ref[j, :, lo : lo + HD], v_ref[j, :, lo : lo + HD], (0, 0))
-            out_ref[j, lo : lo + HD] = state.astype(BF)
-        out_ref[j, width:] = notes
-
-
-def total_kernel(width, x_ref, out_ref):
-    blocks = x_ref.shape[0]
-    total = x_ref[0, :width].astype(F32)
-    for b in range(1, blocks):
-        total = total + x_ref[b, :width].astype(F32)
-    out_ref[:width] = total.astype(BF)
-    notes = [x_ref[b, width : width + NOTES].astype(F32) for b in range(blocks)]
-    out_ref[width:] = jnp.concatenate(notes, axis=0).astype(BF)
-
-
-def before_kernel(width, flags_ref, x_ref, far_ref, resid_ref, out_ref):
+    spare = jnp.zeros((out_ref.shape[0] - width - NOTES, routes.shape[1]), F32)
+    out_ref[width:] = jnp.concatenate(rows + [spare], axis=0).astype(BF)
+
+
+def before_kernel(width, flags_ref, x_ref, near_ref, far_ref, resid_ref, out_ref):
     blocks = x_ref.shape[0]
     tok = resid_ref.shape[-2]
     split = len(resid_ref.shape) == 3
     cols = resid_ref.shape[2] if split else resid_ref.shape[1] // blocks
-    running = jnp.where(flags_ref[1] == 1, far_ref[:width].astype(F32), 0.0)
+    upper = flags_ref[1] == 1
+    near = near_ref[width : width + NOTES].astype(F32)
+    far = far_ref[width : width + NOTES].astype(F32)
+    notes = jnp.concatenate([jnp.where(upper, far, near), jnp.where(upper, near, far)], axis=0)
+    notes = notes.astype(BF)
+    running = jnp.where(upper, far_ref[:width].astype(F32), 0.0)
     for b in range(blocks):
         out_ref[b, :width] = running.astype(BF)
+        out_ref[b, out_ref.shape[1] - 2 * NOTES :] = notes
         if b < blocks - 1:
-            running = running + x_ref[b, :width].astype(F32)
+            running = running + x_ref[b].astype(F32)
         for m in range(0, cols, 128):
             lanes = min(128, cols - m)
             lo = width + m // 128 * tok
@@ -94,6 +98,19 @@
                 out_ref[b, lo : lo + tok, :lanes] = resid_ref[:, b * cols + m : b * cols + m + lanes]
             if lanes < 128:
                 out_ref[b, lo : lo + tok, lanes:] = jnp.zeros((tok, 128 - lanes), BF)
+
+
+def notes_of(sums_ref, half):
+    blocks, height, _ = sums_ref.shape
+    first = height - 2 * NOTES
+    parts = []
+    for b in range(blocks):
+        both = sums_ref[b, first:].astype(F32)
+        if isinstance(half, int):
+            parts.append(both[half * NOTES : (half + 1) * NOTES])
+        else:
+            parts.append(jnp.where(half == 0, both[:NOTES], both[NOTES:]))
+    return jnp.concatenate(parts, axis=0)
 
 
 def attention_kernel(q_ref, k_ref, v_ref, before_ref, gain_ref, out_ref):
@@ -123,13 +140,11 @@
     return dot(hits.astype(BF), before)
 
 
-def dispatch_kernel(
-    per_expert, flags_ref, acc_ref, other_ref, resid_ref, notes_ref, far_ref, *refs
-):
+def dispatch_kernel(per_expert, flags_ref, acc_ref, other_ref, resid_ref, *refs):
     outs, place_ref = refs[:-1], refs[-1]
     core = flags_ref[0]
     blocks, tok, cols = other_ref.shape
-    base = resid_ref.shape[1] - -(-cols // 128) * tok
+    base = resid_ref.shape[1] - 2 * NOTES - -(-cols // 128) * tok
     parts = []
     for b in range(blocks):
         own = acc_ref[core * blocks + b] + other_ref[b].astype(F32)
@@ -139,9 +154,7 @@
         ]
         parts.append((own + jnp.concatenate(pieces, axis=1).astype(F32)).astype(BF))
     hidden = jnp.concatenate(parts, axis=0)
-    first = notes_ref.shape[0] - NOTES * blocks
-    near = core == flags_ref[1]
-    notes = jnp.where(near, notes_ref[first:].astype(F32), far_ref[first:].astype(F32))
+    notes = notes_of(resid_ref, core)
     expert = lax.broadcasted_iota(jnp.int32, (EXPERTS, tok), 0).astype(F32)
     for b in range(blocks):
         at = b * NOTES
@@ -156,13 +169,12 @@
         out_ref[...] = dot(pick, hidden).astype(BF)
 
 
-def return_kernel(flags_ref, mine_ref, theirs_ref, x_refs, notes_ref, far_ref, outs, row_ref):
+def return_kernel(flags_ref, mine_ref, theirs_ref, x_refs, sums_ref, outs, row_ref):
     core, upper, expert, leads = flags_ref[0], flags_ref[1], flags_ref[3], flags_ref[4]
     far_own, far_other, near_own, near_other = x_refs
     pieces, rows, _ = near_own.shape
     blocks = rows // CAP
-    tok = notes_ref.shape[1]
-    first = notes_ref.shape[0] - NOTES * blocks
+    tok = sums_ref.shape[2]
     piece_width = mine_ref.shape[1] // FOLD
     slot = lax.broadcasted_iota(jnp.int32, (rows, blocks * tok), 0).astype(F32)
     block_of = lax.broadcasted_iota(jnp.int32, (blocks, tok), 0).astype(F32)
@@ -178,7 +190,7 @@
         return jnp.where(core == upper, piece_of(near, m), piece_of(far, m))
 
     for half in range(2):
-        notes = jnp.where(upper == half, notes_ref[first:].astype(F32), far_ref[first:].astype(F32))
+        notes = notes_of(sums_ref, half)
 
         def line(i):
             return jnp.concatenate(
@@ -214,10 +226,8 @@
         out_ref[...] = row_ref[k]
 
 
-def return_entry(flags_ref, mine_ref, theirs_ref, a, b, c, d, notes_ref, far_ref, *refs):
-    return_kernel(
-        flags_ref, mine_ref, theirs_ref, (a, b, c, d), notes_ref, far_ref, refs[:-1], refs[-1]
-    )
+def return_entry(flags_ref, mine_ref, theirs_ref, a, b, c, d, sums_ref, *refs):
+    return_kernel(flags_ref, mine_ref, theirs_ref, (a, b, c, d), sums_ref, refs[:-1], refs[-1])
 
 
 def combine_kernel(per_expert, order, flags_ref, routes_ref, *refs):
@@ -380,7 +390,7 @@
         in_specs=[smem] * scalars + [vmem] * inside + [anywhere] * hbm,
         out_specs=out_specs,
         scratch_shapes=scratch,
-        compiler_params=pltpu.CompilerParams(vmem_limit_bytes=room * VMEM_BYTES),
+        compiler_params=pltpu.CompilerParams(vmem_limit_bytes=int(room * VMEM_BYTES)),
         name=name,
     )(*operands)
 
@@ -466,13 +476,14 @@
 
     hbm_blocks = pltpu.VMEM((half, tok, width), BF)
     states = on_chip(
-        functools.partial(state_kernel, local, half), "states", ((half, width + 16, HD), BF),
-        routes_by_lane, route_weights.T, keys, values,
-        hbm=2, scratch=(hbm_blocks, hbm_blocks, pltpu.SemaphoreType.DMA((2, half))),
+        functools.partial(state_kernel, local, half), "states", ((half, width, HD), BF),
+        keys, values,
+        hbm=2, scratch=(hbm_blocks, hbm_blocks, pltpu.SemaphoreType.DMA((2, half))), room=ROOM_ALL,
     )
     blocks = lax.all_to_all(states, "seq", 0, 0, axis_index_groups=groups, tiled=True)
     own_sum = on_chip(
-        functools.partial(total_kernel, width), "totals", ((width + half * NOTES, HD), BF), blocks
+        total_kernel, "totals", ((width + 2 * NOTES, HD), BF),
+        routes_by_lane, route_weights.T, blocks,
     )
     far_sum = lax.ppermute(own_sum, "seq", [(s, (s + half) % seq_count) for s in chips])
     sliced = jnp.where(me // half == core, resid, crossed)
@@ -480,8 +491,8 @@
         sliced = sliced.reshape(tok, half, cols).transpose(1, 0, 2)
     chunks = -(-cols // 128)
     sums = on_chip(
-        functools.partial(before_kernel, width), "sums", ((half, width + chunks * tok, HD), BF),
-        flags, blocks, far_sum, sliced, scalars=1,
+        functools.partial(before_kernel, width), "sums", ((half, width + chunks * tok + 2 * NOTES, HD), BF),
+        flags, blocks, own_sum, far_sum, sliced, scalars=1,
     )
     sums = lax.all_to_all(sums, "seq", 0, 0, axis_index_groups=groups, tiled=True)
     normed = on_chip(
@@ -496,7 +507,7 @@
     pieces = list(on_chip(
         functools.partial(dispatch_kernel, per_expert), "dispatch",
         [((rows, cols), BF)] * seq_count,
-        flags, acc, other, sums, own_sum, far_sum,
+        flags, acc, other, sums,
         scalars=1, room=half // 4, scratch=[pltpu.VMEM((EXPERTS, half * tok), F32)],
     ))
     got = [None] * seq_count
@@ -521,7 +532,7 @@
     piece = half_width // FOLD
     out = on_chip(
         return_entry, "weigh", [((FOLD * CAP, piece), BF)] * seq_count,
-        flags, mine, swap_cores(theirs), *parts, own_sum, far_sum,
+        flags, mine, swap_cores(theirs), *parts, sums,
         scalars=1, room=half // 4, scratch=[pltpu.VMEM((seq_count, FOLD * CAP, piece), BF)],
     )
     order = list(range(half, seq_count)) + list(range(half))

time: 179 us -> 178 us (level)
    unnamed x34 -> x22, local copies, waits for them, and re-layouts: 5.31 us -> 4.12 us
where the time goes in v3:
time: 178 us; the launch traced here: 177 us
  waiting for transfers between devices  80.5 us (45%)
  starting transfers between devices  51.4 us (29%)
  Pallas kernels  34.6 us (19%)
  matrix products  5.8 us (3%)
  local copies, waits for them, and re-layouts  4.4 us (2%)
    ppermute x14, starting transfers between devices, xor_shift(): lax.ppermute(x, 'seq', [(s, s ^ k) for s in range(lax.axis_size('seq'))])  25.9 us
    ppermute x14, waiting for transfers between devices, xor_shift(): lax.ppermute(x, 'seq', [(s, s ^ k) for s in range(lax.axis_size('seq'))])  20.3 us
    pallas_call x1, Pallas kernels, experts(): pl.pallas_call(moe_kernel, out_shape=(out, out), in_specs=[smem] + [vmem]...  19.4 us
    ppermute x7, waiting for transfers between devices, ring_project(): back[i] = lax.ppermute(back[i], 'seq', ahead)  18.2 us
    all_to_all x1, waiting for transfers between devices, per_device(): lax.all_to_all(sums, 'seq', 0, 0, axis_index_groups=groups, tiled=True)  12.6 us
    all_to_all x1, waiting for transfers between devices, per_device(): lax.all_to_all(states, 'seq', 0, 0, axis_index_groups=groups, tiled=True)  11.3 us
    ppermute x7, starting transfers between devices, ring_project(): back[i] = lax.ppermute(back[i], 'seq', ahead)  10.5 us
    pallas_call x7, Pallas kernels, on_chip(): pl.pallas_call(kernel, out_shape=out_shape, in_specs=[smem] * scalars + [...  10.2 us
  transfers between devices with their start and end apart: 36, of which 22 were waited for; matrix products, arithmetic and copies ran while one was open for 3% of the time, Pallas kernels for 3%

profile of v3, /device:TPU:0, one launch (start us, length us, event | category | flops | bytes accessed | tf_op | source)
XLA Modules:
  0.0 177.5 jit_solution(2493159740513565511)
XLA Ops:
  0.0 2.8 %states.1 = bf16[4,512,128]{2,1,0:T(8,128)(2,1)} custom-call(bf16[128,2048]{1,0:T(8,128)(2,1)} %k_ref.1, bf16[128,2048]{1,0:T(8,128)(2,1)} %v_ref.1), custom_call_target="tpu_custom_call" | custom-call | tf_op jit(solution)/shard_map/states/pallas_call | solution.py:387
  2.9 5.3 %all-to-all-start = ((bf16[4,512,128]{2,1,0:T(8,128)(2,1)}), bf16[4,512,128]{2,1,0:T(8,128)(2,1)S(1)}, u32[]{:S(2)}, u32[]{:S(2)}) async-start(bf16[4,512,128]{2,1,0:T(8,128)(2,1)} %states.1), calls=%async_computation | async-start | bytes 1048576 | tf_op jit(solution)/shard_map/all_to_all | solution.py:483
  8.1 0.7 collective-permute-start.1
  8.9 11.3 %all-to-all-done.x_ref = bf16[4,512,128]{2,1,0:T(8,128)(2,1)S(1)} async-done(((bf16[4,512,128]{2,1,0:T(8,128)(2,1)}), bf16[4,512,128]{2,1,0:T(8,128)(2,1)S(1)}, u32[]{:S(2)}, u32[]{:S(2)}) %all-to-all-start) | async-done | bytes 524320 | tf_op jit(solution)/shard_map/all_to_all | solution.py:483
  20.4 8.0 %collective-permute-done.far_ref = bf16[528,128]{1,0:T(8,128)(2,1)S(1)} collective-permute-done((bf16[528,128]{1,0:T(8,128)(2,1)S(1)}, bf16[528,128]{1,0:T(8,128)(2,1)S(1)}, u32[]{:S(2)}, u32[]{:S(2)}) %collective-permute-start) | collective-permute-done | bytes 135200 | tf_op jit(solution)/shard_map/ppermute | solution.py:488
  28.4 0.7 sums.1
  29.1 1.0 copy-done.2
  30.1 3.6 %all-to-all-start.1 = ((bf16[4,912,128]{2,1,0:T(8,128)(2,1)}), bf16[4,912,128]{2,1,0:T(8,128)(2,1)S(1)}, u32[]{:S(2)}, u32[]{:S(2)}) async-start(bf16[4,912,128]{2,1,0:T(8,128)(2,1)} %copy-done.2), calls=%async_computation.1 | async-start | bytes 1867776 | tf_op jit(solution)/shard_map/all_to_all | solution.py:497
  34.0 12.6 %all-to-all-done.1.before_ref.resid_ref.sums_ref = bf16[4,912,128]{2,1,0:T(8,128)(2,1)S(1)} async-done(((bf16[4,912,128]{2,1,0:T(8,128)(2,1)}), bf16[4,912,128]{2,1,0:T(8,128)(2,1)S(1)}, u32[]{:S(2)}, u32[]{:S(2)}) %all-to-all-start.1) | async-done | bytes 933920 | tf_op jit(solution)/shard_map/all_to_all | solution.py:497
  46.6 1.0 copy-done.3
  47.6 1.0 copy-done.4
  48.7 1.0 copy-done.5
  49.7 1.0 attention.1
  50.7 1.5 collective-permute-start.4
  52.2 0.6 collective-permute-start.5
  52.8 1.4 collective-permute-start.2
  54.2 0.6 collective-permute-start.3
  55.7 4.4 %collective-permute-done.4 = bf16[64,2048]{1,0:T(8,128)(2,1)S(1)} collective-permute-done((bf16[64,2048]{1,0:T(8,128)(2,1)S(1)}, bf16[64,2048]{1,0:T(8,128)(2,1)S(1)}, u32[]{:S(2)}, u32[]{:S(2)}) %collective-permute-start.4) | collective-permute-done | bytes 262176 | tf_op jit(solution)/shard_map/ppermute | solution.py:443
  60.0 1.3 collective-permute-start.8
  61.4 0.6 collective-permute-start.9
  62.1 3.6 %collective-permute-done.2 = bf16[64,2048]{1,0:T(8,128)(2,1)S(1)} collective-permute-done((bf16[64,2048]{1,0:T(8,128)(2,1)S(1)}, bf16[64,2048]{1,0:T(8,128)(2,1)S(1)}, u32[]{:S(2)}, u32[]{:S(2)}) %collective-permute-start.2) | collective-permute-done | bytes 262176 | tf_op jit(solution)/shard_map/ppermute | solution.py:443
  65.7 1.3 collective-permute-start.6
  67.0 0.6 collective-permute-start.7
  68.1 0.4 fusion.12
  68.8 0.4 fusion.10
  69.2 2.1 %collective-permute-done.8 = bf16[64,2048]{1,0:T(8,128)(2,1)S(1)} collective-permute-done((bf16[64,2048]{1,0:T(8,128)(2,1)S(1)}, bf16[64,2048]{1,0:T(8,128)(2,1)S(1)}, u32[]{:S(2)}, u32[]{:S(2)}) %collective-permute-start.8) | collective-permute-done | bytes 262176 | tf_op jit(solution)/shard_map/ppermute | solution.py:443
  71.3 1.3 collective-permute-start.12
  72.6 0.6 collective-permute-start.13
  73.3 3.6 %collective-permute-done.6 = bf16[64,2048]{1,0:T(8,128)(2,1)S(1)} collective-permute-done((bf16[64,2048]{1,0:T(8,128)(2,1)S(1)}, bf16[64,2048]{1,0:T(8,128)(2,1)S(1)}, u32[]{:S(2)}, u32[]{:S(2)}) %collective-permute-start.6) | collective-permute-done | bytes 262176 | tf_op jit(solution)/shard_map/ppermute | solution.py:443
  76.9 1.3 collective-permute-start.10
  78.3 0.6 collective-permute-start.11
  80.4 3.5 %collective-permute-done.13 = bf16[64,2048]{1,0:T(8,128)(2,1)S(1)} collective-permute-done((bf16[64,2048]{1,0:T(8,128)(2,1)S(1)}, bf16[64,2048]{1,0:T(8,128)(2,1)S(1)}, u32[]{:S(2)}, u32[]{:S(2)}) %collective-permute-start.13) | collective-permute-done | bytes 262176 | tf_op jit(solution)/shard_map/ppermute | solution.py:446
  83.9 0.6 collective-permute-start.15
  84.5 1.8 collective-permute-done.10
  86.3 2.2 %collective-permute-start.14 = (bf16[64,2048]{1,0:T(8,128)(2,1)S(1)}, bf16[64,2048]{1,0:T(8,128)(2,1)S(1)}, u32[]{:S(2)}, u32[]{:S(2)}) collective-permute-start(bf16[64,2048]{1,0:T(8,128)(2,1)S(1)} %collective-permute-done.10), channel_id=1, source_target_pairs={{0,4},{4,8},{8,12},{12,14},{14,10},{10,6},{6,2},{2,0},{1,5},{5,9},... | collective-permute-start | bytes 786440 | tf_op jit(solution)/shard_map/ppermute | solution.py:443
  88.9 0.6 collective-permute-done.11
  90.2 0.4 fusion.2
  90.6 2.8 %collective-permute-done.14 = bf16[64,2048]{1,0:T(8,128)(2,1)S(1)} collective-permute-done((bf16[64,2048]{1,0:T(8,128)(2,1)S(1)}, bf16[64,2048]{1,0:T(8,128)(2,1)S(1)}, u32[]{:S(2)}, u32[]{:S(2)}) %collective-permute-start.14) | collective-permute-done | bytes 262176 | tf_op jit(solution)/shard_map/ppermute | solution.py:443
  94.4 1.7 collective-permute-done.16.other_ref
  96.1 1.5 dispatch.1
  97.6 2.5 %collective-permute-start.17 = (bf16[144,384]{1,0:T(8,128)(2,1)S(1)}, bf16[144,384]{1,0:T(8,128)(2,1)S(1)}, u32[]{:S(2)}, u32[]{:S(2)}) collective-permute-start(bf16[144,384]{1,0:T(8,128)(2,1)S(1)} %get-tuple-element.33), channel_id=1, source_target_pairs={{0,2},{2,0},{4,6},{6,4},{8,10},{10,8},{12,14},{14,12},{1,3},{3,1},... | collective-permute-start | bytes 331784 | tf_op jit(solution)/shard_map/ppermute | solution.py:412
  100.1 1.7 collective-permute-start.18
  101.8 2.9 %collective-permute-start.20 = (bf16[144,384]{1,0:T(8,128)(2,1)S(1)}, bf16[144,384]{1,0:T(8,128)(2,1)S(1)}, u32[]{:S(2)}, u32[]{:S(2)}) collective-permute-start(bf16[144,384]{1,0:T(8,128)(2,1)S(1)} %get-tuple-element.36), channel_id=1, source_target_pairs={{0,8},{2,10},{4,12},{6,14},{8,0},{10,2},{12,4},{14,6},{1,9},{3,11}... | collective-permute-start | bytes 331784 | tf_op jit(solution)/shard_map/ppermute | solution.py:412
  104.7 1.2 collective-permute-start.21
  105.9 2.6 %collective-permute-start.22 = (bf16[144,384]{1,0:T(8,128)(2,1)S(1)}, bf16[144,384]{1,0:T(8,128)(2,1)S(1)}, u32[]{:S(2)}, u32[]{:S(2)}) collective-permute-start(bf16[144,384]{1,0:T(8,128)(2,1)S(1)} %get-tuple-element.38), channel_id=1, source_target_pairs={{0,12},{2,14},{4,8},{6,10},{8,4},{10,6},{12,0},{14,2},{1,13},{3,15... | collective-permute-start | bytes 331784 | tf_op jit(solution)/shard_map/ppermute | solution.py:412
  108.7 3.1 %collective-permute-start.23 = (bf16[144,384]{1,0:T(8,128)(2,1)S(1)}, bf16[144,384]{1,0:T(8,128)(2,1)S(1)}, u32[]{:S(2)}, u32[]{:S(2)}) collective-permute-start(bf16[144,384]{1,0:T(8,128)(2,1)S(1)} %get-tuple-element.39), channel_id=1, source_target_pairs={{0,14},{2,12},{4,10},{6,8},{8,6},{10,4},{12,2},{14,0},{1,15},{3,13... | collective-permute-start | bytes 331784 | tf_op jit(solution)/shard_map/ppermute | solution.py:412
  111.8 5.0 %load_gate.1.gate_ref = bf16[3072,2304]{1,0:T(8,128)(2,1)S(1)} custom-call(bf16[3072,2304]{1,0:T(8,128)(2,1)} %source.1), custom_call_target="tpu_custom_call" | custom-call | bytes 14155776 | tf_op jit(solution)/shard_map/load_gate/pallas_call | solution.py:399
  116.9 4.2 %collective-permute-done.21 = bf16[144,384]{1,0:T(8,128)(2,1)S(1)} collective-permute-done((bf16[144,384]{1,0:T(8,128)(2,1)S(1)}, bf16[144,384]{1,0:T(8,128)(2,1)S(1)}, u32[]{:S(2)}, u32[]{:S(2)}) %collective-permute-start.21) | collective-permute-done | bytes 110624 | tf_op jit(solution)/shard_map/ppermute | solution.py:412
  121.3 0.6 collective-permute-start.24
  122.0 1.1 collective-permute-done.25.near_other.d
  123.0 0.6 collective-permute-done.24.far_other.b
  123.7 19.4 %experts.1 = (bf16[288,1536]{1,0:T(8,128)(2,1)S(1)}, bf16[288,1536]{1,0:T(8,128)(2,1)S(1)}) custom-call(s32[9]{0:T(128)S(1)} %pad_add_fusion.info_ref, bf16[4,144,384]{2,1,0:T(8,128)(2,1)S(1)} %pad_maximum_fusion.far_own.a, bf16[4,144,384]{2,1,0:T(8,128)(2,1)S(1)} %collective-permute-done.24.far_other.b, ...), custom_call_target="tpu_custom_call" | custom-call | flops 12230590464 | bytes 42467328 | tf_op jit(solution)/shard_map/experts/pallas_call | solution.py:357
  143.3 2.3 %collective-permute-done.26.theirs_ref = bf16[288,1536]{1,0:T(8,128)(2,1)S(1)} collective-permute-done((bf16[288,1536]{1,0:T(8,128)(2,1)S(1)}, bf16[288,1536]{1,0:T(8,128)(2,1)S(1)}, u32[]{:S(2)}, u32[]{:S(2)}) %collective-permute-start.26) | collective-permute-done | bytes 884768 | tf_op jit(solution)/shard_map/ppermute | solution.py:25
  145.6 1.8 %weigh.1 = (bf16[144,384]{1,0:T(8,128)(2,1)S(1)}, bf16[144,384]{1,0:T(8,128)(2,1)S(1)}, bf16[144,384]{1,0:T(8,128)(2,1)S(1)}, bf16[144,384]{1,0:T(8,128)(2,1)S(1...) custom-call(s32[6]{0:T(128)S(1)} %stack.51.flags_ref, ...), custom_call_target="tpu_custom_call" | custom-call | tf_op jit(solution)/shard_map/weigh/pallas_call | solution.py:387
  147.4 5.5 %collective-permute-start.27 = (bf16[144,384]{1,0:T(8,128)(2,1)S(1)}, bf16[144,384]{1,0:T(8,128)(2,1)S(1)}, u32[]{:S(2)}, u32[]{:S(2)}) collective-permute-start(bf16[144,384]{1,0:T(8,128)(2,1)S(1)} %get-tuple-element.51), channel_id=1, source_target_pairs={{0,8},{2,10},{4,12},{6,14},{8,0},{10,2},{12,4},{14,6},{1,9},{3,11}... | collective-permute-start | bytes 331784 | tf_op jit(solution)/shard_map/ppermute | solution.py:412
  152.9 1.0 collective-permute-start.28
  153.9 1.1 collective-permute-start.29
  154.9 2.7 %collective-permute-start.30 = (bf16[144,384]{1,0:T(8,128)(2,1)S(1)}, bf16[144,384]{1,0:T(8,128)(2,1)S(1)}, u32[]{:S(2)}, u32[]{:S(2)}) collective-permute-start(bf16[144,384]{1,0:T(8,128)(2,1)S(1)} %get-tuple-element.54), channel_id=1, source_target_pairs={{0,14},{2,12},{4,10},{6,8},{8,6},{10,4},{12,2},{14,0},{1,15},{3,13... | collective-permute-start | bytes 331784 | tf_op jit(solution)/shard_map/ppermute | solution.py:412
  157.7 1.5 collective-permute-start.31
  159.2 7.0 %collective-permute-done.27.refs_0_ = bf16[144,384]{1,0:T(8,128)(2,1)S(1)} collective-permute-done((bf16[144,384]{1,0:T(8,128)(2,1)S(1)}, bf16[144,384]{1,0:T(8,128)(2,1)S(1)}, u32[]{:S(2)}, u32[]{:S(2)}) %collective-permute-start.27) | collective-permute-done | bytes 110624 | tf_op jit(solution)/shard_map/ppermute | solution.py:412
  166.2 3.3 %collective-permute-done.28.refs_1_ = bf16[144,384]{1,0:T(8,128)(2,1)S(1)} collective-permute-done((bf16[144,384]{1,0:T(8,128)(2,1)S(1)}, bf16[144,384]{1,0:T(8,128)(2,1)S(1)}, u32[]{:S(2)}, u32[]{:S(2)}) %collective-permute-start.28) | collective-permute-done | bytes 110624 | tf_op jit(solution)/shard_map/ppermute | solution.py:412
  169.5 1.4 collective-permute-done.32.refs_6_
  170.9 4.2 %collective-permute-done.33.refs_7_ = bf16[144,384]{1,0:T(8,128)(2,1)S(1)} collective-permute-done((bf16[144,384]{1,0:T(8,128)(2,1)S(1)}, bf16[144,384]{1,0:T(8,128)(2,1)S(1)}, u32[]{:S(2)}, u32[]{:S(2)}) %collective-permute-start.33) | collective-permute-done | bytes 110624 | tf_op jit(solution)/shard_map/ppermute | solution.py:412
  175.1 2.3 %combine.1 = bf16[128,1536]{1,0:T(8,128)(2,1)} custom-call(s32[6]{0:T(128)S(1)} %stack.51.flags_ref, s32[2,128]{1,0:T(2,128)S(1)} %bitcast.113, bf16[144,384]{1,0:T(8,128)(2,1)S(1)} %collective-permute-done.27.refs_0_, bf16[144,384]{1,0:T(8,128)(2,1)S(1)} %collective-permute-done.28.refs_1_, bf16[144,384]{1,0:T(8,128)(2,1)S(1)} %collective-permute-done.29.refs_2_, ...), custom_call_target="tpu_custom_call" | custom-call | tf_op jit(solution)/shard_map/combine/pallas_call | solution.py:387
  (64 shorter events, 6.2 us)
Async XLA Ops:
  0.0 55.0 %copy-start = (bf16[2048,384]{1,0:T(8,128)(2,1)S(1)}, bf16[2048,384]{1,0:T(8,128)(2,1)}, u32[]{:S(2)}) copy-start(bf16[2048,384]{1,0:T(8,128)(2,1)} %param.17) | copy-start | bytes 4718596
  0.0 8.1 %copy-start.10 = (bf16[128,1536]{1,0:T(8,128)(2,1)S(1)}, bf16[128,1536]{1,0:T(8,128)(2,1)}, u32[]{:S(2)}) copy-start(bf16[128,1536]{1,0:T(8,128)(2,1)} %param.15) | copy-start | bytes 1179652
  0.0 20.2 %copy-start.8 = (f32[128,2]{0,1:T(2,128)S(1)}, f32[128,2]{0,1:T(2,128)}, u32[]{:S(2)}) copy-start(f32[128,2]{0,1:T(2,128)} %param.20) | copy-start | bytes 3076
  0.0 20.2 %copy-start.7 = (s32[128,2]{0,1:T(2,128)S(1)}, s32[128,2]{0,1:T(2,128)}, u32[]{:S(2)}) copy-start(s32[128,2]{0,1:T(2,128)} %param.19) | copy-start | bytes 3076
  2.9 17.4 %all-to-all-start = ((bf16[4,512,128]{2,1,0:T(8,128)(2,1)}), bf16[4,512,128]{2,1,0:T(8,128)(2,1)S(1)}, u32[]{:S(2)}, u32[]{:S(2)}) async-start(bf16[4,512,128]{2,1,0:T(8,128)(2,1)} %states.1), calls=%async_computation | async-start | bytes 1048576 | tf_op jit(solution)/shard_map/all_to_all | solution.py:483
  8.1 12.3 %collective-permute-start.1 = (bf16[128,1536]{1,0:T(8,128)(2,1)S(1)}, bf16[128,1536]{1,0:T(8,128)(2,1)S(1)}, u32[]{:S(2)}, u32[]{:S(2)}) collective-permute-start(bf16[128,1536]{1,0:T(8,128)(2,1)S(1)} %copy-done.10), channel_id=1, source_target_pairs={{1,8},{3,10},{5,12},{7,14},{8,1},{10,3},{12,5},{14,7},{17,24},{19,... | collective-permute-start | bytes 1179656 | tf_op jit(solution)/shard_map/ppermute | solution.py:475
  20.3 8.1 %collective-permute-start = (bf16[528,128]{1,0:T(8,128)(2,1)S(1)}, bf16[528,128]{1,0:T(8,128)(2,1)S(1)}, u32[]{:S(2)}, u32[]{:S(2)}) collective-permute-start(bf16[528,128]{1,0:T(8,128)(2,1)S(1)} %totals.1.near_ref), channel_id=1, source_target_pairs={{0,8},{2,10},{4,12},{6,14},{8,0},{10,2},{12,4},{14,6},{1,9},{3,11}... | collective-permute-start | bytes 405512 | tf_op jit(solution)/shard_map/ppermute | solution.py:488
  29.1 1.0 copy-start.2
  30.1 16.5 %copy-start.6 = (f32[2048]{0:T(1024)S(1)}, f32[2048]{0:T(1024)}, u32[]{:S(2)}) copy-start(f32[2048]{0:T(1024)} %param.16) | copy-start | bytes 24580
  30.1 16.5 %all-to-all-start.1 = ((bf16[4,912,128]{2,1,0:T(8,128)(2,1)}), bf16[4,912,128]{2,1,0:T(8,128)(2,1)S(1)}, u32[]{:S(2)}, u32[]{:S(2)}) async-start(bf16[4,912,128]{2,1,0:T(8,128)(2,1)} %copy-done.2), calls=%async_computation.1 | async-start | bytes 1867776 | tf_op jit(solution)/shard_map/all_to_all | solution.py:497
  46.6 1.0 copy-start.3
  47.6 1.0 copy-start.4
  48.7 1.0 copy-start.5
  50.7 9.3 %collective-permute-start.4 = (bf16[64,2048]{1,0:T(8,128)(2,1)S(1)}, bf16[64,2048]{1,0:T(8,128)(2,1)S(1)}, u32[]{:S(2)}, u32[]{:S(2)}) collective-permute-start(bf16[64,2048]{1,0:T(8,128)(2,1)S(1)} %get-tuple-element.59), channel_id=1, source_target_pairs={{0,4},{4,8},{8,12},{12,14},{14,10},{10,6},{6,2},{2,0},{1,5},{5,9},... | collective-permute-start | bytes 786440 | tf_op jit(solution)/shard_map/ppermute | solution.py:443
  52.2 9.2 %collective-permute-start.5 = (bf16[64,2048]{1,0:T(8,128)(2,1)S(1)}, bf16[64,2048]{1,0:T(8,128)(2,1)S(1)}, u32[]{:S(2)}, u32[]{:S(2)}) collective-permute-start(bf16[64,2048]{1,0:T(8,128)(2,1)S(1)} %get-tuple-element.59), channel_id=1, source_target_pairs={{4,0},{8,4},{12,8},{14,12},{10,14},{6,10},{2,6},{0,2},{5,1},{9,5},... | collective-permute-start | bytes 786440 | tf_op jit(solution)/shard_map/ppermute | solution.py:446
  52.8 12.8 %collective-permute-start.2 = (bf16[64,2048]{1,0:T(8,128)(2,1)S(1)}, bf16[64,2048]{1,0:T(8,128)(2,1)S(1)}, u32[]{:S(2)}, u32[]{:S(2)}) collective-permute-start(bf16[64,2048]{1,0:T(8,128)(2,1)S(1)} %get-tuple-element.60), channel_id=1, source_target_pairs={{0,4},{4,8},{8,12},{12,14},{14,10},{10,6},{6,2},{2,0},{1,5},{5,9},... | collective-permute-start | bytes 786440 | tf_op jit(solution)/shard_map/ppermute | solution.py:443
  54.2 12.8 %collective-permute-start.3 = (bf16[64,2048]{1,0:T(8,128)(2,1)S(1)}, bf16[64,2048]{1,0:T(8,128)(2,1)S(1)}, u32[]{:S(2)}, u32[]{:S(2)}) collective-permute-start(bf16[64,2048]{1,0:T(8,128)(2,1)S(1)} %get-tuple-element.60), channel_id=1, source_target_pairs={{4,0},{8,4},{12,8},{14,12},{10,14},{6,10},{2,6},{0,2},{5,1},{9,5},... | collective-permute-start | bytes 786440 | tf_op jit(solution)/shard_map/ppermute | solution.py:446
  60.0 11.2 %collective-permute-start.8 = (bf16[64,2048]{1,0:T(8,128)(2,1)S(1)}, bf16[64,2048]{1,0:T(8,128)(2,1)S(1)}, u32[]{:S(2)}, u32[]{:S(2)}) collective-permute-start(bf16[64,2048]{1,0:T(8,128)(2,1)S(1)} %collective-permute-done.4), channel_id=1, source_target_pairs={{0,4},{4,8},{8,12},{12,14},{14,10},{10,6},{6,2},{2,0},{1,5},{5,9},... | collective-permute-start | bytes 786440 | tf_op jit(solution)/shard_map/ppermute | solution.py:443
  61.4 11.2 %collective-permute-start.9 = (bf16[64,2048]{1,0:T(8,128)(2,1)S(1)}, bf16[64,2048]{1,0:T(8,128)(2,1)S(1)}, u32[]{:S(2)}, u32[]{:S(2)}) collective-permute-start(bf16[64,2048]{1,0:T(8,128)(2,1)S(1)} %collective-permute-done.5), channel_id=1, source_target_pairs={{4,0},{8,4},{12,8},{14,12},{10,14},{6,10},{2,6},{0,2},{5,1},{9,5},... | collective-permute-start | bytes 786440 | tf_op jit(solution)/shard_map/ppermute | solution.py:446
  65.7 11.2 %collective-permute-start.6 = (bf16[64,2048]{1,0:T(8,128)(2,1)S(1)}, bf16[64,2048]{1,0:T(8,128)(2,1)S(1)}, u32[]{:S(2)}, u32[]{:S(2)}) collective-permute-start(bf16[64,2048]{1,0:T(8,128)(2,1)S(1)} %collective-permute-done.2), channel_id=1, source_target_pairs={{0,4},{4,8},{8,12},{12,14},{14,10},{10,6},{6,2},{2,0},{1,5},{5,9},... | collective-permute-start | bytes 786440 | tf_op jit(solution)/shard_map/ppermute | solution.py:443
  67.0 11.2 %collective-permute-start.7 = (bf16[64,2048]{1,0:T(8,128)(2,1)S(1)}, bf16[64,2048]{1,0:T(8,128)(2,1)S(1)}, u32[]{:S(2)}, u32[]{:S(2)}) collective-permute-start(bf16[64,2048]{1,0:T(8,128)(2,1)S(1)} %collective-permute-done.3), channel_id=1, source_target_pairs={{4,0},{8,4},{12,8},{14,12},{10,14},{6,10},{2,6},{0,2},{5,1},{9,5},... | collective-permute-start | bytes 786440 | tf_op jit(solution)/shard_map/ppermute | solution.py:446
  71.3 18.6 %collective-permute-start.12 = (bf16[64,2048]{1,0:T(8,128)(2,1)S(1)}, bf16[64,2048]{1,0:T(8,128)(2,1)S(1)}, u32[]{:S(2)}, u32[]{:S(2)}) collective-permute-start(bf16[64,2048]{1,0:T(8,128)(2,1)S(1)} %collective-permute-done.8), channel_id=1, source_target_pairs={{0,4},{4,8},{8,12},{12,14},{14,10},{10,6},{6,2},{2,0},{1,5},{5,9},... | collective-permute-start | bytes 786440 | tf_op jit(solution)/shard_map/ppermute | solution.py:443
  72.6 11.2 %collective-permute-start.13 = (bf16[64,2048]{1,0:T(8,128)(2,1)S(1)}, bf16[64,2048]{1,0:T(8,128)(2,1)S(1)}, u32[]{:S(2)}, u32[]{:S(2)}) collective-permute-start(bf16[64,2048]{1,0:T(8,128)(2,1)S(1)} %collective-permute-done.9), channel_id=1, source_target_pairs={{4,0},{8,4},{12,8},{14,12},{10,14},{6,10},{2,6},{0,2},{5,1},{9,5},... | collective-permute-start | bytes 786440 | tf_op jit(solution)/shard_map/ppermute | solution.py:446
  76.9 9.4 %collective-permute-start.10 = (bf16[64,2048]{1,0:T(8,128)(2,1)S(1)}, bf16[64,2048]{1,0:T(8,128)(2,1)S(1)}, u32[]{:S(2)}, u32[]{:S(2)}) collective-permute-start(bf16[64,2048]{1,0:T(8,128)(2,1)S(1)} %collective-permute-done.6), channel_id=1, source_target_pairs={{0,4},{4,8},{8,12},{12,14},{14,10},{10,6},{6,2},{2,0},{1,5},{5,9},... | collective-permute-start | bytes 786440 | tf_op jit(solution)/shard_map/ppermute | solution.py:443
  78.3 11.2 %collective-permute-start.11 = (bf16[64,2048]{1,0:T(8,128)(2,1)S(1)}, bf16[64,2048]{1,0:T(8,128)(2,1)S(1)}, u32[]{:S(2)}, u32[]{:S(2)}) collective-permute-start(bf16[64,2048]{1,0:T(8,128)(2,1)S(1)} %collective-permute-done.7), channel_id=1, source_target_pairs={{4,0},{8,4},{12,8},{14,12},{10,14},{6,10},{2,6},{0,2},{5,1},{9,5},... | collective-permute-start | bytes 786440 | tf_op jit(solution)/shard_map/ppermute | solution.py:446
  83.9 10.0 %collective-permute-start.15 = (bf16[64,2048]{1,0:T(8,128)(2,1)S(1)}, bf16[64,2048]{1,0:T(8,128)(2,1)S(1)}, u32[]{:S(2)}, u32[]{:S(2)}) collective-permute-start(bf16[64,2048]{1,0:T(8,128)(2,1)S(1)} %collective-permute-done.13), channel_id=1, source_target_pairs={{4,0},{8,4},{12,8},{14,12},{10,14},{6,10},{2,6},{0,2},{5,1},{9,5},... | collective-permute-start | bytes 786440 | tf_op jit(solution)/shard_map/ppermute | solution.py:446
  86.3 7.2 %collective-permute-start.14 = (bf16[64,2048]{1,0:T(8,128)(2,1)S(1)}, bf16[64,2048]{1,0:T(8,128)(2,1)S(1)}, u32[]{:S(2)}, u32[]{:S(2)}) collective-permute-start(bf16[64,2048]{1,0:T(8,128)(2,1)S(1)} %collective-permute-done.10), channel_id=1, source_target_pairs={{0,4},{4,8},{8,12},{12,14},{14,10},{10,6},{6,2},{2,0},{1,5},{5,9},... | collective-permute-start | bytes 786440 | tf_op jit(solution)/shard_map/ppermute | solution.py:443
  94.3 1.8 %collective-permute-start.16 = (bf16[4,128,384]{2,1,0:T(8,128)(2,1)S(1)}, bf16[4,128,384]{2,1,0:T(8,128)(2,1)S(1)}, u32[]{:S(2)}, u32[]{:S(2)}) collective-permute-start(bf16[4,128,384]{2,1,0:T(8,128)(2,1)S(1)} %dynamic-slice_convert_fusion), channel_id=1, source_target_pairs={{0,1},{1,0},{2,3},{3,2},{4,5},{5,4},{6,7},{7,6},{8,9},{9,8},{10,11... | collective-permute-start | bytes 1179656 | tf_op jit(solution)/shard_map/ppermute | solution.py:25
  97.6 8.4 %collective-permute-start.17 = (bf16[144,384]{1,0:T(8,128)(2,1)S(1)}, bf16[144,384]{1,0:T(8,128)(2,1)S(1)}, u32[]{:S(2)}, u32[]{:S(2)}) collective-permute-start(bf16[144,384]{1,0:T(8,128)(2,1)S(1)} %get-tuple-element.33), channel_id=1, source_target_pairs={{0,2},{2,0},{4,6},{6,4},{8,10},{10,8},{12,14},{14,12},{1,3},{3,1},... | collective-permute-start | bytes 331784 | tf_op jit(solution)/shard_map/ppermute | solution.py:412
  100.1 8.6 %collective-permute-start.18 = (bf16[144,384]{1,0:T(8,128)(2,1)S(1)}, bf16[144,384]{1,0:T(8,128)(2,1)S(1)}, u32[]{:S(2)}, u32[]{:S(2)}) collective-permute-start(bf16[144,384]{1,0:T(8,128)(2,1)S(1)} %get-tuple-element.34), channel_id=1, source_target_pairs={{0,4},{2,6},{4,0},{6,2},{8,12},{10,14},{12,8},{14,10},{1,5},{3,7},... | collective-permute-start | bytes 331784 | tf_op jit(solution)/shard_map/ppermute | solution.py:412
  101.8 15.1 %collective-permute-start.19 = (bf16[144,384]{1,0:T(8,128)(2,1)S(1)}, bf16[144,384]{1,0:T(8,128)(2,1)S(1)}, u32[]{:S(2)}, u32[]{:S(2)}) collective-permute-start(bf16[144,384]{1,0:T(8,128)(2,1)S(1)} %get-tuple-element.35), channel_id=1, source_target_pairs={{0,6},{2,4},{4,2},{6,0},{8,14},{10,12},{12,10},{14,8},{1,7},{3,5},... | collective-permute-start | bytes 331784 | tf_op jit(solution)/shard_map/ppermute | solution.py:412
  101.8 15.1 %collective-permute-start.20 = (bf16[144,384]{1,0:T(8,128)(2,1)S(1)}, bf16[144,384]{1,0:T(8,128)(2,1)S(1)}, u32[]{:S(2)}, u32[]{:S(2)}) collective-permute-start(bf16[144,384]{1,0:T(8,128)(2,1)S(1)} %get-tuple-element.36), channel_id=1, source_target_pairs={{0,8},{2,10},{4,12},{6,14},{8,0},{10,2},{12,4},{14,6},{1,9},{3,11}... | collective-permute-start | bytes 331784 | tf_op jit(solution)/shard_map/ppermute | solution.py:412
  104.7 16.4 %collective-permute-start.21 = (bf16[144,384]{1,0:T(8,128)(2,1)S(1)}, bf16[144,384]{1,0:T(8,128)(2,1)S(1)}, u32[]{:S(2)}, u32[]{:S(2)}) collective-permute-start(bf16[144,384]{1,0:T(8,128)(2,1)S(1)} %get-tuple-element.37), channel_id=1, source_target_pairs={{0,10},{2,8},{4,14},{6,12},{8,2},{10,0},{12,6},{14,4},{1,11},{3,9}... | collective-permute-start | bytes 331784 | tf_op jit(solution)/shard_map/ppermute | solution.py:412
  105.9 15.2 %collective-permute-start.22 = (bf16[144,384]{1,0:T(8,128)(2,1)S(1)}, bf16[144,384]{1,0:T(8,128)(2,1)S(1)}, u32[]{:S(2)}, u32[]{:S(2)}) collective-permute-start(bf16[144,384]{1,0:T(8,128)(2,1)S(1)} %get-tuple-element.38), channel_id=1, source_target_pairs={{0,12},{2,14},{4,8},{6,10},{8,4},{10,6},{12,0},{14,2},{1,13},{3,15... | collective-permute-start | bytes 331784 | tf_op jit(solution)/shard_map/ppermute | solution.py:412
  108.7 12.4 %collective-permute-start.23 = (bf16[144,384]{1,0:T(8,128)(2,1)S(1)}, bf16[144,384]{1,0:T(8,128)(2,1)S(1)}, u32[]{:S(2)}, u32[]{:S(2)}) collective-permute-start(bf16[144,384]{1,0:T(8,128)(2,1)S(1)} %get-tuple-element.39), channel_id=1, source_target_pairs={{0,14},{2,12},{4,10},{6,8},{8,6},{10,4},{12,2},{14,0},{1,15},{3,13... | collective-permute-start | bytes 331784 | tf_op jit(solution)/shard_map/ppermute | solution.py:412
  116.9 6.8 %copy-start.9 = (f32[3072]{0:T(1024)S(1)}, f32[3072]{0:T(1024)}, u32[]{:S(2)}) copy-start(f32[3072]{0:T(1024)} %param.18) | copy-start | bytes 36868
  121.2 1.9 %collective-permute-start.25 = (bf16[4,144,384]{2,1,0:T(8,128)(2,1)S(1)}, bf16[4,144,384]{2,1,0:T(8,128)(2,1)S(1)}, u32[]{:S(2)}, u32[]{:S(2)}) collective-permute-start(bf16[4,144,384]{2,1,0:T(8,128)(2,1)S(1)} %pad_maximum_fusion.1.near_own.c), channel_id=1, source_target_pairs={{0,1},{1,0},{2,3},{3,2},{4,5},{5,4},{6,7},{7,6},{8,9},{9,8},{10,11... | collective-permute-start | bytes 1327112 | tf_op jit(solution)/shard_map/ppermute | solution.py:25
  121.3 2.3 %collective-permute-start.24 = (bf16[4,144,384]{2,1,0:T(8,128)(2,1)S(1)}, bf16[4,144,384]{2,1,0:T(8,128)(2,1)S(1)}, u32[]{:S(2)}, u32[]{:S(2)}) collective-permute-start(bf16[4,144,384]{2,1,0:T(8,128)(2,1)S(1)} %pad_maximum_fusion.far_own.a), channel_id=1, source_target_pairs={{0,1},{1,0},{2,3},{3,2},{4,5},{5,4},{6,7},{7,6},{8,9},{9,8},{10,11... | collective-permute-start | bytes 1327112 | tf_op jit(solution)/shard_map/ppermute | solution.py:25
  143.1 2.5 %collective-permute-start.26 = (bf16[288,1536]{1,0:T(8,128)(2,1)S(1)}, bf16[288,1536]{1,0:T(8,128)(2,1)S(1)}, u32[]{:S(2)}, u32[]{:S(2)}) collective-permute-start(bf16[288,1536]{1,0:T(8,128)(2,1)S(1)} %get-tuple-element.50), channel_id=1, source_target_pairs={{0,1},{1,0},{2,3},{3,2},{4,5},{5,4},{6,7},{7,6},{8,9},{9,8},{10,11... | collective-permute-start | bytes 2654216 | tf_op jit(solution)/shard_map/ppermute | solution.py:25
  145.6 31.9 %copy-start.1 = (bf16[2048,384]{1,0:T(8,128)(2,1)S(1)}, bf16[2048,384]{1,0:T(8,128)(2,1)}, u32[]{:S(2)}) copy-start(bf16[2048,384]{1,0:T(8,128)(2,1)} %param.17) | copy-start | bytes 4718596
  147.4 18.8 %collective-permute-start.27 = (bf16[144,384]{1,0:T(8,128)(2,1)S(1)}, bf16[144,384]{1,0:T(8,128)(2,1)S(1)}, u32[]{:S(2)}, u32[]{:S(2)}) collective-permute-start(bf16[144,384]{1,0:T(8,128)(2,1)S(1)} %get-tuple-element.51), channel_id=1, source_target_pairs={{0,8},{2,10},{4,12},{6,14},{8,0},{10,2},{12,4},{14,6},{1,9},{3,11}... | collective-permute-start | bytes 331784 | tf_op jit(solution)/shard_map/ppermute | solution.py:412
  152.9 16.6 %collective-permute-start.28 = (bf16[144,384]{1,0:T(8,128)(2,1)S(1)}, bf16[144,384]{1,0:T(8,128)(2,1)S(1)}, u32[]{:S(2)}, u32[]{:S(2)}) collective-permute-start(bf16[144,384]{1,0:T(8,128)(2,1)S(1)} %get-tuple-element.52), channel_id=1, source_target_pairs={{0,10},{2,8},{4,14},{6,12},{8,2},{10,0},{12,6},{14,4},{1,11},{3,9}... | collective-permute-start | bytes 331784 | tf_op jit(solution)/shard_map/ppermute | solution.py:412
  153.9 15.6 %collective-permute-start.29 = (bf16[144,384]{1,0:T(8,128)(2,1)S(1)}, bf16[144,384]{1,0:T(8,128)(2,1)S(1)}, u32[]{:S(2)}, u32[]{:S(2)}) collective-permute-start(bf16[144,384]{1,0:T(8,128)(2,1)S(1)} %get-tuple-element.53), channel_id=1, source_target_pairs={{0,12},{2,14},{4,8},{6,10},{8,4},{10,6},{12,0},{14,2},{1,13},{3,15... | collective-permute-start | bytes 331784 | tf_op jit(solution)/shard_map/ppermute | solution.py:412
  154.9 14.6 %collective-permute-start.30 = (bf16[144,384]{1,0:T(8,128)(2,1)S(1)}, bf16[144,384]{1,0:T(8,128)(2,1)S(1)}, u32[]{:S(2)}, u32[]{:S(2)}) collective-permute-start(bf16[144,384]{1,0:T(8,128)(2,1)S(1)} %get-tuple-element.54), channel_id=1, source_target_pairs={{0,14},{2,12},{4,10},{6,8},{8,6},{10,4},{12,2},{14,0},{1,15},{3,13... | collective-permute-start | bytes 331784 | tf_op jit(solution)/shard_map/ppermute | solution.py:412
  157.7 11.9 %collective-permute-start.31 = (bf16[144,384]{1,0:T(8,128)(2,1)S(1)}, bf16[144,384]{1,0:T(8,128)(2,1)S(1)}, u32[]{:S(2)}, u32[]{:S(2)}) collective-permute-start(bf16[144,384]{1,0:T(8,128)(2,1)S(1)} %get-tuple-element.56), channel_id=1, source_target_pairs={{0,2},{2,0},{4,6},{6,4},{8,10},{10,8},{12,14},{14,12},{1,3},{3,1},... | collective-permute-start | bytes 331784 | tf_op jit(solution)/shard_map/ppermute | solution.py:412
  166.2 4.7 %collective-permute-start.32 = (bf16[144,384]{1,0:T(8,128)(2,1)S(1)}, bf16[144,384]{1,0:T(8,128)(2,1)S(1)}, u32[]{:S(2)}, u32[]{:S(2)}) collective-permute-start(bf16[144,384]{1,0:T(8,128)(2,1)S(1)} %get-tuple-element.57), channel_id=1, source_target_pairs={{0,4},{2,6},{4,0},{6,2},{8,12},{10,14},{12,8},{14,10},{1,5},{3,7},... | collective-permute-start | bytes 331784 | tf_op jit(solution)/shard_map/ppermute | solution.py:412
  169.5 5.6 %collective-permute-start.33 = (bf16[144,384]{1,0:T(8,128)(2,1)S(1)}, bf16[144,384]{1,0:T(8,128)(2,1)S(1)}, u32[]{:S(2)}, u32[]{:S(2)}) collective-permute-start(bf16[144,384]{1,0:T(8,128)(2,1)S(1)} %get-tuple-element.58), channel_id=1, source_target_pairs={{0,6},{2,4},{4,2},{6,0},{8,14},{10,12},{12,10},{14,8},{1,7},{3,5},... | collective-permute-start | bytes 331784 | tf_op jit(solution)/shard_map/ppermute | solution.py:412

commit v4 on v3

--- a/solution.py
+++ b/solution.py
@@ -113,20 +113,27 @@
     return jnp.concatenate(parts, axis=0)
 
 
-def attention_kernel(q_ref, k_ref, v_ref, before_ref, gain_ref, out_ref):
+def intra_kernel(q_ref, k_ref, v_ref, out_ref):
+    tok, all_lanes = q_ref.shape
+    row = lax.broadcasted_iota(jnp.int32, (tok, tok), 0)
+    column = lax.broadcasted_iota(jnp.int32, (tok, tok), 1)
+    causal = row >= column
+    for n in range(all_lanes // HD):
+        at = slice(n * HD, (n + 1) * HD)
+        scores = contract(q_ref[:, at], k_ref[:, at], (1, 1))
+        scores = jnp.where(causal, scores, 0.0).astype(BF)
+        out_ref[:, at] = dot(scores, v_ref[:, at])
+
+
+def attention_kernel(q_ref, intra_ref, before_ref, gain_ref, out_ref):
     tok, all_lanes = q_ref.shape
     owners = before_ref.shape[0]
     each = all_lanes // HD // owners
-    row = lax.broadcasted_iota(jnp.int32, (tok, tok), 0)
-    column = lax.broadcasted_iota(jnp.int32, (tok, tok), 1)
-    causal = row >= column
     for n in range(owners * each):
         at = slice(n * HD, (n + 1) * HD)
         state_at = slice(n % each * HD, (n % each + 1) * HD)
-        q = q_ref[:, at]
-        inter = dot(q, before_ref[n // each, state_at])
-        scores = jnp.where(causal, contract(q, k_ref[:, at], (1, 1)), 0.0).astype(BF)
-        attention = inter + dot(scores, v_ref[:, at])
+        inter = dot(q_ref[:, at], before_ref[n // each, state_at])
+        attention = inter + intra_ref[:, at]
         mean = jnp.mean(attention * attention, axis=-1, keepdims=True)
         normed = attention * lax.rsqrt(mean + EPS) * gain_ref[0:1, at]
         out_ref[:, at] = normed.astype(BF)
@@ -486,6 +493,8 @@
         routes_by_lane, route_weights.T, blocks,
     )
     far_sum = lax.ppermute(own_sum, "seq", [(s, (s + half) % seq_count) for s in chips])
+    intra = on_chip(intra_kernel, "intra", ((tok, heads * HD), F32), query, keys, values)
+    far_sum, intra = lax.optimization_barrier((far_sum, intra))
     sliced = jnp.where(me // half == core, resid, crossed)
     if cols % 128:
         sliced = sliced.reshape(tok, half, cols).transpose(1, 0, 2)
@@ -497,7 +506,7 @@
     sums = lax.all_to_all(sums, "seq", 0, 0, axis_index_groups=groups, tiled=True)
     normed = on_chip(
         attention_kernel, "attention", ((tok, heads * HD), BF),
-        query, keys, values, sums, attn_gain.reshape(1, heads * HD),
+        query, intra, sums, attn_gain.reshape(1, heads * HD),
     )
     acc = ring_project(normed, out_weight, seq_count, me)
     theirs = lax.dynamic_slice_in_dim(acc, (1 - core) * half, half, 0)

time: 178 us -> 177 us (level)
  waiting for transfers between devices: 80.5 us -> 74 us
  local copies, waits for them, and re-layouts: 4.4 us -> 7.65 us
  Pallas kernels: 34.6 us -> 36.7 us
    all_to_all x1, waiting for transfers between devices: 11.3 us -> 4.3 us  [per_device(): lax.all_to_all(states, 'seq', 0, 0, axis_index_groups=groups, tiled=True)]
    unnamed x22 -> x28, local copies, waits for them, and re-layouts: 4.12 us -> 7.37 us
    pallas_call x7 -> x8, Pallas kernels: 10.2 us -> 12.3 us  [on_chip(): pl.pallas_call(kernel, out_shape=out_shape, in_specs=[smem] * scalars + [...]
  transfers between devices with their start and end apart: 36 -> 36, of which waited for: 22 -> 22; matrix products, arithmetic and copies ran while one was open for 3% -> 3% of each run, Pallas kernels for 3% -> 4%
where the time goes in v4:
time: 177 us; the launch traced here: 176 us
  waiting for transfers between devices  74 us (42%)
  starting transfers between devices  51.2 us (29%)
  Pallas kernels  36.7 us (21%)
  local copies, waits for them, and re-layouts  7.65 us (4%)
  matrix products  5.83 us (3%)
    ppermute x14, starting transfers between devices, xor_shift(): lax.ppermute(x, 'seq', [(s, s ^ k) for s in range(lax.axis_size('seq'))])  25.9 us
    ppermute x14, waiting for transfers between devices, xor_shift(): lax.ppermute(x, 'seq', [(s, s ^ k) for s in range(lax.axis_size('seq'))])  20.4 us
    pallas_call x1, Pallas kernels, experts(): pl.pallas_call(moe_kernel, out_shape=(out, out), in_specs=[smem] + [vmem]...  19.4 us
    ppermute x7, waiting for transfers between devices, ring_project(): back[i] = lax.ppermute(back[i], 'seq', ahead)  17.9 us
    all_to_all x1, waiting for transfers between devices, per_device(): lax.all_to_all(sums, 'seq', 0, 0, axis_index_groups=groups, tiled=True)  12.3 us
    pallas_call x8, Pallas kernels, on_chip(): pl.pallas_call(kernel, out_shape=out_shape, in_specs=[smem] * scalars + [...  12.3 us
    ppermute x7, starting transfers between devices, ring_project(): back[i] = lax.ppermute(back[i], 'seq', ahead)  9.31 us
    ppermute x1, waiting for transfers between devices, per_device(): lax.ppermute(own_sum, 'seq', [(s, (s + half) % seq_count) for s in chips])  8.85 us
  transfers between devices with their start and end apart: 36, of which 22 were waited for; matrix products, arithmetic and copies ran while one was open for 3% of the time, Pallas kernels for 4%

profile of v4, /device:TPU:0, one launch (start us, length us, event | category | flops | bytes accessed | tf_op | source)
XLA Modules:
  0.0 176.3 jit_solution(7000042636925127886)
XLA Ops:
  0.0 2.8 %states.1 = bf16[4,512,128]{2,1,0:T(8,128)(2,1)} custom-call(bf16[128,2048]{1,0:T(8,128)(2,1)} %k_ref.1, bf16[128,2048]{1,0:T(8,128)(2,1)} %v_ref.1), custom_call_target="tpu_custom_call" | custom-call | tf_op jit(solution)/shard_map/states/pallas_call | solution.py:394
  2.9 5.3 %all-to-all-start = ((bf16[4,512,128]{2,1,0:T(8,128)(2,1)}), bf16[4,512,128]{2,1,0:T(8,128)(2,1)S(1)}, u32[]{:S(2)}, u32[]{:S(2)}) async-start(bf16[4,512,128]{2,1,0:T(8,128)(2,1)} %states.1), calls=%async_computation | async-start | bytes 1048576 | tf_op jit(solution)/shard_map/all_to_all | solution.py:490
  8.1 0.8 collective-permute-start.1
  9.0 1.0 copy-done.5
  10.0 1.0 copy-done.6
  11.1 1.0 copy-done.7
  12.1 2.6 %intra.1.intra_ref = f32[128,2048]{1,0:T(8,128)S(1)} custom-call(bf16[128,2048]{1,0:T(8,128)(2,1)S(1)} %copy-done.7, bf16[128,2048]{1,0:T(8,128)(2,1)S(1)} %copy-done.5, bf16[128,2048]{1,0:T(8,128)(2,1)S(1)} %copy-done.6), custom_call_target="tpu_custom_call" | custom-call | tf_op jit(solution)/shard_map/intra/pallas_call | solution.py:394
  14.7 1.0 copy-done.2
  15.8 4.3 %all-to-all-done.x_ref = bf16[4,512,128]{2,1,0:T(8,128)(2,1)S(1)} async-done(((bf16[4,512,128]{2,1,0:T(8,128)(2,1)}), bf16[4,512,128]{2,1,0:T(8,128)(2,1)S(1)}, u32[]{:S(2)}, u32[]{:S(2)}) %all-to-all-start) | async-done | bytes 524320 | tf_op jit(solution)/shard_map/all_to_all | solution.py:490
  20.3 8.8 %collective-permute-done.far_ref = bf16[528,128]{1,0:T(8,128)(2,1)S(1)} collective-permute-done((bf16[528,128]{1,0:T(8,128)(2,1)S(1)}, bf16[528,128]{1,0:T(8,128)(2,1)S(1)}, u32[]{:S(2)}, u32[]{:S(2)}) %collective-permute-start) | collective-permute-done | bytes 135200 | tf_op jit(solution)/shard_map/ppermute | solution.py:495
  29.1 0.7 sums.1
  29.8 1.0 copy-done.4
  30.8 3.6 %all-to-all-start.1 = ((bf16[4,912,128]{2,1,0:T(8,128)(2,1)}), bf16[4,912,128]{2,1,0:T(8,128)(2,1)S(1)}, u32[]{:S(2)}, u32[]{:S(2)}) async-start(bf16[4,912,128]{2,1,0:T(8,128)(2,1)} %copy-done.4), calls=%async_computation.1 | async-start | bytes 1867776 | tf_op jit(solution)/shard_map/all_to_all | solution.py:506
  34.7 12.3 %all-to-all-done.1.before_ref.resid_ref.sums_ref = bf16[4,912,128]{2,1,0:T(8,128)(2,1)S(1)} async-done(((bf16[4,912,128]{2,1,0:T(8,128)(2,1)}), bf16[4,912,128]{2,1,0:T(8,128)(2,1)S(1)}, u32[]{:S(2)}, u32[]{:S(2)}) %all-to-all-start.1) | async-done | bytes 933920 | tf_op jit(solution)/shard_map/all_to_all | solution.py:506
  47.0 1.2 copy-done.3
  48.2 1.0 copy-done.8
  49.8 1.3 collective-permute-start.4
  51.1 0.8 collective-permute-start.5
  51.9 1.3 collective-permute-start.2
  53.2 0.8 collective-permute-start.3
  54.7 4.3 %collective-permute-done.4 = bf16[64,2048]{1,0:T(8,128)(2,1)S(1)} collective-permute-done((bf16[64,2048]{1,0:T(8,128)(2,1)S(1)}, bf16[64,2048]{1,0:T(8,128)(2,1)S(1)}, u32[]{:S(2)}, u32[]{:S(2)}) %collective-permute-start.4) | collective-permute-done | bytes 262176 | tf_op jit(solution)/shard_map/ppermute | solution.py:450
  59.1 1.2 collective-permute-start.8
  60.4 0.8 collective-permute-start.9
  61.1 3.6 %collective-permute-done.2 = bf16[64,2048]{1,0:T(8,128)(2,1)S(1)} collective-permute-done((bf16[64,2048]{1,0:T(8,128)(2,1)S(1)}, bf16[64,2048]{1,0:T(8,128)(2,1)S(1)}, u32[]{:S(2)}, u32[]{:S(2)}) %collective-permute-start.2) | collective-permute-done | bytes 262176 | tf_op jit(solution)/shard_map/ppermute | solution.py:450
  64.7 1.2 collective-permute-start.6
  66.0 0.8 collective-permute-start.7
  68.2 2.1 %collective-permute-done.8 = bf16[64,2048]{1,0:T(8,128)(2,1)S(1)} collective-permute-done((bf16[64,2048]{1,0:T(8,128)(2,1)S(1)}, bf16[64,2048]{1,0:T(8,128)(2,1)S(1)}, u32[]{:S(2)}, u32[]{:S(2)}) %collective-permute-start.8) | collective-permute-done | bytes 262176 | tf_op jit(solution)/shard_map/ppermute | solution.py:450
  70.3 1.2 collective-permute-start.12
  71.6 0.8 collective-permute-start.13
  72.4 3.6 %collective-permute-done.6 = bf16[64,2048]{1,0:T(8,128)(2,1)S(1)} collective-permute-done((bf16[64,2048]{1,0:T(8,128)(2,1)S(1)}, bf16[64,2048]{1,0:T(8,128)(2,1)S(1)}, u32[]{:S(2)}, u32[]{:S(2)}) %collective-permute-start.6) | collective-permute-done | bytes 262176 | tf_op jit(solution)/shard_map/ppermute | solution.py:450
  75.9 1.2 collective-permute-start.10
  77.2 0.8 collective-permute-start.11
  79.4 3.4 %collective-permute-done.13 = bf16[64,2048]{1,0:T(8,128)(2,1)S(1)} collective-permute-done((bf16[64,2048]{1,0:T(8,128)(2,1)S(1)}, bf16[64,2048]{1,0:T(8,128)(2,1)S(1)}, u32[]{:S(2)}, u32[]{:S(2)}) %collective-permute-start.13) | collective-permute-done | bytes 262176 | tf_op jit(solution)/shard_map/ppermute | solution.py:453
  82.8 0.8 collective-permute-start.15
  83.6 1.8 %collective-permute-done.10 = bf16[64,2048]{1,0:T(8,128)(2,1)S(1)} collective-permute-done((bf16[64,2048]{1,0:T(8,128)(2,1)S(1)}, bf16[64,2048]{1,0:T(8,128)(2,1)S(1)}, u32[]{:S(2)}, u32[]{:S(2)}) %collective-permute-start.10) | collective-permute-done | bytes 262176 | tf_op jit(solution)/shard_map/ppermute | solution.py:450
  85.4 1.8 %collective-permute-start.14 = (bf16[64,2048]{1,0:T(8,128)(2,1)S(1)}, bf16[64,2048]{1,0:T(8,128)(2,1)S(1)}, u32[]{:S(2)}, u32[]{:S(2)}) collective-permute-start(bf16[64,2048]{1,0:T(8,128)(2,1)S(1)} %collective-permute-done.10), channel_id=1, source_target_pairs={{0,4},{4,8},{8,12},{12,14},{14,10},{10,6},{6,2},{2,0},{1,5},{5,9},... | collective-permute-start | bytes 786440 | tf_op jit(solution)/shard_map/ppermute | solution.py:450
  87.6 0.8 collective-permute-done.11
  89.6 2.4 %collective-permute-done.14 = bf16[64,2048]{1,0:T(8,128)(2,1)S(1)} collective-permute-done((bf16[64,2048]{1,0:T(8,128)(2,1)S(1)}, bf16[64,2048]{1,0:T(8,128)(2,1)S(1)}, u32[]{:S(2)}, u32[]{:S(2)}) %collective-permute-start.14) | collective-permute-done | bytes 262176 | tf_op jit(solution)/shard_map/ppermute | solution.py:450
  93.1 1.7 collective-permute-done.16.other_ref
  94.8 1.5 dispatch.1
  96.3 2.4 %collective-permute-start.17 = (bf16[144,384]{1,0:T(8,128)(2,1)S(1)}, bf16[144,384]{1,0:T(8,128)(2,1)S(1)}, u32[]{:S(2)}, u32[]{:S(2)}) collective-permute-start(bf16[144,384]{1,0:T(8,128)(2,1)S(1)} %get-tuple-element.37), channel_id=1, source_target_pairs={{0,2},{2,0},{4,6},{6,4},{8,10},{10,8},{12,14},{14,12},{1,3},{3,1},... | collective-permute-start | bytes 331784 | tf_op jit(solution)/shard_map/ppermute | solution.py:419
  98.7 1.7 collective-permute-start.18
  100.4 2.9 %collective-permute-start.20 = (bf16[144,384]{1,0:T(8,128)(2,1)S(1)}, bf16[144,384]{1,0:T(8,128)(2,1)S(1)}, u32[]{:S(2)}, u32[]{:S(2)}) collective-permute-start(bf16[144,384]{1,0:T(8,128)(2,1)S(1)} %get-tuple-element.40), channel_id=1, source_target_pairs={{0,8},{2,10},{4,12},{6,14},{8,0},{10,2},{12,4},{14,6},{1,9},{3,11}... | collective-permute-start | bytes 331784 | tf_op jit(solution)/shard_map/ppermute | solution.py:419
  103.3 1.2 collective-permute-start.21
  104.5 2.6 %collective-permute-start.22 = (bf16[144,384]{1,0:T(8,128)(2,1)S(1)}, bf16[144,384]{1,0:T(8,128)(2,1)S(1)}, u32[]{:S(2)}, u32[]{:S(2)}) collective-permute-start(bf16[144,384]{1,0:T(8,128)(2,1)S(1)} %get-tuple-element.42), channel_id=1, source_target_pairs={{0,12},{2,14},{4,8},{6,10},{8,4},{10,6},{12,0},{14,2},{1,13},{3,15... | collective-permute-start | bytes 331784 | tf_op jit(solution)/shard_map/ppermute | solution.py:419
  107.5 3.1 %collective-permute-start.23 = (bf16[144,384]{1,0:T(8,128)(2,1)S(1)}, bf16[144,384]{1,0:T(8,128)(2,1)S(1)}, u32[]{:S(2)}, u32[]{:S(2)}) collective-permute-start(bf16[144,384]{1,0:T(8,128)(2,1)S(1)} %get-tuple-element.43), channel_id=1, source_target_pairs={{0,14},{2,12},{4,10},{6,8},{8,6},{10,4},{12,2},{14,0},{1,15},{3,13... | collective-permute-start | bytes 331784 | tf_op jit(solution)/shard_map/ppermute | solution.py:419
  110.6 5.0 %load_gate.1.gate_ref = bf16[3072,2304]{1,0:T(8,128)(2,1)S(1)} custom-call(bf16[3072,2304]{1,0:T(8,128)(2,1)} %source.1), custom_call_target="tpu_custom_call" | custom-call | bytes 14155776 | tf_op jit(solution)/shard_map/load_gate/pallas_call | solution.py:406
  115.6 4.0 %collective-permute-done.21 = bf16[144,384]{1,0:T(8,128)(2,1)S(1)} collective-permute-done((bf16[144,384]{1,0:T(8,128)(2,1)S(1)}, bf16[144,384]{1,0:T(8,128)(2,1)S(1)}, u32[]{:S(2)}, u32[]{:S(2)}) %collective-permute-start.21) | collective-permute-done | bytes 110624 | tf_op jit(solution)/shard_map/ppermute | solution.py:419
  119.9 0.6 collective-permute-start.24
  120.5 1.1 collective-permute-done.25.near_other.d
  121.6 0.6 collective-permute-done.24.far_other.b
  122.2 19.4 %experts.1 = (bf16[288,1536]{1,0:T(8,128)(2,1)S(1)}, bf16[288,1536]{1,0:T(8,128)(2,1)S(1)}) custom-call(s32[9]{0:T(128)S(1)} %pad_add_fusion.info_ref, bf16[4,144,384]{2,1,0:T(8,128)(2,1)S(1)} %pad_maximum_fusion.far_own.a, bf16[4,144,384]{2,1,0:T(8,128)(2,1)S(1)} %collective-permute-done.24.far_other.b, ...), custom_call_target="tpu_custom_call" | custom-call | flops 12230590464 | bytes 42467328 | tf_op jit(solution)/shard_map/experts/pallas_call | solution.py:364
  141.8 2.3 %collective-permute-done.26.theirs_ref = bf16[288,1536]{1,0:T(8,128)(2,1)S(1)} collective-permute-done((bf16[288,1536]{1,0:T(8,128)(2,1)S(1)}, bf16[288,1536]{1,0:T(8,128)(2,1)S(1)}, u32[]{:S(2)}, u32[]{:S(2)}) %collective-permute-start.26) | collective-permute-done | bytes 884768 | tf_op jit(solution)/shard_map/ppermute | solution.py:25
  144.1 1.8 %weigh.1 = (bf16[144,384]{1,0:T(8,128)(2,1)S(1)}, bf16[144,384]{1,0:T(8,128)(2,1)S(1)}, bf16[144,384]{1,0:T(8,128)(2,1)S(1)}, bf16[144,384]{1,0:T(8,128)(2,1)S(1...) custom-call(s32[6]{0:T(128)S(1)} %stack.51.flags_ref, ...), custom_call_target="tpu_custom_call" | custom-call | tf_op jit(solution)/shard_map/weigh/pallas_call | solution.py:394
  145.9 5.6 %collective-permute-start.27 = (bf16[144,384]{1,0:T(8,128)(2,1)S(1)}, bf16[144,384]{1,0:T(8,128)(2,1)S(1)}, u32[]{:S(2)}, u32[]{:S(2)}) collective-permute-start(bf16[144,384]{1,0:T(8,128)(2,1)S(1)} %get-tuple-element.55), channel_id=1, source_target_pairs={{0,8},{2,10},{4,12},{6,14},{8,0},{10,2},{12,4},{14,6},{1,9},{3,11}... | collective-permute-start | bytes 331784 | tf_op jit(solution)/shard_map/ppermute | solution.py:419
  151.5 1.2 collective-permute-start.28
  152.6 0.9 collective-permute-start.29
  153.5 2.9 %collective-permute-start.30 = (bf16[144,384]{1,0:T(8,128)(2,1)S(1)}, bf16[144,384]{1,0:T(8,128)(2,1)S(1)}, u32[]{:S(2)}, u32[]{:S(2)}) collective-permute-start(bf16[144,384]{1,0:T(8,128)(2,1)S(1)} %get-tuple-element.58), channel_id=1, source_target_pairs={{0,14},{2,12},{4,10},{6,8},{8,6},{10,4},{12,2},{14,0},{1,15},{3,13... | collective-permute-start | bytes 331784 | tf_op jit(solution)/shard_map/ppermute | solution.py:419
  156.4 1.5 collective-permute-start.31
  157.9 6.9 %collective-permute-done.27.refs_0_ = bf16[144,384]{1,0:T(8,128)(2,1)S(1)} collective-permute-done((bf16[144,384]{1,0:T(8,128)(2,1)S(1)}, bf16[144,384]{1,0:T(8,128)(2,1)S(1)}, u32[]{:S(2)}, u32[]{:S(2)}) %collective-permute-start.27) | collective-permute-done | bytes 110624 | tf_op jit(solution)/shard_map/ppermute | solution.py:419
  164.8 3.4 %collective-permute-done.28.refs_1_ = bf16[144,384]{1,0:T(8,128)(2,1)S(1)} collective-permute-done((bf16[144,384]{1,0:T(8,128)(2,1)S(1)}, bf16[144,384]{1,0:T(8,128)(2,1)S(1)}, u32[]{:S(2)}, u32[]{:S(2)}) %collective-permute-start.28) | collective-permute-done | bytes 110624 | tf_op jit(solution)/shard_map/ppermute | solution.py:419
  168.3 1.3 collective-permute-done.32.refs_6_
  169.6 4.3 %collective-permute-done.33.refs_7_ = bf16[144,384]{1,0:T(8,128)(2,1)S(1)} collective-permute-done((bf16[144,384]{1,0:T(8,128)(2,1)S(1)}, bf16[144,384]{1,0:T(8,128)(2,1)S(1)}, u32[]{:S(2)}, u32[]{:S(2)}) %collective-permute-start.33) | collective-permute-done | bytes 110624 | tf_op jit(solution)/shard_map/ppermute | solution.py:419
  173.9 2.3 %combine.1 = bf16[128,1536]{1,0:T(8,128)(2,1)} custom-call(s32[6]{0:T(128)S(1)} %stack.51.flags_ref, s32[2,128]{1,0:T(2,128)S(1)} %bitcast.113, bf16[144,384]{1,0:T(8,128)(2,1)S(1)} %collective-permute-done.27.refs_0_, bf16[144,384]{1,0:T(8,128)(2,1)S(1)} %collective-permute-done.28.refs_1_, bf16[144,384]{1,0:T(8,128)(2,1)S(1)} %collective-permute-done.29.refs_2_, ...), custom_call_target="tpu_custom_call" | custom-call | tf_op jit(solution)/shard_map/combine/pallas_call | solution.py:394
  (71 shorter events, 8.2 us)
Async XLA Ops:
  0.0 54.0 %copy-start = (bf16[2048,384]{1,0:T(8,128)(2,1)S(1)}, bf16[2048,384]{1,0:T(8,128)(2,1)}, u32[]{:S(2)}) copy-start(bf16[2048,384]{1,0:T(8,128)(2,1)} %param.17) | copy-start | bytes 4718596
  0.0 8.1 %copy-start.13 = (bf16[128,1536]{1,0:T(8,128)(2,1)S(1)}, bf16[128,1536]{1,0:T(8,128)(2,1)}, u32[]{:S(2)}) copy-start(bf16[128,1536]{1,0:T(8,128)(2,1)} %param.15) | copy-start | bytes 1179652
  2.9 17.2 %all-to-all-start = ((bf16[4,512,128]{2,1,0:T(8,128)(2,1)}), bf16[4,512,128]{2,1,0:T(8,128)(2,1)S(1)}, u32[]{:S(2)}, u32[]{:S(2)}) async-start(bf16[4,512,128]{2,1,0:T(8,128)(2,1)} %states.1), calls=%async_computation | async-start | bytes 1048576 | tf_op jit(solution)/shard_map/all_to_all | solution.py:490
  8.1 11.9 %copy-start.10 = (s32[128,2]{0,1:T(2,128)S(1)}, s32[128,2]{0,1:T(2,128)}, u32[]{:S(2)}) copy-start(s32[128,2]{0,1:T(2,128)} %param.19) | copy-start | bytes 3076
  8.1 11.9 %copy-start.11 = (f32[128,2]{0,1:T(2,128)S(1)}, f32[128,2]{0,1:T(2,128)}, u32[]{:S(2)}) copy-start(f32[128,2]{0,1:T(2,128)} %param.20) | copy-start | bytes 3076
  8.1 12.1 %collective-permute-start.1 = (bf16[128,1536]{1,0:T(8,128)(2,1)S(1)}, bf16[128,1536]{1,0:T(8,128)(2,1)S(1)}, u32[]{:S(2)}, u32[]{:S(2)}) collective-permute-start(bf16[128,1536]{1,0:T(8,128)(2,1)S(1)} %copy-done.13), channel_id=1, source_target_pairs={{1,8},{3,10},{5,12},{7,14},{8,1},{10,3},{12,5},{14,7},{17,24},{19,... | collective-permute-start | bytes 1179656 | tf_op jit(solution)/shard_map/ppermute | solution.py:482
  9.0 1.0 copy-start.5
  10.0 1.0 copy-start.6
  11.1 1.0 copy-start.7
  14.7 1.0 copy-start.2
  20.2 9.0 %collective-permute-start = (bf16[528,128]{1,0:T(8,128)(2,1)S(1)}, bf16[528,128]{1,0:T(8,128)(2,1)S(1)}, u32[]{:S(2)}, u32[]{:S(2)}) collective-permute-start(bf16[528,128]{1,0:T(8,128)(2,1)S(1)} %totals.1.near_ref), channel_id=1, source_target_pairs={{0,8},{2,10},{4,12},{6,14},{8,0},{10,2},{12,4},{14,6},{1,9},{3,11}... | collective-permute-start | bytes 405512 | tf_op jit(solution)/shard_map/ppermute | solution.py:495
  29.8 1.0 copy-start.4
  30.8 16.2 %copy-start.9 = (f32[2048]{0:T(1024)S(1)}, f32[2048]{0:T(1024)}, u32[]{:S(2)}) copy-start(f32[2048]{0:T(1024)} %param.16) | copy-start | bytes 24580
  30.8 16.2 %all-to-all-start.1 = ((bf16[4,912,128]{2,1,0:T(8,128)(2,1)}), bf16[4,912,128]{2,1,0:T(8,128)(2,1)S(1)}, u32[]{:S(2)}, u32[]{:S(2)}) async-start(bf16[4,912,128]{2,1,0:T(8,128)(2,1)} %copy-done.4), calls=%async_computation.1 | async-start | bytes 1867776 | tf_op jit(solution)/shard_map/all_to_all | solution.py:506
  47.0 1.2 copy-start.3
  48.2 1.0 copy-start.8
  49.8 9.3 %collective-permute-start.4 = (bf16[64,2048]{1,0:T(8,128)(2,1)S(1)}, bf16[64,2048]{1,0:T(8,128)(2,1)S(1)}, u32[]{:S(2)}, u32[]{:S(2)}) collective-permute-start(bf16[64,2048]{1,0:T(8,128)(2,1)S(1)} %get-tuple-element.63), channel_id=1, source_target_pairs={{0,4},{4,8},{8,12},{12,14},{14,10},{10,6},{6,2},{2,0},{1,5},{5,9},... | collective-permute-start | bytes 786440 | tf_op jit(solution)/shard_map/ppermute | solution.py:450
  51.1 9.2 %collective-permute-start.5 = (bf16[64,2048]{1,0:T(8,128)(2,1)S(1)}, bf16[64,2048]{1,0:T(8,128)(2,1)S(1)}, u32[]{:S(2)}, u32[]{:S(2)}) collective-permute-start(bf16[64,2048]{1,0:T(8,128)(2,1)S(1)} %get-tuple-element.63), channel_id=1, source_target_pairs={{4,0},{8,4},{12,8},{14,12},{10,14},{6,10},{2,6},{0,2},{5,1},{9,5},... | collective-permute-start | bytes 786440 | tf_op jit(solution)/shard_map/ppermute | solution.py:453
  51.9 12.8 %collective-permute-start.2 = (bf16[64,2048]{1,0:T(8,128)(2,1)S(1)}, bf16[64,2048]{1,0:T(8,128)(2,1)S(1)}, u32[]{:S(2)}, u32[]{:S(2)}) collective-permute-start(bf16[64,2048]{1,0:T(8,128)(2,1)S(1)} %get-tuple-element.64), channel_id=1, source_target_pairs={{0,4},{4,8},{8,12},{12,14},{14,10},{10,6},{6,2},{2,0},{1,5},{5,9},... | collective-permute-start | bytes 786440 | tf_op jit(solution)/shard_map/ppermute | solution.py:450
  53.2 12.8 %collective-permute-start.3 = (bf16[64,2048]{1,0:T(8,128)(2,1)S(1)}, bf16[64,2048]{1,0:T(8,128)(2,1)S(1)}, u32[]{:S(2)}, u32[]{:S(2)}) collective-permute-start(bf16[64,2048]{1,0:T(8,128)(2,1)S(1)} %get-tuple-element.64), channel_id=1, source_target_pairs={{4,0},{8,4},{12,8},{14,12},{10,14},{6,10},{2,6},{0,2},{5,1},{9,5},... | collective-permute-start | bytes 786440 | tf_op jit(solution)/shard_map/ppermute | solution.py:453
  59.1 11.2 %collective-permute-start.8 = (bf16[64,2048]{1,0:T(8,128)(2,1)S(1)}, bf16[64,2048]{1,0:T(8,128)(2,1)S(1)}, u32[]{:S(2)}, u32[]{:S(2)}) collective-permute-start(bf16[64,2048]{1,0:T(8,128)(2,1)S(1)} %collective-permute-done.4), channel_id=1, source_target_pairs={{0,4},{4,8},{8,12},{12,14},{14,10},{10,6},{6,2},{2,0},{1,5},{5,9},... | collective-permute-start | bytes 786440 | tf_op jit(solution)/shard_map/ppermute | solution.py:450
  60.4 11.2 %collective-permute-start.9 = (bf16[64,2048]{1,0:T(8,128)(2,1)S(1)}, bf16[64,2048]{1,0:T(8,128)(2,1)S(1)}, u32[]{:S(2)}, u32[]{:S(2)}) collective-permute-start(bf16[64,2048]{1,0:T(8,128)(2,1)S(1)} %collective-permute-done.5), channel_id=1, source_target_pairs={{4,0},{8,4},{12,8},{14,12},{10,14},{6,10},{2,6},{0,2},{5,1},{9,5},... | collective-permute-start | bytes 786440 | tf_op jit(solution)/shard_map/ppermute | solution.py:453
  64.7 11.2 %collective-permute-start.6 = (bf16[64,2048]{1,0:T(8,128)(2,1)S(1)}, bf16[64,2048]{1,0:T(8,128)(2,1)S(1)}, u32[]{:S(2)}, u32[]{:S(2)}) collective-permute-start(bf16[64,2048]{1,0:T(8,128)(2,1)S(1)} %collective-permute-done.2), channel_id=1, source_target_pairs={{0,4},{4,8},{8,12},{12,14},{14,10},{10,6},{6,2},{2,0},{1,5},{5,9},... | collective-permute-start | bytes 786440 | tf_op jit(solution)/shard_map/ppermute | solution.py:450
  66.0 11.2 %collective-permute-start.7 = (bf16[64,2048]{1,0:T(8,128)(2,1)S(1)}, bf16[64,2048]{1,0:T(8,128)(2,1)S(1)}, u32[]{:S(2)}, u32[]{:S(2)}) collective-permute-start(bf16[64,2048]{1,0:T(8,128)(2,1)S(1)} %collective-permute-done.3), channel_id=1, source_target_pairs={{4,0},{8,4},{12,8},{14,12},{10,14},{6,10},{2,6},{0,2},{5,1},{9,5},... | collective-permute-start | bytes 786440 | tf_op jit(solution)/shard_map/ppermute | solution.py:453
  70.3 18.5 %collective-permute-start.12 = (bf16[64,2048]{1,0:T(8,128)(2,1)S(1)}, bf16[64,2048]{1,0:T(8,128)(2,1)S(1)}, u32[]{:S(2)}, u32[]{:S(2)}) collective-permute-start(bf16[64,2048]{1,0:T(8,128)(2,1)S(1)} %collective-permute-done.8), channel_id=1, source_target_pairs={{0,4},{4,8},{8,12},{12,14},{14,10},{10,6},{6,2},{2,0},{1,5},{5,9},... | collective-permute-start | bytes 786440 | tf_op jit(solution)/shard_map/ppermute | solution.py:450
  71.6 11.2 %collective-permute-start.13 = (bf16[64,2048]{1,0:T(8,128)(2,1)S(1)}, bf16[64,2048]{1,0:T(8,128)(2,1)S(1)}, u32[]{:S(2)}, u32[]{:S(2)}) collective-permute-start(bf16[64,2048]{1,0:T(8,128)(2,1)S(1)} %collective-permute-done.9), channel_id=1, source_target_pairs={{4,0},{8,4},{12,8},{14,12},{10,14},{6,10},{2,6},{0,2},{5,1},{9,5},... | collective-permute-start | bytes 786440 | tf_op jit(solution)/shard_map/ppermute | solution.py:453
  75.9 9.5 %collective-permute-start.10 = (bf16[64,2048]{1,0:T(8,128)(2,1)S(1)}, bf16[64,2048]{1,0:T(8,128)(2,1)S(1)}, u32[]{:S(2)}, u32[]{:S(2)}) collective-permute-start(bf16[64,2048]{1,0:T(8,128)(2,1)S(1)} %collective-permute-done.6), channel_id=1, source_target_pairs={{0,4},{4,8},{8,12},{12,14},{14,10},{10,6},{6,2},{2,0},{1,5},{5,9},... | collective-permute-start | bytes 786440 | tf_op jit(solution)/shard_map/ppermute | solution.py:450
  77.2 11.2 %collective-permute-start.11 = (bf16[64,2048]{1,0:T(8,128)(2,1)S(1)}, bf16[64,2048]{1,0:T(8,128)(2,1)S(1)}, u32[]{:S(2)}, u32[]{:S(2)}) collective-permute-start(bf16[64,2048]{1,0:T(8,128)(2,1)S(1)} %collective-permute-done.7), channel_id=1, source_target_pairs={{4,0},{8,4},{12,8},{14,12},{10,14},{6,10},{2,6},{0,2},{5,1},{9,5},... | collective-permute-start | bytes 786440 | tf_op jit(solution)/shard_map/ppermute | solution.py:453
  82.8 9.8 %collective-permute-start.15 = (bf16[64,2048]{1,0:T(8,128)(2,1)S(1)}, bf16[64,2048]{1,0:T(8,128)(2,1)S(1)}, u32[]{:S(2)}, u32[]{:S(2)}) collective-permute-start(bf16[64,2048]{1,0:T(8,128)(2,1)S(1)} %collective-permute-done.13), channel_id=1, source_target_pairs={{4,0},{8,4},{12,8},{14,12},{10,14},{6,10},{2,6},{0,2},{5,1},{9,5},... | collective-permute-start | bytes 786440 | tf_op jit(solution)/shard_map/ppermute | solution.py:453
  85.4 6.6 %collective-permute-start.14 = (bf16[64,2048]{1,0:T(8,128)(2,1)S(1)}, bf16[64,2048]{1,0:T(8,128)(2,1)S(1)}, u32[]{:S(2)}, u32[]{:S(2)}) collective-permute-start(bf16[64,2048]{1,0:T(8,128)(2,1)S(1)} %collective-permute-done.10), channel_id=1, source_target_pairs={{0,4},{4,8},{8,12},{12,14},{14,10},{10,6},{6,2},{2,0},{1,5},{5,9},... | collective-permute-start | bytes 786440 | tf_op jit(solution)/shard_map/ppermute | solution.py:450
  93.0 1.8 %collective-permute-start.16 = (bf16[4,128,384]{2,1,0:T(8,128)(2,1)S(1)}, bf16[4,128,384]{2,1,0:T(8,128)(2,1)S(1)}, u32[]{:S(2)}, u32[]{:S(2)}) collective-permute-start(bf16[4,128,384]{2,1,0:T(8,128)(2,1)S(1)} %dynamic-slice_convert_fusion), channel_id=1, source_target_pairs={{0,1},{1,0},{2,3},{3,2},{4,5},{5,4},{6,7},{7,6},{8,9},{9,8},{10,11... | collective-permute-start | bytes 1179656 | tf_op jit(solution)/shard_map/ppermute | solution.py:25
  96.3 8.2 %collective-permute-start.17 = (bf16[144,384]{1,0:T(8,128)(2,1)S(1)}, bf16[144,384]{1,0:T(8,128)(2,1)S(1)}, u32[]{:S(2)}, u32[]{:S(2)}) collective-permute-start(bf16[144,384]{1,0:T(8,128)(2,1)S(1)} %get-tuple-element.37), channel_id=1, source_target_pairs={{0,2},{2,0},{4,6},{6,4},{8,10},{10,8},{12,14},{14,12},{1,3},{3,1},... | collective-permute-start | bytes 331784 | tf_op jit(solution)/shard_map/ppermute | solution.py:419
  98.7 8.9 %collective-permute-start.18 = (bf16[144,384]{1,0:T(8,128)(2,1)S(1)}, bf16[144,384]{1,0:T(8,128)(2,1)S(1)}, u32[]{:S(2)}, u32[]{:S(2)}) collective-permute-start(bf16[144,384]{1,0:T(8,128)(2,1)S(1)} %get-tuple-element.38), channel_id=1, source_target_pairs={{0,4},{2,6},{4,0},{6,2},{8,12},{10,14},{12,8},{14,10},{1,5},{3,7},... | collective-permute-start | bytes 331784 | tf_op jit(solution)/shard_map/ppermute | solution.py:419
  100.4 15.2 %collective-permute-start.19 = (bf16[144,384]{1,0:T(8,128)(2,1)S(1)}, bf16[144,384]{1,0:T(8,128)(2,1)S(1)}, u32[]{:S(2)}, u32[]{:S(2)}) collective-permute-start(bf16[144,384]{1,0:T(8,128)(2,1)S(1)} %get-tuple-element.39), channel_id=1, source_target_pairs={{0,6},{2,4},{4,2},{6,0},{8,14},{10,12},{12,10},{14,8},{1,7},{3,5},... | collective-permute-start | bytes 331784 | tf_op jit(solution)/shard_map/ppermute | solution.py:419
  100.4 15.2 %collective-permute-start.20 = (bf16[144,384]{1,0:T(8,128)(2,1)S(1)}, bf16[144,384]{1,0:T(8,128)(2,1)S(1)}, u32[]{:S(2)}, u32[]{:S(2)}) collective-permute-start(bf16[144,384]{1,0:T(8,128)(2,1)S(1)} %get-tuple-element.40), channel_id=1, source_target_pairs={{0,8},{2,10},{4,12},{6,14},{8,0},{10,2},{12,4},{14,6},{1,9},{3,11}... | collective-permute-start | bytes 331784 | tf_op jit(solution)/shard_map/ppermute | solution.py:419
  103.3 16.4 %collective-permute-start.21 = (bf16[144,384]{1,0:T(8,128)(2,1)S(1)}, bf16[144,384]{1,0:T(8,128)(2,1)S(1)}, u32[]{:S(2)}, u32[]{:S(2)}) collective-permute-start(bf16[144,384]{1,0:T(8,128)(2,1)S(1)} %get-tuple-element.41), channel_id=1, source_target_pairs={{0,10},{2,8},{4,14},{6,12},{8,2},{10,0},{12,6},{14,4},{1,11},{3,9}... | collective-permute-start | bytes 331784 | tf_op jit(solution)/shard_map/ppermute | solution.py:419
  104.5 15.2 %collective-permute-start.22 = (bf16[144,384]{1,0:T(8,128)(2,1)S(1)}, bf16[144,384]{1,0:T(8,128)(2,1)S(1)}, u32[]{:S(2)}, u32[]{:S(2)}) collective-permute-start(bf16[144,384]{1,0:T(8,128)(2,1)S(1)} %get-tuple-element.42), channel_id=1, source_target_pairs={{0,12},{2,14},{4,8},{6,10},{8,4},{10,6},{12,0},{14,2},{1,13},{3,15... | collective-permute-start | bytes 331784 | tf_op jit(solution)/shard_map/ppermute | solution.py:419
  107.5 12.1 %collective-permute-start.23 = (bf16[144,384]{1,0:T(8,128)(2,1)S(1)}, bf16[144,384]{1,0:T(8,128)(2,1)S(1)}, u32[]{:S(2)}, u32[]{:S(2)}) collective-permute-start(bf16[144,384]{1,0:T(8,128)(2,1)S(1)} %get-tuple-element.43), channel_id=1, source_target_pairs={{0,14},{2,12},{4,10},{6,8},{8,6},{10,4},{12,2},{14,0},{1,15},{3,13... | collective-permute-start | bytes 331784 | tf_op jit(solution)/shard_map/ppermute | solution.py:419
  115.6 6.6 %copy-start.12 = (f32[3072]{0:T(1024)S(1)}, f32[3072]{0:T(1024)}, u32[]{:S(2)}) copy-start(f32[3072]{0:T(1024)} %param.18) | copy-start | bytes 36868
  119.7 1.9 %collective-permute-start.25 = (bf16[4,144,384]{2,1,0:T(8,128)(2,1)S(1)}, bf16[4,144,384]{2,1,0:T(8,128)(2,1)S(1)}, u32[]{:S(2)}, u32[]{:S(2)}) collective-permute-start(bf16[4,144,384]{2,1,0:T(8,128)(2,1)S(1)} %pad_maximum_fusion.1.near_own.c), channel_id=1, source_target_pairs={{0,1},{1,0},{2,3},{3,2},{4,5},{5,4},{6,7},{7,6},{8,9},{9,8},{10,11... | collective-permute-start | bytes 1327112 | tf_op jit(solution)/shard_map/ppermute | solution.py:25
  119.9 2.3 %collective-permute-start.24 = (bf16[4,144,384]{2,1,0:T(8,128)(2,1)S(1)}, bf16[4,144,384]{2,1,0:T(8,128)(2,1)S(1)}, u32[]{:S(2)}, u32[]{:S(2)}) collective-permute-start(bf16[4,144,384]{2,1,0:T(8,128)(2,1)S(1)} %pad_maximum_fusion.far_own.a), channel_id=1, source_target_pairs={{0,1},{1,0},{2,3},{3,2},{4,5},{5,4},{6,7},{7,6},{8,9},{9,8},{10,11... | collective-permute-start | bytes 1327112 | tf_op jit(solution)/shard_map/ppermute | solution.py:25
  141.6 2.5 %collective-permute-start.26 = (bf16[288,1536]{1,0:T(8,128)(2,1)S(1)}, bf16[288,1536]{1,0:T(8,128)(2,1)S(1)}, u32[]{:S(2)}, u32[]{:S(2)}) collective-permute-start(bf16[288,1536]{1,0:T(8,128)(2,1)S(1)} %get-tuple-element.54), channel_id=1, source_target_pairs={{0,1},{1,0},{2,3},{3,2},{4,5},{5,4},{6,7},{7,6},{8,9},{9,8},{10,11... | collective-permute-start | bytes 2654216 | tf_op jit(solution)/shard_map/ppermute | solution.py:25
  144.1 32.1 %copy-start.1 = (bf16[2048,384]{1,0:T(8,128)(2,1)S(1)}, bf16[2048,384]{1,0:T(8,128)(2,1)}, u32[]{:S(2)}) copy-start(bf16[2048,384]{1,0:T(8,128)(2,1)} %param.17) | copy-start | bytes 4718596
  145.9 18.9 %collective-permute-start.27 = (bf16[144,384]{1,0:T(8,128)(2,1)S(1)}, bf16[144,384]{1,0:T(8,128)(2,1)S(1)}, u32[]{:S(2)}, u32[]{:S(2)}) collective-permute-start(bf16[144,384]{1,0:T(8,128)(2,1)S(1)} %get-tuple-element.55), channel_id=1, source_target_pairs={{0,8},{2,10},{4,12},{6,14},{8,0},{10,2},{12,4},{14,6},{1,9},{3,11}... | collective-permute-start | bytes 331784 | tf_op jit(solution)/shard_map/ppermute | solution.py:419
  151.5 16.8 %collective-permute-start.28 = (bf16[144,384]{1,0:T(8,128)(2,1)S(1)}, bf16[144,384]{1,0:T(8,128)(2,1)S(1)}, u32[]{:S(2)}, u32[]{:S(2)}) collective-permute-start(bf16[144,384]{1,0:T(8,128)(2,1)S(1)} %get-tuple-element.56), channel_id=1, source_target_pairs={{0,10},{2,8},{4,14},{6,12},{8,2},{10,0},{12,6},{14,4},{1,11},{3,9}... | collective-permute-start | bytes 331784 | tf_op jit(solution)/shard_map/ppermute | solution.py:419
  152.6 15.6 %collective-permute-start.29 = (bf16[144,384]{1,0:T(8,128)(2,1)S(1)}, bf16[144,384]{1,0:T(8,128)(2,1)S(1)}, u32[]{:S(2)}, u32[]{:S(2)}) collective-permute-start(bf16[144,384]{1,0:T(8,128)(2,1)S(1)} %get-tuple-element.57), channel_id=1, source_target_pairs={{0,12},{2,14},{4,8},{6,10},{8,4},{10,6},{12,0},{14,2},{1,13},{3,15... | collective-permute-start | bytes 331784 | tf_op jit(solution)/shard_map/ppermute | solution.py:419
  153.5 14.8 %collective-permute-start.30 = (bf16[144,384]{1,0:T(8,128)(2,1)S(1)}, bf16[144,384]{1,0:T(8,128)(2,1)S(1)}, u32[]{:S(2)}, u32[]{:S(2)}) collective-permute-start(bf16[144,384]{1,0:T(8,128)(2,1)S(1)} %get-tuple-element.58), channel_id=1, source_target_pairs={{0,14},{2,12},{4,10},{6,8},{8,6},{10,4},{12,2},{14,0},{1,15},{3,13... | collective-permute-start | bytes 331784 | tf_op jit(solution)/shard_map/ppermute | solution.py:419
  156.4 11.9 %collective-permute-start.31 = (bf16[144,384]{1,0:T(8,128)(2,1)S(1)}, bf16[144,384]{1,0:T(8,128)(2,1)S(1)}, u32[]{:S(2)}, u32[]{:S(2)}) collective-permute-start(bf16[144,384]{1,0:T(8,128)(2,1)S(1)} %get-tuple-element.60), channel_id=1, source_target_pairs={{0,2},{2,0},{4,6},{6,4},{8,10},{10,8},{12,14},{14,12},{1,3},{3,1},... | collective-permute-start | bytes 331784 | tf_op jit(solution)/shard_map/ppermute | solution.py:419
  164.8 4.7 %collective-permute-start.32 = (bf16[144,384]{1,0:T(8,128)(2,1)S(1)}, bf16[144,384]{1,0:T(8,128)(2,1)S(1)}, u32[]{:S(2)}, u32[]{:S(2)}) collective-permute-start(bf16[144,384]{1,0:T(8,128)(2,1)S(1)} %get-tuple-element.61), channel_id=1, source_target_pairs={{0,4},{2,6},{4,0},{6,2},{8,12},{10,14},{12,8},{14,10},{1,5},{3,7},... | collective-permute-start | bytes 331784 | tf_op jit(solution)/shard_map/ppermute | solution.py:419
  168.3 5.6 %collective-permute-start.33 = (bf16[144,384]{1,0:T(8,128)(2,1)S(1)}, bf16[144,384]{1,0:T(8,128)(2,1)S(1)}, u32[]{:S(2)}, u32[]{:S(2)}) collective-permute-start(bf16[144,384]{1,0:T(8,128)(2,1)S(1)} %get-tuple-element.62), channel_id=1, source_target_pairs={{0,6},{2,4},{4,2},{6,0},{8,14},{10,12},{12,10},{14,8},{1,7},{3,5},... | collective-permute-start | bytes 331784 | tf_op jit(solution)/shard_map/ppermute | solution.py:419

commit v5 on v4

--- a/solution.py
+++ b/solution.py
@@ -310,20 +310,26 @@
     place((far_other, near_other), pl.multiple_of((1 - core) * rows, rows))
 
     for i in range(tiles):
-        at = slice(i * tile, (i + 1) * tile)
-        gate = dot(x_ref[...], gate_ref[:, at])
-        upward = None
         for k in range(parts):
             copies[i, k].wait()
-            value = dot(x_ref[:, k * depth : (k + 1) * depth], up_ref[i, k])
-            upward = value if k == 0 else upward + value
-        inner_ref[:, at] = (gate / (1.0 + jnp.exp(-gate)) * upward).astype(BF)
-    inner = inner_ref[...]
+        step = 256 if tile % 256 == 0 else tile
+        for lo in range(0, tile, step):
+            at = slice(i * tile + lo, i * tile + lo + step)
+            gate = dot(x_ref[...], gate_ref[:, at])
+            upward = None
+            for k in range(parts):
+                x = x_ref[:, k * depth : (k + 1) * depth]
+                value = dot(x, up_ref[i, k, :, lo : lo + step])
+                upward = value if k == 0 else upward + value
+            inner_ref[:, at] = (gate / (1.0 + jnp.exp(-gate)) * upward).astype(BF)
     for i, copy in enumerate(downs):
         copy.wait()
-        lo = i * out_tile % half
         out_ref = theirs_ref if i * out_tile < half else mine_ref
-        out_ref[:, lo : lo + out_tile] = dot(inner, down_ref[i]).astype(BF)
+        step = 256 if out_tile % 256 == 0 else out_tile
+        for lo in range(0, out_tile, step):
+            start = i * out_tile % half + lo
+            value = dot(inner_ref[...], down_ref[i, :, lo : lo + step])
+            out_ref[:, start : start + step] = value.astype(BF)
 
 
 def tile_of(size):

time: 177 us -> 177 us (level)
  no operation moved by 1% of the time
where the time goes in v5:
time: 177 us
  waiting for transfers between devices  74 us (42%)
  starting transfers between devices  51.2 us (29%)
  Pallas kernels  37.2 us (21%)
  local copies, waits for them, and re-layouts  7.65 us (4%)
  matrix products  5.83 us (3%)
    ppermute x14, starting transfers between devices, xor_shift(): lax.ppermute(x, 'seq', [(s, s ^ k) for s in range(lax.axis_size('seq'))])  25.9 us
    ppermute x14, waiting for transfers between devices, xor_shift(): lax.ppermute(x, 'seq', [(s, s ^ k) for s in range(lax.axis_size('seq'))])  20.4 us
    pallas_call x1, Pallas kernels, experts(): pl.pallas_call(moe_kernel, out_shape=(out, out), in_specs=[smem] + [vmem]...  19.9 us
    ppermute x7, waiting for transfers between devices, ring_project(): back[i] = lax.ppermute(back[i], 'seq', ahead)  17.9 us
    all_to_all x1, waiting for transfers between devices, per_device(): lax.all_to_all(sums, 'seq', 0, 0, axis_index_groups=groups, tiled=True)  12.3 us
    pallas_call x8, Pallas kernels, on_chip(): pl.pallas_call(kernel, out_shape=out_shape, in_specs=[smem] * scalars + [...  12.3 us
    ppermute x7, starting transfers between devices, ring_project(): back[i] = lax.ppermute(back[i], 'seq', ahead)  9.31 us
    ppermute x1, waiting for transfers between devices, per_device(): lax.ppermute(own_sum, 'seq', [(s, (s + half) % seq_count) for s in chips])  8.85 us
  transfers between devices with their start and end apart: 36, of which 22 were waited for; matrix products, arithmetic and copies ran while one was open for 3% of the time, Pallas kernels for 4%

profile of v5, /device:TPU:0, one launch (start us, length us, event | category | flops | bytes accessed | tf_op | source)
XLA Modules:
  0.0 176.8 jit_solution(8807819189934912358)
XLA Ops:
  0.0 2.8 %states.1 = bf16[4,512,128]{2,1,0:T(8,128)(2,1)} custom-call(bf16[128,2048]{1,0:T(8,128)(2,1)} %k_ref.1, bf16[128,2048]{1,0:T(8,128)(2,1)} %v_ref.1), custom_call_target="tpu_custom_call" | custom-call | tf_op jit(solution)/shard_map/states/pallas_call | solution.py:400
  2.9 5.3 %all-to-all-start = ((bf16[4,512,128]{2,1,0:T(8,128)(2,1)}), bf16[4,512,128]{2,1,0:T(8,128)(2,1)S(1)}, u32[]{:S(2)}, u32[]{:S(2)}) async-start(bf16[4,512,128]{2,1,0:T(8,128)(2,1)} %states.1), calls=%async_computation | async-start | bytes 1048576 | tf_op jit(solution)/shard_map/all_to_all | solution.py:496
  8.1 0.8 collective-permute-start.1
  9.0 1.0 copy-done.5
  10.0 1.0 copy-done.6
  11.1 1.0 copy-done.7
  12.1 2.6 %intra.1.intra_ref = f32[128,2048]{1,0:T(8,128)S(1)} custom-call(bf16[128,2048]{1,0:T(8,128)(2,1)S(1)} %copy-done.7, bf16[128,2048]{1,0:T(8,128)(2,1)S(1)} %copy-done.5, bf16[128,2048]{1,0:T(8,128)(2,1)S(1)} %copy-done.6), custom_call_target="tpu_custom_call" | custom-call | tf_op jit(solution)/shard_map/intra/pallas_call | solution.py:400
  14.7 1.0 copy-done.2
  15.8 4.3 %all-to-all-done.x_ref = bf16[4,512,128]{2,1,0:T(8,128)(2,1)S(1)} async-done(((bf16[4,512,128]{2,1,0:T(8,128)(2,1)}), bf16[4,512,128]{2,1,0:T(8,128)(2,1)S(1)}, u32[]{:S(2)}, u32[]{:S(2)}) %all-to-all-start) | async-done | bytes 524320 | tf_op jit(solution)/shard_map/all_to_all | solution.py:496
  20.3 8.8 %collective-permute-done.far_ref = bf16[528,128]{1,0:T(8,128)(2,1)S(1)} collective-permute-done((bf16[528,128]{1,0:T(8,128)(2,1)S(1)}, bf16[528,128]{1,0:T(8,128)(2,1)S(1)}, u32[]{:S(2)}, u32[]{:S(2)}) %collective-permute-start) | collective-permute-done | bytes 135200 | tf_op jit(solution)/shard_map/ppermute | solution.py:501
  29.1 0.7 sums.1
  29.8 1.0 copy-done.4
  30.8 3.6 %all-to-all-start.1 = ((bf16[4,912,128]{2,1,0:T(8,128)(2,1)}), bf16[4,912,128]{2,1,0:T(8,128)(2,1)S(1)}, u32[]{:S(2)}, u32[]{:S(2)}) async-start(bf16[4,912,128]{2,1,0:T(8,128)(2,1)} %copy-done.4), calls=%async_computation.1 | async-start | bytes 1867776 | tf_op jit(solution)/shard_map/all_to_all | solution.py:512
  34.7 12.3 %all-to-all-done.1.before_ref.resid_ref.sums_ref = bf16[4,912,128]{2,1,0:T(8,128)(2,1)S(1)} async-done(((bf16[4,912,128]{2,1,0:T(8,128)(2,1)}), bf16[4,912,128]{2,1,0:T(8,128)(2,1)S(1)}, u32[]{:S(2)}, u32[]{:S(2)}) %all-to-all-start.1) | async-done | bytes 933920 | tf_op jit(solution)/shard_map/all_to_all | solution.py:512
  47.0 1.2 copy-done.3
  48.2 1.0 copy-done.8
  49.8 1.3 collective-permute-start.4
  51.1 0.8 collective-permute-start.5
  51.9 1.3 collective-permute-start.2
  53.2 0.8 collective-permute-start.3
  54.7 4.3 %collective-permute-done.4 = bf16[64,2048]{1,0:T(8,128)(2,1)S(1)} collective-permute-done((bf16[64,2048]{1,0:T(8,128)(2,1)S(1)}, bf16[64,2048]{1,0:T(8,128)(2,1)S(1)}, u32[]{:S(2)}, u32[]{:S(2)}) %collective-permute-start.4) | collective-permute-done | bytes 262176 | tf_op jit(solution)/shard_map/ppermute | solution.py:456
  59.1 1.2 collective-permute-start.8
  60.4 0.8 collective-permute-start.9
  61.1 3.6 %collective-permute-done.2 = bf16[64,2048]{1,0:T(8,128)(2,1)S(1)} collective-permute-done((bf16[64,2048]{1,0:T(8,128)(2,1)S(1)}, bf16[64,2048]{1,0:T(8,128)(2,1)S(1)}, u32[]{:S(2)}, u32[]{:S(2)}) %collective-permute-start.2) | collective-permute-done | bytes 262176 | tf_op jit(solution)/shard_map/ppermute | solution.py:456
  64.7 1.2 collective-permute-start.6
  66.0 0.8 collective-permute-start.7
  68.2 2.1 %collective-permute-done.8 = bf16[64,2048]{1,0:T(8,128)(2,1)S(1)} collective-permute-done((bf16[64,2048]{1,0:T(8,128)(2,1)S(1)}, bf16[64,2048]{1,0:T(8,128)(2,1)S(1)}, u32[]{:S(2)}, u32[]{:S(2)}) %collective-permute-start.8) | collective-permute-done | bytes 262176 | tf_op jit(solution)/shard_map/ppermute | solution.py:456
  70.3 1.2 collective-permute-start.12
  71.6 0.8 collective-permute-start.13
  72.4 3.6 %collective-permute-done.6 = bf16[64,2048]{1,0:T(8,128)(2,1)S(1)} collective-permute-done((bf16[64,2048]{1,0:T(8,128)(2,1)S(1)}, bf16[64,2048]{1,0:T(8,128)(2,1)S(1)}, u32[]{:S(2)}, u32[]{:S(2)}) %collective-permute-start.6) | collective-permute-done | bytes 262176 | tf_op jit(solution)/shard_map/ppermute | solution.py:456
  75.9 1.2 collective-permute-start.10
  77.2 0.8 collective-permute-start.11
  79.4 3.4 %collective-permute-done.13 = bf16[64,2048]{1,0:T(8,128)(2,1)S(1)} collective-permute-done((bf16[64,2048]{1,0:T(8,128)(2,1)S(1)}, bf16[64,2048]{1,0:T(8,128)(2,1)S(1)}, u32[]{:S(2)}, u32[]{:S(2)}) %collective-permute-start.13) | collective-permute-done | bytes 262176 | tf_op jit(solution)/shard_map/ppermute | solution.py:459
  82.8 0.8 collective-permute-start.15
  83.6 1.8 %collective-permute-done.10 = bf16[64,2048]{1,0:T(8,128)(2,1)S(1)} collective-permute-done((bf16[64,2048]{1,0:T(8,128)(2,1)S(1)}, bf16[64,2048]{1,0:T(8,128)(2,1)S(1)}, u32[]{:S(2)}, u32[]{:S(2)}) %collective-permute-start.10) | collective-permute-done | bytes 262176 | tf_op jit(solution)/shard_map/ppermute | solution.py:456
  85.4 1.8 %collective-permute-start.14 = (bf16[64,2048]{1,0:T(8,128)(2,1)S(1)}, bf16[64,2048]{1,0:T(8,128)(2,1)S(1)}, u32[]{:S(2)}, u32[]{:S(2)}) collective-permute-start(bf16[64,2048]{1,0:T(8,128)(2,1)S(1)} %collective-permute-done.10), channel_id=1, source_target_pairs={{0,4},{4,8},{8,12},{12,14},{14,10},{10,6},{6,2},{2,0},{1,5},{5,9},... | collective-permute-start | bytes 786440 | tf_op jit(solution)/shard_map/ppermute | solution.py:456
  87.6 0.8 collective-permute-done.11
  89.6 2.4 %collective-permute-done.14 = bf16[64,2048]{1,0:T(8,128)(2,1)S(1)} collective-permute-done((bf16[64,2048]{1,0:T(8,128)(2,1)S(1)}, bf16[64,2048]{1,0:T(8,128)(2,1)S(1)}, u32[]{:S(2)}, u32[]{:S(2)}) %collective-permute-start.14) | collective-permute-done | bytes 262176 | tf_op jit(solution)/shard_map/ppermute | solution.py:456
  93.1 1.7 collective-permute-done.16.other_ref
  94.8 1.5 dispatch.1
  96.3 2.4 %collective-permute-start.17 = (bf16[144,384]{1,0:T(8,128)(2,1)S(1)}, bf16[144,384]{1,0:T(8,128)(2,1)S(1)}, u32[]{:S(2)}, u32[]{:S(2)}) collective-permute-start(bf16[144,384]{1,0:T(8,128)(2,1)S(1)} %get-tuple-element.37), channel_id=1, source_target_pairs={{0,2},{2,0},{4,6},{6,4},{8,10},{10,8},{12,14},{14,12},{1,3},{3,1},... | collective-permute-start | bytes 331784 | tf_op jit(solution)/shard_map/ppermute | solution.py:425
  98.7 1.7 collective-permute-start.18
  100.4 2.9 %collective-permute-start.20 = (bf16[144,384]{1,0:T(8,128)(2,1)S(1)}, bf16[144,384]{1,0:T(8,128)(2,1)S(1)}, u32[]{:S(2)}, u32[]{:S(2)}) collective-permute-start(bf16[144,384]{1,0:T(8,128)(2,1)S(1)} %get-tuple-element.40), channel_id=1, source_target_pairs={{0,8},{2,10},{4,12},{6,14},{8,0},{10,2},{12,4},{14,6},{1,9},{3,11}... | collective-permute-start | bytes 331784 | tf_op jit(solution)/shard_map/ppermute | solution.py:425
  103.3 1.2 collective-permute-start.21
  104.5 2.6 %collective-permute-start.22 = (bf16[144,384]{1,0:T(8,128)(2,1)S(1)}, bf16[144,384]{1,0:T(8,128)(2,1)S(1)}, u32[]{:S(2)}, u32[]{:S(2)}) collective-permute-start(bf16[144,384]{1,0:T(8,128)(2,1)S(1)} %get-tuple-element.42), channel_id=1, source_target_pairs={{0,12},{2,14},{4,8},{6,10},{8,4},{10,6},{12,0},{14,2},{1,13},{3,15... | collective-permute-start | bytes 331784 | tf_op jit(solution)/shard_map/ppermute | solution.py:425
  107.5 3.1 %collective-permute-start.23 = (bf16[144,384]{1,0:T(8,128)(2,1)S(1)}, bf16[144,384]{1,0:T(8,128)(2,1)S(1)}, u32[]{:S(2)}, u32[]{:S(2)}) collective-permute-start(bf16[144,384]{1,0:T(8,128)(2,1)S(1)} %get-tuple-element.43), channel_id=1, source_target_pairs={{0,14},{2,12},{4,10},{6,8},{8,6},{10,4},{12,2},{14,0},{1,15},{3,13... | collective-permute-start | bytes 331784 | tf_op jit(solution)/shard_map/ppermute | solution.py:425
  110.6 5.0 %load_gate.1.gate_ref = bf16[3072,2304]{1,0:T(8,128)(2,1)S(1)} custom-call(bf16[3072,2304]{1,0:T(8,128)(2,1)} %source.1), custom_call_target="tpu_custom_call" | custom-call | bytes 14155776 | tf_op jit(solution)/shard_map/load_gate/pallas_call | solution.py:412
  115.6 4.0 %collective-permute-done.21 = bf16[144,384]{1,0:T(8,128)(2,1)S(1)} collective-permute-done((bf16[144,384]{1,0:T(8,128)(2,1)S(1)}, bf16[144,384]{1,0:T(8,128)(2,1)S(1)}, u32[]{:S(2)}, u32[]{:S(2)}) %collective-permute-start.21) | collective-permute-done | bytes 110624 | tf_op jit(solution)/shard_map/ppermute | solution.py:425
  119.9 0.6 collective-permute-start.24
  120.5 1.1 collective-permute-done.25.near_other.d
  121.6 0.6 collective-permute-done.24.far_other.b
  122.2 19.9 %experts.1 = (bf16[288,1536]{1,0:T(8,128)(2,1)S(1)}, bf16[288,1536]{1,0:T(8,128)(2,1)S(1)}) custom-call(s32[9]{0:T(128)S(1)} %pad_add_fusion.info_ref, bf16[4,144,384]{2,1,0:T(8,128)(2,1)S(1)} %pad_maximum_fusion.far_own.a, bf16[4,144,384]{2,1,0:T(8,128)(2,1)S(1)} %collective-permute-done.24.far_other.b, ...), custom_call_target="tpu_custom_call" | custom-call | flops 12230590464 | bytes 42467328 | tf_op jit(solution)/shard_map/experts/pallas_call | solution.py:370
  142.3 2.3 %collective-permute-done.26.theirs_ref = bf16[288,1536]{1,0:T(8,128)(2,1)S(1)} collective-permute-done((bf16[288,1536]{1,0:T(8,128)(2,1)S(1)}, bf16[288,1536]{1,0:T(8,128)(2,1)S(1)}, u32[]{:S(2)}, u32[]{:S(2)}) %collective-permute-start.26) | collective-permute-done | bytes 884768 | tf_op jit(solution)/shard_map/ppermute | solution.py:25
  144.6 1.8 %weigh.1 = (bf16[144,384]{1,0:T(8,128)(2,1)S(1)}, bf16[144,384]{1,0:T(8,128)(2,1)S(1)}, bf16[144,384]{1,0:T(8,128)(2,1)S(1)}, bf16[144,384]{1,0:T(8,128)(2,1)S(1...) custom-call(s32[6]{0:T(128)S(1)} %stack.51.flags_ref, ...), custom_call_target="tpu_custom_call" | custom-call | tf_op jit(solution)/shard_map/weigh/pallas_call | solution.py:400
  146.4 5.5 %collective-permute-start.27 = (bf16[144,384]{1,0:T(8,128)(2,1)S(1)}, bf16[144,384]{1,0:T(8,128)(2,1)S(1)}, u32[]{:S(2)}, u32[]{:S(2)}) collective-permute-start(bf16[144,384]{1,0:T(8,128)(2,1)S(1)} %get-tuple-element.55), channel_id=1, source_target_pairs={{0,8},{2,10},{4,12},{6,14},{8,0},{10,2},{12,4},{14,6},{1,9},{3,11}... | collective-permute-start | bytes 331784 | tf_op jit(solution)/shard_map/ppermute | solution.py:425
  152.0 1.2 collective-permute-start.28
  153.1 0.9 collective-permute-start.29
  154.0 2.9 %collective-permute-start.30 = (bf16[144,384]{1,0:T(8,128)(2,1)S(1)}, bf16[144,384]{1,0:T(8,128)(2,1)S(1)}, u32[]{:S(2)}, u32[]{:S(2)}) collective-permute-start(bf16[144,384]{1,0:T(8,128)(2,1)S(1)} %get-tuple-element.58), channel_id=1, source_target_pairs={{0,14},{2,12},{4,10},{6,8},{8,6},{10,4},{12,2},{14,0},{1,15},{3,13... | collective-permute-start | bytes 331784 | tf_op jit(solution)/shard_map/ppermute | solution.py:425
  156.9 1.5 collective-permute-start.31
  158.4 6.9 %collective-permute-done.27.refs_0_ = bf16[144,384]{1,0:T(8,128)(2,1)S(1)} collective-permute-done((bf16[144,384]{1,0:T(8,128)(2,1)S(1)}, bf16[144,384]{1,0:T(8,128)(2,1)S(1)}, u32[]{:S(2)}, u32[]{:S(2)}) %collective-permute-start.27) | collective-permute-done | bytes 110624 | tf_op jit(solution)/shard_map/ppermute | solution.py:425
  165.3 3.4 %collective-permute-done.28.refs_1_ = bf16[144,384]{1,0:T(8,128)(2,1)S(1)} collective-permute-done((bf16[144,384]{1,0:T(8,128)(2,1)S(1)}, bf16[144,384]{1,0:T(8,128)(2,1)S(1)}, u32[]{:S(2)}, u32[]{:S(2)}) %collective-permute-start.28) | collective-permute-done | bytes 110624 | tf_op jit(solution)/shard_map/ppermute | solution.py:425
  168.8 1.3 collective-permute-done.32.refs_6_
  170.1 4.3 %collective-permute-done.33.refs_7_ = bf16[144,384]{1,0:T(8,128)(2,1)S(1)} collective-permute-done((bf16[144,384]{1,0:T(8,128)(2,1)S(1)}, bf16[144,384]{1,0:T(8,128)(2,1)S(1)}, u32[]{:S(2)}, u32[]{:S(2)}) %collective-permute-start.33) | collective-permute-done | bytes 110624 | tf_op jit(solution)/shard_map/ppermute | solution.py:425
  174.4 2.3 %combine.1 = bf16[128,1536]{1,0:T(8,128)(2,1)} custom-call(s32[6]{0:T(128)S(1)} %stack.51.flags_ref, s32[2,128]{1,0:T(2,128)S(1)} %bitcast.113, bf16[144,384]{1,0:T(8,128)(2,1)S(1)} %collective-permute-done.27.refs_0_, bf16[144,384]{1,0:T(8,128)(2,1)S(1)} %collective-permute-done.28.refs_1_, bf16[144,384]{1,0:T(8,128)(2,1)S(1)} %collective-permute-done.29.refs_2_, ...), custom_call_target="tpu_custom_call" | custom-call | tf_op jit(solution)/shard_map/combine/pallas_call | solution.py:400
  (71 shorter events, 8.2 us)
Async XLA Ops:
  0.0 54.0 %copy-start = (bf16[2048,384]{1,0:T(8,128)(2,1)S(1)}, bf16[2048,384]{1,0:T(8,128)(2,1)}, u32[]{:S(2)}) copy-start(bf16[2048,384]{1,0:T(8,128)(2,1)} %param.17) | copy-start | bytes 4718596
  0.0 8.1 %copy-start.13 = (bf16[128,1536]{1,0:T(8,128)(2,1)S(1)}, bf16[128,1536]{1,0:T(8,128)(2,1)}, u32[]{:S(2)}) copy-start(bf16[128,1536]{1,0:T(8,128)(2,1)} %param.15) | copy-start | bytes 1179652
  2.9 17.2 %all-to-all-start = ((bf16[4,512,128]{2,1,0:T(8,128)(2,1)}), bf16[4,512,128]{2,1,0:T(8,128)(2,1)S(1)}, u32[]{:S(2)}, u32[]{:S(2)}) async-start(bf16[4,512,128]{2,1,0:T(8,128)(2,1)} %states.1), calls=%async_computation | async-start | bytes 1048576 | tf_op jit(solution)/shard_map/all_to_all | solution.py:496
  8.1 11.9 %copy-start.10 = (s32[128,2]{0,1:T(2,128)S(1)}, s32[128,2]{0,1:T(2,128)}, u32[]{:S(2)}) copy-start(s32[128,2]{0,1:T(2,128)} %param.19) | copy-start | bytes 3076
  8.1 11.9 %copy-start.11 = (f32[128,2]{0,1:T(2,128)S(1)}, f32[128,2]{0,1:T(2,128)}, u32[]{:S(2)}) copy-start(f32[128,2]{0,1:T(2,128)} %param.20) | copy-start | bytes 3076
  8.1 12.1 %collective-permute-start.1 = (bf16[128,1536]{1,0:T(8,128)(2,1)S(1)}, bf16[128,1536]{1,0:T(8,128)(2,1)S(1)}, u32[]{:S(2)}, u32[]{:S(2)}) collective-permute-start(bf16[128,1536]{1,0:T(8,128)(2,1)S(1)} %copy-done.13), channel_id=1, source_target_pairs={{1,8},{3,10},{5,12},{7,14},{8,1},{10,3},{12,5},{14,7},{17,24},{19,... | collective-permute-start | bytes 1179656 | tf_op jit(solution)/shard_map/ppermute | solution.py:488
  9.0 1.0 copy-start.5
  10.0 1.0 copy-start.6
  11.1 1.0 copy-start.7
  14.7 1.0 copy-start.2
  20.2 9.0 %collective-permute-start = (bf16[528,128]{1,0:T(8,128)(2,1)S(1)}, bf16[528,128]{1,0:T(8,128)(2,1)S(1)}, u32[]{:S(2)}, u32[]{:S(2)}) collective-permute-start(bf16[528,128]{1,0:T(8,128)(2,1)S(1)} %totals.1.near_ref), channel_id=1, source_target_pairs={{0,8},{2,10},{4,12},{6,14},{8,0},{10,2},{12,4},{14,6},{1,9},{3,11}... | collective-permute-start | bytes 405512 | tf_op jit(solution)/shard_map/ppermute | solution.py:501
  29.8 1.0 copy-start.4
  30.8 16.2 %copy-start.9 = (f32[2048]{0:T(1024)S(1)}, f32[2048]{0:T(1024)}, u32[]{:S(2)}) copy-start(f32[2048]{0:T(1024)} %param.16) | copy-start | bytes 24580
  30.8 16.2 %all-to-all-start.1 = ((bf16[4,912,128]{2,1,0:T(8,128)(2,1)}), bf16[4,912,128]{2,1,0:T(8,128)(2,1)S(1)}, u32[]{:S(2)}, u32[]{:S(2)}) async-start(bf16[4,912,128]{2,1,0:T(8,128)(2,1)} %copy-done.4), calls=%async_computation.1 | async-start | bytes 1867776 | tf_op jit(solution)/shard_map/all_to_all | solution.py:512
  47.0 1.2 copy-start.3
  48.2 1.0 copy-start.8
  49.8 9.3 %collective-permute-start.4 = (bf16[64,2048]{1,0:T(8,128)(2,1)S(1)}, bf16[64,2048]{1,0:T(8,128)(2,1)S(1)}, u32[]{:S(2)}, u32[]{:S(2)}) collective-permute-start(bf16[64,2048]{1,0:T(8,128)(2,1)S(1)} %get-tuple-element.63), channel_id=1, source_target_pairs={{0,4},{4,8},{8,12},{12,14},{14,10},{10,6},{6,2},{2,0},{1,5},{5,9},... | collective-permute-start | bytes 786440 | tf_op jit(solution)/shard_map/ppermute | solution.py:456
  51.1 9.2 %collective-permute-start.5 = (bf16[64,2048]{1,0:T(8,128)(2,1)S(1)}, bf16[64,2048]{1,0:T(8,128)(2,1)S(1)}, u32[]{:S(2)}, u32[]{:S(2)}) collective-permute-start(bf16[64,2048]{1,0:T(8,128)(2,1)S(1)} %get-tuple-element.63), channel_id=1, source_target_pairs={{4,0},{8,4},{12,8},{14,12},{10,14},{6,10},{2,6},{0,2},{5,1},{9,5},... | collective-permute-start | bytes 786440 | tf_op jit(solution)/shard_map/ppermute | solution.py:459
  51.9 12.8 %collective-permute-start.2 = (bf16[64,2048]{1,0:T(8,128)(2,1)S(1)}, bf16[64,2048]{1,0:T(8,128)(2,1)S(1)}, u32[]{:S(2)}, u32[]{:S(2)}) collective-permute-start(bf16[64,2048]{1,0:T(8,128)(2,1)S(1)} %get-tuple-element.64), channel_id=1, source_target_pairs={{0,4},{4,8},{8,12},{12,14},{14,10},{10,6},{6,2},{2,0},{1,5},{5,9},... | collective-permute-start | bytes 786440 | tf_op jit(solution)/shard_map/ppermute | solution.py:456
  53.2 12.8 %collective-permute-start.3 = (bf16[64,2048]{1,0:T(8,128)(2,1)S(1)}, bf16[64,2048]{1,0:T(8,128)(2,1)S(1)}, u32[]{:S(2)}, u32[]{:S(2)}) collective-permute-start(bf16[64,2048]{1,0:T(8,128)(2,1)S(1)} %get-tuple-element.64), channel_id=1, source_target_pairs={{4,0},{8,4},{12,8},{14,12},{10,14},{6,10},{2,6},{0,2},{5,1},{9,5},... | collective-permute-start | bytes 786440 | tf_op jit(solution)/shard_map/ppermute | solution.py:459
  59.1 11.2 %collective-permute-start.8 = (bf16[64,2048]{1,0:T(8,128)(2,1)S(1)}, bf16[64,2048]{1,0:T(8,128)(2,1)S(1)}, u32[]{:S(2)}, u32[]{:S(2)}) collective-permute-start(bf16[64,2048]{1,0:T(8,128)(2,1)S(1)} %collective-permute-done.4), channel_id=1, source_target_pairs={{0,4},{4,8},{8,12},{12,14},{14,10},{10,6},{6,2},{2,0},{1,5},{5,9},... | collective-permute-start | bytes 786440 | tf_op jit(solution)/shard_map/ppermute | solution.py:456
  60.4 11.2 %collective-permute-start.9 = (bf16[64,2048]{1,0:T(8,128)(2,1)S(1)}, bf16[64,2048]{1,0:T(8,128)(2,1)S(1)}, u32[]{:S(2)}, u32[]{:S(2)}) collective-permute-start(bf16[64,2048]{1,0:T(8,128)(2,1)S(1)} %collective-permute-done.5), channel_id=1, source_target_pairs={{4,0},{8,4},{12,8},{14,12},{10,14},{6,10},{2,6},{0,2},{5,1},{9,5},... | collective-permute-start | bytes 786440 | tf_op jit(solution)/shard_map/ppermute | solution.py:459
  64.7 11.2 %collective-permute-start.6 = (bf16[64,2048]{1,0:T(8,128)(2,1)S(1)}, bf16[64,2048]{1,0:T(8,128)(2,1)S(1)}, u32[]{:S(2)}, u32[]{:S(2)}) collective-permute-start(bf16[64,2048]{1,0:T(8,128)(2,1)S(1)} %collective-permute-done.2), channel_id=1, source_target_pairs={{0,4},{4,8},{8,12},{12,14},{14,10},{10,6},{6,2},{2,0},{1,5},{5,9},... | collective-permute-start | bytes 786440 | tf_op jit(solution)/shard_map/ppermute | solution.py:456
  66.0 11.2 %collective-permute-start.7 = (bf16[64,2048]{1,0:T(8,128)(2,1)S(1)}, bf16[64,2048]{1,0:T(8,128)(2,1)S(1)}, u32[]{:S(2)}, u32[]{:S(2)}) collective-permute-start(bf16[64,2048]{1,0:T(8,128)(2,1)S(1)} %collective-permute-done.3), channel_id=1, source_target_pairs={{4,0},{8,4},{12,8},{14,12},{10,14},{6,10},{2,6},{0,2},{5,1},{9,5},... | collective-permute-start | bytes 786440 | tf_op jit(solution)/shard_map/ppermute | solution.py:459
  70.3 18.5 %collective-permute-start.12 = (bf16[64,2048]{1,0:T(8,128)(2,1)S(1)}, bf16[64,2048]{1,0:T(8,128)(2,1)S(1)}, u32[]{:S(2)}, u32[]{:S(2)}) collective-permute-start(bf16[64,2048]{1,0:T(8,128)(2,1)S(1)} %collective-permute-done.8), channel_id=1, source_target_pairs={{0,4},{4,8},{8,12},{12,14},{14,10},{10,6},{6,2},{2,0},{1,5},{5,9},... | collective-permute-start | bytes 786440 | tf_op jit(solution)/shard_map/ppermute | solution.py:456
  71.6 11.2 %collective-permute-start.13 = (bf16[64,2048]{1,0:T(8,128)(2,1)S(1)}, bf16[64,2048]{1,0:T(8,128)(2,1)S(1)}, u32[]{:S(2)}, u32[]{:S(2)}) collective-permute-start(bf16[64,2048]{1,0:T(8,128)(2,1)S(1)} %collective-permute-done.9), channel_id=1, source_target_pairs={{4,0},{8,4},{12,8},{14,12},{10,14},{6,10},{2,6},{0,2},{5,1},{9,5},... | collective-permute-start | bytes 786440 | tf_op jit(solution)/shard_map/ppermute | solution.py:459
  75.9 9.5 %collective-permute-start.10 = (bf16[64,2048]{1,0:T(8,128)(2,1)S(1)}, bf16[64,2048]{1,0:T(8,128)(2,1)S(1)}, u32[]{:S(2)}, u32[]{:S(2)}) collective-permute-start(bf16[64,2048]{1,0:T(8,128)(2,1)S(1)} %collective-permute-done.6), channel_id=1, source_target_pairs={{0,4},{4,8},{8,12},{12,14},{14,10},{10,6},{6,2},{2,0},{1,5},{5,9},... | collective-permute-start | bytes 786440 | tf_op jit(solution)/shard_map/ppermute | solution.py:456
  77.2 11.2 %collective-permute-start.11 = (bf16[64,2048]{1,0:T(8,128)(2,1)S(1)}, bf16[64,2048]{1,0:T(8,128)(2,1)S(1)}, u32[]{:S(2)}, u32[]{:S(2)}) collective-permute-start(bf16[64,2048]{1,0:T(8,128)(2,1)S(1)} %collective-permute-done.7), channel_id=1, source_target_pairs={{4,0},{8,4},{12,8},{14,12},{10,14},{6,10},{2,6},{0,2},{5,1},{9,5},... | collective-permute-start | bytes 786440 | tf_op jit(solution)/shard_map/ppermute | solution.py:459
  82.8 9.8 %collective-permute-start.15 = (bf16[64,2048]{1,0:T(8,128)(2,1)S(1)}, bf16[64,2048]{1,0:T(8,128)(2,1)S(1)}, u32[]{:S(2)}, u32[]{:S(2)}) collective-permute-start(bf16[64,2048]{1,0:T(8,128)(2,1)S(1)} %collective-permute-done.13), channel_id=1, source_target_pairs={{4,0},{8,4},{12,8},{14,12},{10,14},{6,10},{2,6},{0,2},{5,1},{9,5},... | collective-permute-start | bytes 786440 | tf_op jit(solution)/shard_map/ppermute | solution.py:459
  85.4 6.6 %collective-permute-start.14 = (bf16[64,2048]{1,0:T(8,128)(2,1)S(1)}, bf16[64,2048]{1,0:T(8,128)(2,1)S(1)}, u32[]{:S(2)}, u32[]{:S(2)}) collective-permute-start(bf16[64,2048]{1,0:T(8,128)(2,1)S(1)} %collective-permute-done.10), channel_id=1, source_target_pairs={{0,4},{4,8},{8,12},{12,14},{14,10},{10,6},{6,2},{2,0},{1,5},{5,9},... | collective-permute-start | bytes 786440 | tf_op jit(solution)/shard_map/ppermute | solution.py:456
  93.0 1.8 %collective-permute-start.16 = (bf16[4,128,384]{2,1,0:T(8,128)(2,1)S(1)}, bf16[4,128,384]{2,1,0:T(8,128)(2,1)S(1)}, u32[]{:S(2)}, u32[]{:S(2)}) collective-permute-start(bf16[4,128,384]{2,1,0:T(8,128)(2,1)S(1)} %dynamic-slice_convert_fusion), channel_id=1, source_target_pairs={{0,1},{1,0},{2,3},{3,2},{4,5},{5,4},{6,7},{7,6},{8,9},{9,8},{10,11... | collective-permute-start | bytes 1179656 | tf_op jit(solution)/shard_map/ppermute | solution.py:25
  96.3 8.2 %collective-permute-start.17 = (bf16[144,384]{1,0:T(8,128)(2,1)S(1)}, bf16[144,384]{1,0:T(8,128)(2,1)S(1)}, u32[]{:S(2)}, u32[]{:S(2)}) collective-permute-start(bf16[144,384]{1,0:T(8,128)(2,1)S(1)} %get-tuple-element.37), channel_id=1, source_target_pairs={{0,2},{2,0},{4,6},{6,4},{8,10},{10,8},{12,14},{14,12},{1,3},{3,1},... | collective-permute-start | bytes 331784 | tf_op jit(solution)/shard_map/ppermute | solution.py:425
  98.7 8.9 %collective-permute-start.18 = (bf16[144,384]{1,0:T(8,128)(2,1)S(1)}, bf16[144,384]{1,0:T(8,128)(2,1)S(1)}, u32[]{:S(2)}, u32[]{:S(2)}) collective-permute-start(bf16[144,384]{1,0:T(8,128)(2,1)S(1)} %get-tuple-element.38), channel_id=1, source_target_pairs={{0,4},{2,6},{4,0},{6,2},{8,12},{10,14},{12,8},{14,10},{1,5},{3,7},... | collective-permute-start | bytes 331784 | tf_op jit(solution)/shard_map/ppermute | solution.py:425
  100.4 15.2 %collective-permute-start.19 = (bf16[144,384]{1,0:T(8,128)(2,1)S(1)}, bf16[144,384]{1,0:T(8,128)(2,1)S(1)}, u32[]{:S(2)}, u32[]{:S(2)}) collective-permute-start(bf16[144,384]{1,0:T(8,128)(2,1)S(1)} %get-tuple-element.39), channel_id=1, source_target_pairs={{0,6},{2,4},{4,2},{6,0},{8,14},{10,12},{12,10},{14,8},{1,7},{3,5},... | collective-permute-start | bytes 331784 | tf_op jit(solution)/shard_map/ppermute | solution.py:425
  100.4 15.2 %collective-permute-start.20 = (bf16[144,384]{1,0:T(8,128)(2,1)S(1)}, bf16[144,384]{1,0:T(8,128)(2,1)S(1)}, u32[]{:S(2)}, u32[]{:S(2)}) collective-permute-start(bf16[144,384]{1,0:T(8,128)(2,1)S(1)} %get-tuple-element.40), channel_id=1, source_target_pairs={{0,8},{2,10},{4,12},{6,14},{8,0},{10,2},{12,4},{14,6},{1,9},{3,11}... | collective-permute-start | bytes 331784 | tf_op jit(solution)/shard_map/ppermute | solution.py:425
  103.3 16.4 %collective-permute-start.21 = (bf16[144,384]{1,0:T(8,128)(2,1)S(1)}, bf16[144,384]{1,0:T(8,128)(2,1)S(1)}, u32[]{:S(2)}, u32[]{:S(2)}) collective-permute-start(bf16[144,384]{1,0:T(8,128)(2,1)S(1)} %get-tuple-element.41), channel_id=1, source_target_pairs={{0,10},{2,8},{4,14},{6,12},{8,2},{10,0},{12,6},{14,4},{1,11},{3,9}... | collective-permute-start | bytes 331784 | tf_op jit(solution)/shard_map/ppermute | solution.py:425
  104.5 15.2 %collective-permute-start.22 = (bf16[144,384]{1,0:T(8,128)(2,1)S(1)}, bf16[144,384]{1,0:T(8,128)(2,1)S(1)}, u32[]{:S(2)}, u32[]{:S(2)}) collective-permute-start(bf16[144,384]{1,0:T(8,128)(2,1)S(1)} %get-tuple-element.42), channel_id=1, source_target_pairs={{0,12},{2,14},{4,8},{6,10},{8,4},{10,6},{12,0},{14,2},{1,13},{3,15... | collective-permute-start | bytes 331784 | tf_op jit(solution)/shard_map/ppermute | solution.py:425
  107.5 12.1 %collective-permute-start.23 = (bf16[144,384]{1,0:T(8,128)(2,1)S(1)}, bf16[144,384]{1,0:T(8,128)(2,1)S(1)}, u32[]{:S(2)}, u32[]{:S(2)}) collective-permute-start(bf16[144,384]{1,0:T(8,128)(2,1)S(1)} %get-tuple-element.43), channel_id=1, source_target_pairs={{0,14},{2,12},{4,10},{6,8},{8,6},{10,4},{12,2},{14,0},{1,15},{3,13... | collective-permute-start | bytes 331784 | tf_op jit(solution)/shard_map/ppermute | solution.py:425
  115.6 6.6 %copy-start.12 = (f32[3072]{0:T(1024)S(1)}, f32[3072]{0:T(1024)}, u32[]{:S(2)}) copy-start(f32[3072]{0:T(1024)} %param.18) | copy-start | bytes 36868
  119.7 1.9 %collective-permute-start.25 = (bf16[4,144,384]{2,1,0:T(8,128)(2,1)S(1)}, bf16[4,144,384]{2,1,0:T(8,128)(2,1)S(1)}, u32[]{:S(2)}, u32[]{:S(2)}) collective-permute-start(bf16[4,144,384]{2,1,0:T(8,128)(2,1)S(1)} %pad_maximum_fusion.1.near_own.c), channel_id=1, source_target_pairs={{0,1},{1,0},{2,3},{3,2},{4,5},{5,4},{6,7},{7,6},{8,9},{9,8},{10,11... | collective-permute-start | bytes 1327112 | tf_op jit(solution)/shard_map/ppermute | solution.py:25
  119.9 2.3 %collective-permute-start.24 = (bf16[4,144,384]{2,1,0:T(8,128)(2,1)S(1)}, bf16[4,144,384]{2,1,0:T(8,128)(2,1)S(1)}, u32[]{:S(2)}, u32[]{:S(2)}) collective-permute-start(bf16[4,144,384]{2,1,0:T(8,128)(2,1)S(1)} %pad_maximum_fusion.far_own.a), channel_id=1, source_target_pairs={{0,1},{1,0},{2,3},{3,2},{4,5},{5,4},{6,7},{7,6},{8,9},{9,8},{10,11... | collective-permute-start | bytes 1327112 | tf_op jit(solution)/shard_map/ppermute | solution.py:25
  142.1 2.5 %collective-permute-start.26 = (bf16[288,1536]{1,0:T(8,128)(2,1)S(1)}, bf16[288,1536]{1,0:T(8,128)(2,1)S(1)}, u32[]{:S(2)}, u32[]{:S(2)}) collective-permute-start(bf16[288,1536]{1,0:T(8,128)(2,1)S(1)} %get-tuple-element.54), channel_id=1, source_target_pairs={{0,1},{1,0},{2,3},{3,2},{4,5},{5,4},{6,7},{7,6},{8,9},{9,8},{10,11... | collective-permute-start | bytes 2654216 | tf_op jit(solution)/shard_map/ppermute | solution.py:25
  144.6 32.1 %copy-start.1 = (bf16[2048,384]{1,0:T(8,128)(2,1)S(1)}, bf16[2048,384]{1,0:T(8,128)(2,1)}, u32[]{:S(2)}) copy-start(bf16[2048,384]{1,0:T(8,128)(2,1)} %param.17) | copy-start | bytes 4718596
  146.4 18.9 %collective-permute-start.27 = (bf16[144,384]{1,0:T(8,128)(2,1)S(1)}, bf16[144,384]{1,0:T(8,128)(2,1)S(1)}, u32[]{:S(2)}, u32[]{:S(2)}) collective-permute-start(bf16[144,384]{1,0:T(8,128)(2,1)S(1)} %get-tuple-element.55), channel_id=1, source_target_pairs={{0,8},{2,10},{4,12},{6,14},{8,0},{10,2},{12,4},{14,6},{1,9},{3,11}... | collective-permute-start | bytes 331784 | tf_op jit(solution)/shard_map/ppermute | solution.py:425
  152.0 16.8 %collective-permute-start.28 = (bf16[144,384]{1,0:T(8,128)(2,1)S(1)}, bf16[144,384]{1,0:T(8,128)(2,1)S(1)}, u32[]{:S(2)}, u32[]{:S(2)}) collective-permute-start(bf16[144,384]{1,0:T(8,128)(2,1)S(1)} %get-tuple-element.56), channel_id=1, source_target_pairs={{0,10},{2,8},{4,14},{6,12},{8,2},{10,0},{12,6},{14,4},{1,11},{3,9}... | collective-permute-start | bytes 331784 | tf_op jit(solution)/shard_map/ppermute | solution.py:425
  153.1 15.6 %collective-permute-start.29 = (bf16[144,384]{1,0:T(8,128)(2,1)S(1)}, bf16[144,384]{1,0:T(8,128)(2,1)S(1)}, u32[]{:S(2)}, u32[]{:S(2)}) collective-permute-start(bf16[144,384]{1,0:T(8,128)(2,1)S(1)} %get-tuple-element.57), channel_id=1, source_target_pairs={{0,12},{2,14},{4,8},{6,10},{8,4},{10,6},{12,0},{14,2},{1,13},{3,15... | collective-permute-start | bytes 331784 | tf_op jit(solution)/shard_map/ppermute | solution.py:425
  154.0 14.8 %collective-permute-start.30 = (bf16[144,384]{1,0:T(8,128)(2,1)S(1)}, bf16[144,384]{1,0:T(8,128)(2,1)S(1)}, u32[]{:S(2)}, u32[]{:S(2)}) collective-permute-start(bf16[144,384]{1,0:T(8,128)(2,1)S(1)} %get-tuple-element.58), channel_id=1, source_target_pairs={{0,14},{2,12},{4,10},{6,8},{8,6},{10,4},{12,2},{14,0},{1,15},{3,13... | collective-permute-start | bytes 331784 | tf_op jit(solution)/shard_map/ppermute | solution.py:425
  156.9 11.9 %collective-permute-start.31 = (bf16[144,384]{1,0:T(8,128)(2,1)S(1)}, bf16[144,384]{1,0:T(8,128)(2,1)S(1)}, u32[]{:S(2)}, u32[]{:S(2)}) collective-permute-start(bf16[144,384]{1,0:T(8,128)(2,1)S(1)} %get-tuple-element.60), channel_id=1, source_target_pairs={{0,2},{2,0},{4,6},{6,4},{8,10},{10,8},{12,14},{14,12},{1,3},{3,1},... | collective-permute-start | bytes 331784 | tf_op jit(solution)/shard_map/ppermute | solution.py:425
  165.3 4.7 %collective-permute-start.32 = (bf16[144,384]{1,0:T(8,128)(2,1)S(1)}, bf16[144,384]{1,0:T(8,128)(2,1)S(1)}, u32[]{:S(2)}, u32[]{:S(2)}) collective-permute-start(bf16[144,384]{1,0:T(8,128)(2,1)S(1)} %get-tuple-element.61), channel_id=1, source_target_pairs={{0,4},{2,6},{4,0},{6,2},{8,12},{10,14},{12,8},{14,10},{1,5},{3,7},... | collective-permute-start | bytes 331784 | tf_op jit(solution)/shard_map/ppermute | solution.py:425
  168.8 5.6 %collective-permute-start.33 = (bf16[144,384]{1,0:T(8,128)(2,1)S(1)}, bf16[144,384]{1,0:T(8,128)(2,1)S(1)}, u32[]{:S(2)}, u32[]{:S(2)}) collective-permute-start(bf16[144,384]{1,0:T(8,128)(2,1)S(1)} %get-tuple-element.62), channel_id=1, source_target_pairs={{0,6},{2,4},{4,2},{6,0},{8,14},{10,12},{12,10},{14,8},{1,7},{3,5},... | collective-permute-start | bytes 331784 | tf_op jit(solution)/shard_map/ppermute | solution.py:425
